TPU v7x, 256 devices: a whole 4x4x8 slice. The times are simulated.
256 devices in a mesh: rec: 64 (over x, z, core), rep: 4 (over y).
Axes of the slice: x: 4, y: 4, z: 8, core: 2. Of those that a mesh axis runs over, the one named last changes fastest.
Arguments:
- embeddings: float32 [4, 24576, 1024], P('rep', 'rec'), may hold values from -1 to 1
- weight: bfloat16 [1024, 1024], replicated, may hold values from -1.5 to 1.5
- members: int32 [4, 512, 99], P('rep', 'rec'), may hold values from -1 to 24575, as said below
- pair_slots: int32 [4, 8192, 2], P('rep', 'rec'), may hold values from 0 to 791, as said below
- labels: int32 [4, 8192], P('rep', 'rec'), may hold values 0 or 1
Outputs:
- emb_grad: float32 [4, 24576, 1024], P('rep', 'rec')
- weight_grad: float32 [1024, 1024], P('rec')
Inputs may be any that keep to these rules, and one draw needn't show every extreme that they name: `members`: values are records of the same batch. In each block the live slots come first and number 1 to 99; on every index of rec one block has exactly 99. The blocks of one index of rec hold 264 live slots, of which at most 12 name records of one index of rec, and exactly 12 for one of them. A record may stand in several slots. `pair_slots`: both slots of a pair are live and lie in one block of the same index of rec as the pair's row.
All inputs are finite; a program needn't handle non-finite values. No bound on the sum of `labels` on one device may be relied on, other than what follows from the above.
Results may differ from a plain program's by a relative error of at most 0.0065.
Values may be sent and summed in bfloat16 or wider, within the bound.
No kernel may reach another device: no remote copies, remote signals or barrier semaphores. Data moves between devices by JAX's collectives and lax.ppermute only.
A program may use at most 64 MiB of HBM per device.

v0:
```python
import jax
import jax.numpy as jnp
from jax import lax
from jax.sharding import PartitionSpec as P

CAP = 12


margin_shift = 0.5


def owner_terms(rows, live_slot, weight, pair_slots, labels):
    n_blocks, most = live_slot.shape
    feature_dim = rows.shape[1]
    left_proj = jnp.dot(rows, weight, preferred_element_type=jnp.float32).astype(jnp.bfloat16)
    right_proj = lax.dot_general(
        rows, weight, (((1,), (1,)), ((), ())), preferred_element_type=jnp.float32
    ).astype(jnp.bfloat16)
    rows_three = rows.reshape(n_blocks, most, feature_dim)
    left_three = left_proj.reshape(n_blocks, most, feature_dim)
    right_three = right_proj.reshape(n_blocks, most, feature_dim)
    scores = jnp.einsum("bmd,bnd->bmn", left_three, rows_three, preferred_element_type=jnp.float32)
    counts = jnp.sum(live_slot.astype(jnp.float32), axis=1)
    positions = jnp.arange(most)
    pair_live = (
        live_slot[:, :, None] & live_slot[:, None, :] & (positions[:, None] != positions[None, :])
    )
    grad_full = jnp.where(
        pair_live,
        jax.nn.sigmoid(scores - margin_shift) / counts[:, None, None],
        jnp.zeros_like(scores),
    )
    first_slot = pair_slots[:, 0]
    second_slot = pair_slots[:, 1]
    block_of = first_slot // most
    row_first = first_slot % most
    row_second = second_slot % most
    signs = (1 - 2 * labels).astype(jnp.float32)
    picked = scores[block_of, row_first, row_second]
    grad_full = grad_full.at[block_of, row_first, row_second].add(
        signs * jax.nn.sigmoid(signs * (picked - margin_shift))
    )
    grad_bf = grad_full.astype(jnp.bfloat16)
    slot_grad = jnp.einsum("bmn,bnd->bmd", grad_bf, right_three, preferred_element_type=jnp.float32)
    slot_grad = slot_grad + jnp.einsum(
        "bnm,bnd->bmd", grad_bf, left_three, preferred_element_type=jnp.float32
    )
    slot_grad = slot_grad.astype(jnp.bfloat16)
    carried = jnp.einsum(
        "bmn,bnd->bmd", grad_bf, rows_three, preferred_element_type=jnp.float32
    ).astype(jnp.bfloat16)
    weight_term = lax.dot_general(
        rows,
        carried.reshape(-1, feature_dim),
        (((0,), (0,)), ((), ())),
        preferred_element_type=jnp.float32,
    )
    return (slot_grad.reshape(-1, feature_dim), weight_term)


def on_device(embeddings, weight, members, pair_slots, labels):
    rec_count = lax.axis_size("rec")
    rec_rows = embeddings.shape[1]
    feature_dim = embeddings.shape[2]
    member_ids = members[0]
    live_slot = member_ids >= 0
    flat_ids = member_ids.reshape(-1)
    flat_live = flat_ids >= 0
    source_dev = jnp.where(flat_live, flat_ids // rec_rows, rec_count)
    local_row = jnp.where(flat_live, flat_ids % rec_rows, 0)
    one_hot = (source_dev[:, None] == jnp.arange(rec_count)[None, :]).astype(jnp.int32)
    bucket_pos = jnp.sum((jnp.cumsum(one_hot, axis=0) - 1) * one_hot, axis=1)
    requests = (
        jnp.full((rec_count, CAP), -1, jnp.int32)
        .at[source_dev, bucket_pos]
        .set(local_row, mode="drop")
    )
    asked_rows = lax.all_to_all(requests, "rec", split_axis=0, concat_axis=0, tiled=True)
    row_table = embeddings[0].astype(jnp.bfloat16)
    asked_flat = asked_rows.reshape(-1)
    fetch_table = (asked_flat[:, None] == jnp.arange(rec_rows)[None, :]).astype(jnp.bfloat16)
    found_rows = jnp.dot(fetch_table, row_table, preferred_element_type=jnp.float32).astype(
        jnp.bfloat16
    )
    found_rows = found_rows.reshape(rec_count, CAP, feature_dim)
    arrived = lax.all_to_all(found_rows, "rec", split_axis=0, concat_axis=0, tiled=True)
    bucket_index = source_dev * CAP + bucket_pos
    slot_table = (bucket_index[:, None] == jnp.arange(rec_count * CAP)[None, :]).astype(
        jnp.bfloat16
    )
    slot_rows = jnp.dot(
        slot_table, arrived.reshape(-1, feature_dim), preferred_element_type=jnp.float32
    ).astype(jnp.bfloat16)
    slot_grad, weight_term = owner_terms(slot_rows, live_slot, weight, pair_slots[0], labels[0])
    outgoing = lax.dot_general(
        slot_table, slot_grad, (((0,), (0,)), ((), ())), preferred_element_type=jnp.float32
    ).astype(jnp.bfloat16)
    outgoing = outgoing.reshape(rec_count, CAP, feature_dim)
    returned = lax.all_to_all(outgoing, "rec", split_axis=0, concat_axis=0, tiled=True)
    emb_grad = lax.dot_general(
        fetch_table,
        returned.reshape(-1, feature_dim),
        (((0,), (0,)), ((), ())),
        preferred_element_type=jnp.float32,
    )
    summed = lax.psum(weight_term, ("rec", "rep"))
    share_rows = feature_dim // rec_count
    weight_part = lax.dynamic_slice_in_dim(
        summed, lax.axis_index("rec") * share_rows, share_rows, 0
    )
    return (emb_grad[None], weight_part)


def solution(mesh):
    return jax.shard_map(
        on_device,
        mesh=mesh,
        in_specs=(
            P("rep", "rec", None),
            P(),
            P("rep", "rec", None),
            P("rep", "rec", None),
            P("rep", "rec"),
        ),
        out_specs=(P("rep", "rec", None), P("rec", None)),
        check_vma=False,
    )
```

profile of v0, /device:TPU:2, one launch (start us, length us, event | category | flops | bytes accessed | tf_op | source)
XLA Modules:
  0.0 503.8 jit_solution(4040648699400386685)
XLA Ops:
  12.9 42.1 %scatter_fusion = s32[64,12]{0,1:T(8,128)S(1)} fusion(s32[64,12]{0,1:T(8,128)S(1)} %broadcast_in_dim.13, s32[792]{0:T(1024)S(1)} %fusion.20, s32[792]{0:T(1024)S(1)} %get-tuple-element.8), kind=kCustom, calls=%fused_computation.1 | custom fusion | bytes 15840 | tf_op jit(solution)/shard_map/scatter | solution.py:76
  55.1 20.4 %all_to_all.19 = s32[64,1,12]{2,1,0:T(1,128)S(1)} all-to-all(s32[64,1,12]{2,1,0:T(1,128)S(1)} %copy.20), channel_id=1, replica_groups=mesh['rec'=64,'rep'=4] {'rec'}, dimensions={0} | all-to-all | bytes 6144 | tf_op jit(solution)/shard_map/all_to_all | solution.py:78
  76.8 3.6 convolution_convert_fusion.3
  80.4 3.6 reshape.199
  84.0 6.5 %all-to-all-start.1 = ((bf16[64,12,1024]{2,1,0:T(8,128)(2,1)}), bf16[64,12,1024]{2,1,0:T(8,128)(2,1)}, u32[]{:S(2)}, u32[]{:S(2)}) async-start(bf16[64,12,1024]{2,1,0:T(8,128)(2,1)} %reshape.199), calls=%async_computation.1 | async-start | bytes 4194304 | tf_op jit(solution)/shard_map/all_to_all | solution.py:86
  90.6 49.4 %all-to-all-done.1 = bf16[64,12,1024]{2,1,0:T(8,128)(2,1)} async-done(((bf16[64,12,1024]{2,1,0:T(8,128)(2,1)}), bf16[64,12,1024]{2,1,0:T(8,128)(2,1)}, u32[]{:S(2)}, u32[]{:S(2)}) %all-to-all-start.1) | async-done | bytes 1572896 | tf_op jit(solution)/shard_map/all_to_all | solution.py:86
  140.0 3.6 reshape.200
  143.6 2.9 fusion.2
  146.5 3.1 convolution_convert_fusion.1
  149.6 3.0 convolution_convert_fusion.2
  152.7 3.1 reshape.202
  155.8 3.1 reshape.203
  158.8 3.1 reshape.201
  166.2 8.3 %scatter_fusion.1 = f32[8,99,99]{2,0,1:T(8,128)S(1)} fusion(f32[8,99,99]{2,0,1:T(8,128)S(1)} %copy.21, s32[128]{0:T(128)S(1)} %get-tuple-element.2, f32[128]{0:T(128)S(1)} %divide_multiply_fusion), kind=kCustom, calls=%fused_computation.2 | custom fusion | flops 128 | bytes 3072 | tf_op jit(solution)/shard_map/scatter-add | solution.py:40
  178.7 3.1 reshape.204
  181.8 4.5 fusion.3
  186.3 3.6 reshape.205
  189.9 7.7 %all-to-all-start.2 = ((bf16[64,12,1024]{2,1,0:T(8,128)(2,1)}), bf16[64,12,1024]{2,1,0:T(8,128)(2,1)}, u32[]{:S(2)}, u32[]{:S(2)}) async-start(bf16[64,12,1024]{2,1,0:T(8,128)(2,1)} %reshape.205), calls=%async_computation.2 | async-start | bytes 4194304 | tf_op jit(solution)/shard_map/all_to_all | solution.py:99
  197.7 3.3 convolution_convert_fusion
  201.0 3.1 reshape.207
  204.1 6.2 %fusion.27 = f32[1024,1024]{1,0:T(8,128)} fusion(bf16[792,1024]{1,0:T(8,128)(2,1)} %copy-done.2, bf16[792,1024]{1,0:T(8,128)(2,1)} %reshape.207), kind=kOutput, calls=%fused_computation.76 | convolution fusion | flops 1660944384 | bytes 7438336 | tf_op jit(solution)/shard_map/dot_general | solution.py:52
  210.3 278.0 %all-reduce.3.cloned.1.call-done = f32[1024,1024]{1,0:T(8,128)} async-done(((f32[1024,1024]{1,0:T(8,128)}), f32[1024,1024]{1,0:T(8,128)}) %all-reduce.3.cloned.1.call-update) | async-done | bytes 4194320 | tf_op jit(solution)/shard_map/psum | solution.py:106
  489.8 3.6 reshape.206
  493.5 3.4 convolution_bitcast_fusion
  (48 shorter events, 17.0 us)
Async XLA Ops:
  7.2 139.3 %copy-start = (bf16[1024,1024]{1,0:T(8,128)(2,1)S(1)}, bf16[1024,1024]{1,0:T(8,128)(2,1)}, u32[]{:S(2)}) copy-start(bf16[1024,1024]{1,0:T(8,128)(2,1)} %param.6) | copy-start | bytes 6291460
  84.0 6.5 %copy-start.3 = (s32[1,128,2]{1,2,0:T(2,128)S(1)}, s32[1,128,2]{1,2,0:T(2,128)}, u32[]{:S(2)}) copy-start(s32[1,128,2]{1,2,0:T(2,128)} %param.8) | copy-start | bytes 3076
  84.0 56.0 %all-to-all-start.1 = ((bf16[64,12,1024]{2,1,0:T(8,128)(2,1)}), bf16[64,12,1024]{2,1,0:T(8,128)(2,1)}, u32[]{:S(2)}, u32[]{:S(2)}) async-start(bf16[64,12,1024]{2,1,0:T(8,128)(2,1)} %reshape.199), calls=%async_computation.1 | async-start | bytes 4194304 | tf_op jit(solution)/shard_map/all_to_all | solution.py:86
  146.5 3.1 copy-start.2
  162.0 4.2 copy-start.4
  174.5 2.2 copy-start.1
  189.9 299.9 %all-to-all-start.2 = ((bf16[64,12,1024]{2,1,0:T(8,128)(2,1)}), bf16[64,12,1024]{2,1,0:T(8,128)(2,1)}, u32[]{:S(2)}, u32[]{:S(2)}) async-start(bf16[64,12,1024]{2,1,0:T(8,128)(2,1)} %reshape.205), calls=%async_computation.2 | async-start | bytes 4194304 | tf_op jit(solution)/shard_map/all_to_all | solution.py:99
  197.7 290.7 %all-reduce.3.cloned.1.call-start = ((), (), s32[]{:S(2)}) async-start(), calls=%async_computation.3 | async-start | bytes 8388608 | tf_op jit(solution)/shard_map/psum | solution.py:106
Sparse Core Ops, SparseCore 0:
  210.4 277.8 all-reduce.2
where the time goes:
time: 505 us; the launch traced here: 504 us
  waiting for transfers between devices  327 us (65%)
  local copies, waits for them, and re-layouts  76.8 us (15%)
  matrix products  36.8 us (7%)
  blocking collectives  20.4 us (4%)
  starting transfers between devices  14.3 us (3%)
  between operations  14.3 us (3%)
  other arithmetic  13.8 us (3%)
    psum x1, waiting for transfers between devices, on_device(): summed = lax.psum(weight_term, ('rec', 'rep'))  278 us
    all_to_all x1, waiting for transfers between devices, on_device(): lax.all_to_all(found_rows, 'rec', split_axis=0, concat_axis=0, tiled=True)  49.4 us
    scatter x1, local copies, waits for them, and re-layouts, on_device(): requests = jnp.full((rec_count, CAP), -1, jnp.int32).at[source_dev, bucke...  42.1 us
    all_to_all x1, blocking collectives, on_device(): lax.all_to_all(requests, 'rec', split_axis=0, concat_axis=0, tiled=True)  20.4 us
  transfers between devices with their start and end apart: 3, of which 2 were waited for; matrix products, arithmetic and copies ran while one was open for 3% of the time, Pallas kernels for 0%

commit v1 on v0

v1 whole, which is shorter than its diff:
```python
import jax
import jax.numpy as jnp
from jax import lax
from jax.experimental import pallas as pl
from jax.experimental.pallas import tpu as pltpu
from jax.sharding import Mesh, PartitionSpec as P

f32, bf16, i32 = jnp.float32, jnp.bfloat16, jnp.int32

CAP = 12
LIVE = 264
SUB = 272
LAN = 384
MARGIN = 0.5
NX, NZ, NC, NY = 4, 8, 2, 4
REC = ("x", "z", "c")
MIB = 2**20


def iota(shape, dim):
    return lax.broadcasted_iota(i32, shape, dim)


def ones_where(mask):
    return jnp.where(mask, 1.0, 0.0).astype(f32)


def nt(a, b):
    return lax.dot_general(a, b, (((1,), (1,)), ((), ())), preferred_element_type=f32)


def tn(a, b):
    return lax.dot_general(a, b, (((0,), (0,)), ((), ())), preferred_element_type=f32)


def mm(a, b):
    return jnp.dot(a, b, preferred_element_type=f32)


def bucket_tables(members_ref, padded, n_rec, rec_rows):
    blocks, most = members_ref.shape
    padded[...] = jnp.full(padded.shape, -1, i32)
    padded[:, :most] = members_ref[...]
    earlier = ones_where(iota((128, 128), 0) < iota((128, 128), 1)).astype(bf16)
    running = jnp.zeros((n_rec, 1), f32)
    out = []
    for b in range(blocks):
        ids = padded[b : b + 1, :]
        source = (lax.shift_right_arithmetic(ids, 7) * 171) >> 9
        row = ids - source * rec_rows
        source = jnp.where(ids >= 0, source, -1)
        hit = ones_where(iota((n_rec, 128), 0) == source)
        place = mm(hit.astype(bf16), earlier) + running
        running = running + jnp.sum(hit, axis=1, keepdims=True)
        out.append((source, row, hit, place))
    return out


def request_kernel(members_ref, out_ref, padded):
    n_rec = out_ref.shape[0]
    tables = bucket_tables(members_ref, padded, n_rec, LAN)
    lane = iota((n_rec, 128), 1)
    asked = jnp.zeros((n_rec, 128), f32)
    for k in range(CAP):
        found = jnp.zeros((n_rec, 128), f32)
        for source, row, hit, place in tables:
            found = found + jnp.where(place == k, hit, 0.0) * (row + 1).astype(f32)
        asked = jnp.where(lane == k, jnp.sum(found, axis=1, keepdims=True), asked)
    out_ref[...] = asked.astype(i32).reshape(out_ref.shape)


def fetch_kernel(asked_ref, emb_ref, out_ref, pick_ref):
    n_rec = asked_ref.shape[0]
    half = out_ref.shape[1]
    rows = n_rec * 2 * CAP
    asked = asked_ref[...].reshape(n_rec, 1, 128).astype(f32)
    step = iota((n_rec, 2 * CAP, 128), 1)
    step = jnp.where(step >= CAP, step - CAP, step)
    mine = jnp.where(iota((n_rec, 2 * CAP, 128), 2) == step, asked, 0.0)
    wanted = jnp.sum(mine, axis=2, keepdims=True).astype(i32) - 1
    wanted = wanted + jnp.where(iota((n_rec, 2 * CAP, 1), 1) >= CAP, jnp.where(wanted >= 0, LAN, 0), 0)
    pick = ones_where(iota((n_rec, 2 * CAP, 2 * LAN), 2) == wanted).reshape(rows, 2 * LAN).astype(bf16)
    pick_ref[...] = pick
    left = emb_ref[:, :half].astype(bf16)
    right = emb_ref[:, half:].astype(bf16)
    out_ref[...] = mm(pick, jnp.concatenate([left, right], axis=0)).astype(bf16)


def prepare_kernel(members_ref, pairs_ref, labels_ref, gather_ref, spread_ref, share_ref, plus_ref, minus_ref, padded):
    n_rec = gather_ref.shape[1] // (2 * CAP)
    blocks, most = members_ref.shape
    tables = bucket_tables(members_ref, padded, n_rec, LAN)
    sub = iota((LAN, 128), 0)
    lane = iota((1, 128), 1)
    offset = jnp.zeros((1, 1), i32)
    offsets, lengths = [], []
    bucket = jnp.zeros((LAN, 1), f32)
    for b, (source, row, hit, place) in enumerate(tables):
        live = source >= 0
        length = jnp.sum(ones_where(live), axis=1, keepdims=True).astype(i32)
        offsets.append(offset)
        lengths.append(length)
        slot = jnp.where(live, offset + lane, -1)
        offset = offset + length
        at = jnp.sum(hit * place, axis=0, keepdims=True) + (source * (2 * CAP) + 1).astype(f32)
        bucket = bucket + jnp.sum(jnp.where(sub == slot, at, 0.0), axis=1, keepdims=True)
    bucket_col = bucket.astype(i32) - 1
    bucket_col = jnp.where(bucket_col < 0, -4096, bucket_col)
    bucket_row = jnp.transpose(jnp.broadcast_to(bucket, (LAN, 128)))[0:1, :].astype(i32) - 1
    bucket_row = jnp.where(bucket_row < 0, -4096, bucket_row)
    arrivals = gather_ref.shape[1]
    lanes = iota((SUB, arrivals), 1)
    gather_ref[:SUB, :] = ones_where(lanes == bucket_col[:SUB]).astype(bf16)
    gather_ref[SUB:, :] = ones_where(lanes == bucket_col[:SUB] + CAP).astype(bf16)
    rows = iota((arrivals, LAN), 0)
    spread_ref[:, :LAN] = ones_where(rows == bucket_row).astype(bf16)
    spread_ref[:, LAN:] = ones_where(rows == bucket_row + CAP).astype(bf16)

    col, row = iota((SUB, 1), 0), iota((1, LAN), 1)
    block_col, block_row = jnp.zeros((SUB, 1), i32), jnp.zeros((1, LAN), i32)
    count = jnp.zeros((1, LAN), f32) + lengths[0].astype(f32)
    for b in range(1, blocks):
        block_col = jnp.where(col >= offsets[b], b, block_col)
        block_row = jnp.where(row >= offsets[b], b, block_row)
        count = jnp.where(row >= offsets[b], lengths[b].astype(f32), count)
    block_col = jnp.where(col < LIVE, block_col, -1)
    block_row = jnp.where(row < LIVE, block_row, -2)
    inverse = 1.0 / count
    share_ref[...] = jnp.where((block_col == block_row) & (col != row), inverse, 0.0)

    def packed(slots):
        at = jnp.zeros((1, 128), i32) + offsets[0]
        first = jnp.zeros((1, 128), i32)
        for b in range(1, blocks):
            at = jnp.where(slots >= b * most, offsets[b], at)
            first = jnp.where(slots >= b * most, b * most, first)
        return at + slots - first

    label = labels_ref[...].astype(f32)
    one = jnp.where(iota((SUB, 128), 0) == packed(pairs_ref[0:1, :]), 1.0, 0.0)
    two = ones_where(iota((LAN, 128), 0) == packed(pairs_ref[1:2, :])).astype(bf16)
    plus_ref[...] = nt((one * (1.0 - label)).astype(bf16), two)
    minus_ref[...] = nt((one * label).astype(bf16), two)


def owner_kernel(
    arrived_ref, gather_ref, spread_ref, share_ref, plus_ref, minus_ref, weight_ref,
    out_ref, rows_ref, dscore_ref, right_s, stacked_s,
):
    half = arrived_ref.shape[1]
    both = mm(gather_ref[...], arrived_ref[...]).astype(bf16)
    rows_ref[:SUB, :half] = both[:SUB]
    rows_ref[:SUB, half:] = both[SUB:]
    rows_ref[SUB:, :] = jnp.zeros((LAN - SUB, 2 * half), bf16)
    rows = rows_ref[:SUB, :]
    left = mm(rows, weight_ref[...]).astype(bf16)
    right_s[:SUB, :] = nt(rows, weight_ref[...]).astype(bf16)
    right_s[SUB:, :] = jnp.zeros((LAN - SUB, 2 * half), bf16)
    shifted = nt(left, rows_ref[...]) - MARGIN
    small = jnp.exp(-jnp.abs(shifted))
    larger = 1.0 / (1.0 + small)
    smaller = small * larger
    up = jnp.where(shifted >= 0, larger, smaller)
    down = jnp.where(shifted >= 0, smaller, larger)
    dscore = (up * share_ref[...] + (up * plus_ref[...] - down * minus_ref[...])).astype(bf16)
    dscore_ref[...] = dscore
    grad = mm(dscore, right_s[...]) + tn(dscore, left)[:SUB]
    grad = grad.astype(bf16)
    stacked_s[:SUB, :] = grad[:, :half]
    stacked_s[SUB:LAN, :] = jnp.zeros((LAN - SUB, half), bf16)
    stacked_s[LAN : LAN + SUB, :] = grad[:, half:]
    stacked_s[LAN + SUB :, :] = jnp.zeros((LAN - SUB, half), bf16)
    out_ref[...] = mm(spread_ref[...], stacked_s[...]).astype(bf16)


def weight_kernel(core_ref, rows_ref, dscore_ref, keep_ref, send_ref):
    width = rows_ref.shape[1]
    core = core_ref[0]
    carried = mm(dscore_ref[...], rows_ref[...]).astype(bf16)
    tile = 256
    for t in range(width // tile):
        part = tn(rows_ref[:SUB, t * tile : (t + 1) * tile], carried)
        part = part.reshape(tile // 32, 2, 16, width)
        even = jnp.broadcast_to(core, (tile // 32, 16, width)) == 0
        keep_ref[t * 8 : (t + 1) * 8] = jnp.where(even, part[:, 0], part[:, 1])
        send_ref[t * 8 : (t + 1) * 8] = jnp.where(even, part[:, 1], part[:, 0]).astype(bf16)


def return_kernel(pick_ref, back_ref, out_ref):
    half = back_ref.shape[1]
    total = mm(pick_ref[...], back_ref[...])
    rec_rows = out_ref.shape[0]
    out_ref[:, :half] = total[:rec_rows]
    out_ref[:, half:] = total[rec_rows:]


def vmem(n):
    return [pl.BlockSpec(memory_space=pltpu.VMEM)] * n


def call(kernel, outs, n_in, scratch=(), flops=0, moved=0, smem=0):
    single = not isinstance(outs, (list, tuple))
    return pl.pallas_call(
        kernel,
        out_shape=outs,
        in_specs=[pl.BlockSpec(memory_space=pltpu.SMEM)] * smem + vmem(n_in),
        out_specs=vmem(1)[0] if single else vmem(len(outs)),
        scratch_shapes=list(scratch),
        compiler_params=pltpu.CompilerParams(vmem_limit_bytes=40 * MIB),
        cost_estimate=pl.CostEstimate(flops=flops, bytes_accessed=moved, transcendentals=0),
    )


def shifted_blocks(value, axis, size):
    here = lax.axis_index(axis)
    got = []
    for k in range(1, size):
        block = lax.dynamic_index_in_dim(value, (here + k) % size, 0, keepdims=False).astype(bf16)
        got.append(lax.ppermute(block, axis, [(i, (i + k) % size) for i in range(size)]))
    total = lax.dynamic_index_in_dim(value, here, 0, keepdims=False)
    for block in got:
        total = total + block.astype(f32)
    return total


def on_device(embeddings, weight, members, pair_slots, labels):
    n_rec = NX * NZ * NC
    rec_rows, width = embeddings.shape[1:]
    half = width // 2
    arrivals = n_rec * 2 * CAP
    struct = jax.ShapeDtypeStruct
    ids = members[0]
    padded = pltpu.VMEM((ids.shape[0], 128), i32)

    requests = call(request_kernel, struct((n_rec, 1, 128), i32), 1, [padded])(ids)
    asked = lax.all_to_all(requests, REC, split_axis=0, concat_axis=0, tiled=True)
    found, pick = call(
        fetch_kernel, [struct((arrivals, half), bf16), struct((arrivals, 2 * rec_rows), bf16)], 2,
        flops=4 * arrivals * rec_rows * half, moved=6 * MIB,
    )(asked, embeddings[0])
    arrived = lax.all_to_all(
        found.reshape(n_rec, 2 * CAP, half), REC, split_axis=0, concat_axis=0, tiled=True
    ).reshape(arrivals, half)
    gather, spread, share, plus, minus = call(
        prepare_kernel,
        [struct((2 * SUB, arrivals), bf16), struct((arrivals, 2 * LAN), bf16)] + [struct((SUB, LAN), f32)] * 3,
        3, [padded], moved=6 * MIB,
    )(ids, pair_slots[0].T, labels)
    pick_t = pick.T

    out, rows, dscore = call(
        owner_kernel,
        [struct((arrivals, half), bf16), struct((LAN, width), bf16), struct((SUB, LAN), bf16)],
        7,
        [pltpu.VMEM((LAN, width), bf16), pltpu.VMEM((2 * LAN, half), bf16)],
        flops=4 * 10**9, moved=12 * MIB,
    )(arrived, gather, spread, share, plus, minus, weight)
    returned = lax.all_to_all(
        out.reshape(n_rec, 2 * CAP, half), REC, split_axis=0, concat_axis=0, tiled=True
    ).reshape(arrivals, half)

    core = lax.axis_index("c").astype(i32).reshape(1)
    shares = NX * NZ
    keep, send = call(
        weight_kernel, [struct((shares, 16, width), f32), struct((shares, 16, width), bf16)], 2,
        flops=10**9, moved=8 * MIB, smem=1,
    )(core, rows, dscore)
    got = lax.ppermute(send, "c", [(0, 1), (1, 0)])
    summed = (keep + got.astype(f32)).reshape(shares * 16, NY, width // NY).swapaxes(0, 1)
    summed = shifted_blocks(summed, "y", NY)
    summed = shifted_blocks(summed.reshape(NX, NZ * 16, width // NY), "x", NX)
    summed = shifted_blocks(summed.reshape(NZ, 16, width // NY), "z", NZ)
    weight_part = lax.all_gather(summed, "y", axis=1, tiled=True)

    emb_grad = call(
        return_kernel, struct((rec_rows, width), f32), 2,
        flops=4 * arrivals * rec_rows * half, moved=6 * MIB,
    )(pick_t, returned)
    return (emb_grad[None], weight_part)


def solution(mesh):
    fine = Mesh(mesh.devices.reshape(NX, NZ, NC, NY), ("x", "z", "c", "y"))
    return jax.shard_map(
        on_device,
        mesh=fine,
        in_specs=(
            P("y", REC, None),
            P(),
            P("y", REC, None),
            P("y", REC, None),
            P("y", REC),
        ),
        out_specs=(P("y", REC, None), P(REC, None)),
        check_vma=False,
    )
```

time: 505 us -> 168 us (0.33)
  waiting for transfers between devices: 327 us -> 51.2 us
  local copies, waits for them, and re-layouts: 76.8 us -> 24 us
  matrix products: 36.8 us -> 0 us
  starting transfers between devices: 14.3 us -> 38.1 us
  Pallas kernels: 0 us -> 17.3 us
  between operations: 14.3 us -> 0.85 us
  blocking collectives: 20.4 us -> 32.3 us
  other arithmetic: 13.8 us -> 3.06 us
    psum x1 -> x0, waiting for transfers between devices: 278 us -> none  [on_device(): summed = lax.psum(weight_term, ('rec', 'rep'))]
    scatter x1 -> x0, local copies, waits for them, and re-layouts: 42.1 us -> none  [on_device(): requests = jnp.full((rec_count, CAP), -1, jnp.int32).at[source_dev, bucke...]
    dot_general x11 -> x0, matrix products: 36.8 us -> none  [the longest x1 6.22 us: owner_terms(): lax.dot_general(rows, carried.reshape(-1, feature_dim), (((0,), (0,)), ((...]
    reshape x9 -> x1, local copies, waits for them, and re-layouts: 30 us -> 2.2 us  [on_device(): (keep + got.astype(f32)).reshape(shares * 16, NY, width // NY)]
    ppermute x0 -> x14, starting transfers between devices: none -> 24.9 us  [the longest x13 24.7 us: shifted_blocks(): lax.ppermute(block, axis, [(i, (i + k) % size) for i in range(size)])]
    ppermute x0 -> x14, waiting for transfers between devices: none -> 18.7 us  [the longest x13 16 us: shifted_blocks(): lax.ppermute(block, axis, [(i, (i + k) % size) for i in range(size)])]
    pallas_call x0 -> x6, Pallas kernels: none -> 17.3 us  [the longest x1 5.91 us: on_device(): call(owner_kernel, [struct((arrivals, half), bf16), struct((LAN, width),...]
    unnamed x10 -> x38, local copies, waits for them, and re-layouts: 0.03 us -> 17 us
  transfers between devices with their start and end apart: 3 -> 16, of which waited for: 2 -> 6; matrix products, arithmetic and copies ran while one was open for 3% -> 7% of each run, Pallas kernels for 0% -> 2%
where the time goes in v1:
time: 168 us; the launch traced here: 167 us
  waiting for transfers between devices  51.2 us (30%)
  starting transfers between devices  38.1 us (23%)
  blocking collectives  32.3 us (19%)
  local copies, waits for them, and re-layouts  24 us (14%)
  Pallas kernels  17.3 us (10%)
  other arithmetic  3.06 us (2%)
    all_to_all x1, waiting for transfers between devices, on_device(): lax.all_to_all(found.reshape(n_rec, 2 * CAP, half), REC, split_axis=0, co...  32.5 us
    ppermute x13, starting transfers between devices, shifted_blocks(): lax.ppermute(block, axis, [(i, (i + k) % size) for i in range(size)])  24.7 us
    all_to_all x1, blocking collectives, on_device(): lax.all_to_all(requests, REC, split_axis=0, concat_axis=0, tiled=True)  20.4 us
    unnamed x38, local copies, waits for them, and re-layouts  17 us
    ppermute x13, waiting for transfers between devices, shifted_blocks(): lax.ppermute(block, axis, [(i, (i + k) % size) for i in range(size)])  16 us
    all_gather x1, blocking collectives, on_device(): weight_part = lax.all_gather(summed, 'y', axis=1, tiled=True)  11.9 us
    all_to_all x1, starting transfers between devices, on_device(): lax.all_to_all(out.reshape(n_rec, 2 * CAP, half), REC, split_axis=0, conc...  7.5 us
    pallas_call x1, Pallas kernels, on_device(): call(owner_kernel, [struct((arrivals, half), bf16), struct((LAN, width),...  5.91 us
  transfers between devices with their start and end apart: 16, of which 6 were waited for; matrix products, arithmetic and copies ran while one was open for 7% of the time, Pallas kernels for 2%

profile of v1, /device:TPU:2, one launch (start us, length us, event | category | flops | bytes accessed | tf_op | source)
XLA Modules:
  0.0 166.8 jit_solution(2132735282886506086)
XLA Ops:
  2.0 20.4 %all_to_all.15.asked_ref = s32[64,1,128]{2,1,0:T(1,128)S(1)} all-to-all(s32[64,1,128]{2,1,0:T(1,128)S(1)} %shard_map.68), channel_id=1, replica_groups=mesh['x'=4,'z'=8,'c'=2,'y'=4] {'x','z','c'}, dimensions={0} | all-to-all | bytes 65536 | tf_op jit(solution)/shard_map/all_to_all | solution.py:236
  23.8 3.0 %shard_map.69 = (bf16[1536,512]{1,0:T(8,128)(2,1)}, bf16[1536,768]{1,0:T(8,128)(2,1)S(1)}) custom-call(s32[64,1,128]{2,1,0:T(1,128)S(1)} %all_to_all.15.asked_ref, f32[384,1024]{1,0:T(8,128)S(1)} %bitcast.74), custom_call_target="tpu_custom_call" | custom-call | flops 1207959552 | bytes 6291456 | tf_op jit(solution)/shard_map/pallas_call | solution.py:237
  28.2 5.7 %all-to-all-start.1 = ((bf16[64,24,512]{2,1,0:T(8,128)(2,1)}), bf16[64,24,512]{2,1,0:T(8,128)(2,1)S(1)}, u32[]{:S(2)}, u32[]{:S(2)}) async-start(bf16[64,24,512]{2,1,0:T(8,128)(2,1)} %bitcast.3), calls=%async_computation.1 | async-start | bytes 3145728 | tf_op jit(solution)/shard_map/all_to_all | solution.py:241
  34.0 2.3 %shard_map.70 = (bf16[544,1536]{1,0:T(8,128)(2,1)S(1)}, bf16[1536,768]{1,0:T(8,128)(2,1)S(1)}, f32[272,384]{1,0:T(8,128)S(1)}, f32[272,384]{1,0:T(8,128)S(1)}, f32[272,384]{1,0:T(8,128)S(1)}) custom-call(s32[8,99]{1,0:T(8,128)S(1)} %bitcast.72, s32[2,128]{1,0:T(2,128)S(1)} %bitcast.73, s32[1,128]{1,0:T(1,128)S(1)} %copy-done.4), custom_call_target="tpu_custom_call" | custom-call | bytes 6291456 | tf_op jit(solution)/shard_map/pallas_call | solution.py:244
  40.0 32.5 %all-to-all-done.1 = bf16[64,24,512]{2,1,0:T(8,128)(2,1)S(1)} async-done(((bf16[64,24,512]{2,1,0:T(8,128)(2,1)}), bf16[64,24,512]{2,1,0:T(8,128)(2,1)S(1)}, u32[]{:S(2)}, u32[]{:S(2)}) %all-to-all-start.1) | async-done | bytes 1572896 | tf_op jit(solution)/shard_map/all_to_all | solution.py:241
  72.5 1.7 copy-done.6
  78.8 5.9 %shard_map.71 = (bf16[1536,512]{1,0:T(8,128)(2,1)}, bf16[384,1024]{1,0:T(8,128)(2,1)S(1)}, bf16[272,384]{1,0:T(8,128)(2,1)S(1)}) custom-call(bf16[1536,512]{1,0:T(8,128)(2,1)S(1)} %bitcast.70, bf16[544,1536]{1,0:T(8,128)(2,1)S(1)} %get-tuple-element.16.gather_ref, bf16[1536,768]{1,0:T(8,128)(2,1)S(1)} %copy-done.6, f32[272,384]{1,0:T(8,128)S(1)} %copy-done.10, ...), custom_call_target="tpu_custom_call" | custom-call | flops 4000000000 | bytes 12582912 | tf_op jit(solution)/shard_map/pallas_call | solution.py:251
  85.6 7.5 %all-to-all-start.2 = ((bf16[64,24,512]{2,1,0:T(8,128)(2,1)}), bf16[64,24,512]{2,1,0:T(8,128)(2,1)}, u32[]{:S(2)}, u32[]{:S(2)}) async-start(bf16[64,24,512]{2,1,0:T(8,128)(2,1)} %bitcast.7), calls=%async_computation.2 | async-start | bytes 3145728 | tf_op jit(solution)/shard_map/all_to_all | solution.py:258
  96.1 2.6 %collective-permute-done = bf16[32,16,1024]{2,1,0:T(8,128)(2,1)} collective-permute-done((bf16[32,16,1024]{2,1,0:T(8,128)(2,1)S(1)}, bf16[32,16,1024]{2,1,0:T(8,128)(2,1)}, u32[]{:S(2)}, u32[]{:S(2)}) %collective-permute-start) | collective-permute-done | bytes 1048608 | tf_op jit(solution)/shard_map/ppermute | solution.py:268
  98.7 2.9 %convert_add_fusion = f32[32,16,1024]{2,1,0:T(8,128)} fusion(f32[32,16,1024]{2,1,0:T(8,128)S(1)} %get-tuple-element.24, bf16[32,16,1024]{2,1,0:T(8,128)(2,1)} %collective-permute-done), kind=kLoop, calls=%fused_computation | loop fusion | flops 1048576 | bytes 5242880 | tf_op jit(solution)/shard_map/add | solution.py:269
  101.6 2.2 %reshape.54 = f32[512,4,256]{2,1,0:T(4,128)S(1)} reshape(f32[32,16,1024]{2,1,0:T(8,128)} %convert_add_fusion) | data formatting | bytes 4194304 | tf_op jit(solution)/shard_map/reshape | solution.py:269
  105.3 3.1 %collective-permute-start.3 = (bf16[512,256]{1,0:T(8,128)(2,1)S(1)}, bf16[512,256]{1,0:T(8,128)(2,1)S(1)}, u32[]{:S(2)}, u32[]{:S(2)}) collective-permute-start(bf16[512,256]{1,0:T(8,128)(2,1)S(1)} %bitcast.80), channel_id=1, source_target_pairs={{0,3},{1,0},{2,1},{3,2},{4,7},{5,4},{6,5},{7,6},{8,11},{9,8},{10,9... | collective-permute-start | bytes 786440 | tf_op jit(solution)/shard_map/ppermute | solution.py:219
  111.3 8.6 %collective-permute-done.3 = bf16[512,256]{1,0:T(8,128)(2,1)S(1)} collective-permute-done((bf16[512,256]{1,0:T(8,128)(2,1)S(1)}, bf16[512,256]{1,0:T(8,128)(2,1)S(1)}, u32[]{:S(2)}, u32[]{:S(2)}) %collective-permute-start.3) | collective-permute-done | bytes 262176 | tf_op jit(solution)/shard_map/ppermute | solution.py:219
  119.9 3.8 %collective-permute-done.1 = bf16[512,256]{1,0:T(8,128)(2,1)S(1)} collective-permute-done((bf16[512,256]{1,0:T(8,128)(2,1)}, bf16[512,256]{1,0:T(8,128)(2,1)S(1)}, u32[]{:S(2)}, u32[]{:S(2)}) %collective-permute-start.1) | collective-permute-done | bytes 262176 | tf_op jit(solution)/shard_map/ppermute | solution.py:219
  124.6 2.3 %collective-permute-start.5 = (bf16[128,256]{1,0:T(8,128)(2,1)S(1)}, bf16[128,256]{1,0:T(8,128)(2,1)S(1)}, u32[]{:S(2)}, u32[]{:S(2)}) collective-permute-start(bf16[128,256]{1,0:T(8,128)(2,1)S(1)} %get-tuple-element.31), channel_id=1, source_target_pairs={{0,128},{64,192},{128,0},{192,64},{1,129},{65,193},{129,1},{193,65... | collective-permute-start | bytes 196616 | tf_op jit(solution)/shard_map/ppermute | solution.py:219
  127.0 1.9 %collective-permute-start.4 = (bf16[128,256]{1,0:T(8,128)(2,1)S(1)}, bf16[128,256]{1,0:T(8,128)(2,1)S(1)}, u32[]{:S(2)}, u32[]{:S(2)}) collective-permute-start(bf16[128,256]{1,0:T(8,128)(2,1)S(1)} %get-tuple-element.29), channel_id=1, source_target_pairs={{0,64},{64,128},{128,192},{192,0},{1,65},{65,129},{129,193},{193,1... | collective-permute-start | bytes 196616 | tf_op jit(solution)/shard_map/ppermute | solution.py:219
  128.8 2.9 %collective-permute-done.5 = bf16[128,256]{1,0:T(8,128)(2,1)S(1)} collective-permute-done((bf16[128,256]{1,0:T(8,128)(2,1)S(1)}, bf16[128,256]{1,0:T(8,128)(2,1)S(1)}, u32[]{:S(2)}, u32[]{:S(2)}) %collective-permute-start.5) | collective-permute-done | bytes 65568 | tf_op jit(solution)/shard_map/ppermute | solution.py:219
  131.8 2.8 %collective-permute-start.13 = (bf16[16,256]{1,0:T(8,128)(2,1)S(1)}, bf16[16,256]{1,0:T(8,128)(2,1)S(1)}, u32[]{:S(2)}, u32[]{:S(2)}) collective-permute-start(bf16[16,256]{1,0:T(8,128)(2,1)S(1)} %get-tuple-element.33), channel_id=1, source_target_pairs={{0,56},{8,0},{16,8},{24,16},{32,24},{40,32},{48,40},{56,48},{1,57}... | collective-permute-start | bytes 24584 | tf_op jit(solution)/shard_map/ppermute | solution.py:219
  134.6 2.2 %collective-permute-start.12 = (bf16[16,256]{1,0:T(8,128)(2,1)S(1)}, bf16[16,256]{1,0:T(8,128)(2,1)S(1)}, u32[]{:S(2)}, u32[]{:S(2)}) collective-permute-start(bf16[16,256]{1,0:T(8,128)(2,1)S(1)} %get-tuple-element.34), channel_id=1, source_target_pairs={{0,48},{8,56},{16,0},{24,8},{32,16},{40,24},{48,32},{56,40},{1,49}... | collective-permute-start | bytes 24584 | tf_op jit(solution)/shard_map/ppermute | solution.py:219
  138.0 4.0 %collective-permute-start.10 = (bf16[16,256]{1,0:T(8,128)(2,1)S(1)}, bf16[16,256]{1,0:T(8,128)(2,1)S(1)}, u32[]{:S(2)}, u32[]{:S(2)}) collective-permute-start(bf16[16,256]{1,0:T(8,128)(2,1)S(1)} %get-tuple-element.36), channel_id=1, source_target_pairs={{0,32},{8,40},{16,48},{24,56},{32,0},{40,8},{48,16},{56,24},{1,33}... | collective-permute-start | bytes 24584 | tf_op jit(solution)/shard_map/ppermute | solution.py:219
  142.2 3.4 %collective-permute-start.8 = (bf16[16,256]{1,0:T(8,128)(2,1)S(1)}, bf16[16,256]{1,0:T(8,128)(2,1)S(1)}, u32[]{:S(2)}, u32[]{:S(2)}) collective-permute-start(bf16[16,256]{1,0:T(8,128)(2,1)S(1)} %get-tuple-element.38), channel_id=1, source_target_pairs={{0,16},{8,24},{16,32},{24,40},{32,48},{40,56},{48,0},{56,8},{1,17}... | collective-permute-start | bytes 24584 | tf_op jit(solution)/shard_map/ppermute | solution.py:219
  146.8 2.8 %copy.10 = bf16[1536,768]{0,1:T(8,128)(2,1)S(1)} copy(bf16[1536,768]{1,0:T(8,128)(2,1)} %copy-done) | data formatting | bytes 4718592 | tf_op jit(solution)/shard_map/pallas_call | solution.py:237
  150.4 11.9 %all_gather.3 = f32[16,1024]{1,0:T(8,128)S(1)} all-gather(f32[16,256]{1,0:T(8,128)S(1)} %fusion.15), channel_id=1, replica_groups=mesh['x'=4,'z'=8,'c'=2,'y'=4] {'y'}, dimensions={1}, use_global_device_ids=true | all-gather | bytes 81920 | tf_op jit(solution)/shard_map/all_gather | solution.py:273
  162.3 3.9 %shard_map.72 = f32[384,1024]{1,0:T(8,128)} custom-call(bf16[768,1536]{1,0:T(8,128)(2,1)S(1)} %bitcast.69, bf16[1536,512]{1,0:T(8,128)(2,1)} %bitcast.8.back_ref), custom_call_target="tpu_custom_call" | custom-call | flops 1207959552 | bytes 6291456 | tf_op jit(solution)/shard_map/pallas_call | solution.py:275
  (64 shorter events, 25.6 us)
Async XLA Ops:
  22.4 1.4 copy-start.8
  26.8 1.4 copy-start
  28.2 5.7 %copy-start.2 = (s32[1,8,99]{2,1,0:T(8,128)S(1)}, s32[1,8,99]{2,1,0:T(8,128)}, u32[]{:S(2)}) copy-start(s32[1,8,99]{2,1,0:T(8,128)} %param.7) | copy-start | bytes 9508
  28.2 5.7 %copy-start.3 = (s32[1,128,2]{1,2,0:T(2,128)S(1)}, s32[1,128,2]{1,2,0:T(2,128)}, u32[]{:S(2)}) copy-start(s32[1,128,2]{1,2,0:T(2,128)} %param.8) | copy-start | bytes 3076
  28.2 5.7 %copy-start.4 = (s32[1,128]{1,0:T(1,128)S(1)}, s32[1,128]{1,0:T(1,128)}, u32[]{:S(2)}) copy-start(s32[1,128]{1,0:T(1,128)} %labels_ref.1) | copy-start | bytes 1540
  28.2 44.3 %all-to-all-start.1 = ((bf16[64,24,512]{2,1,0:T(8,128)(2,1)}), bf16[64,24,512]{2,1,0:T(8,128)(2,1)S(1)}, u32[]{:S(2)}, u32[]{:S(2)}) async-start(bf16[64,24,512]{2,1,0:T(8,128)(2,1)} %bitcast.3), calls=%async_computation.1 | async-start | bytes 3145728 | tf_op jit(solution)/shard_map/all_to_all | solution.py:241
  36.3 1.4 copy-start.5
  72.5 1.7 copy-start.6
  74.2 1.6 copy-start.7
  85.6 76.7 %all-to-all-start.2 = ((bf16[64,24,512]{2,1,0:T(8,128)(2,1)}), bf16[64,24,512]{2,1,0:T(8,128)(2,1)}, u32[]{:S(2)}, u32[]{:S(2)}) async-start(bf16[64,24,512]{2,1,0:T(8,128)(2,1)} %bitcast.7), calls=%async_computation.2 | async-start | bytes 3145728 | tf_op jit(solution)/shard_map/all_to_all | solution.py:258
  95.8 2.9 %collective-permute-start = (bf16[32,16,1024]{2,1,0:T(8,128)(2,1)S(1)}, bf16[32,16,1024]{2,1,0:T(8,128)(2,1)}, u32[]{:S(2)}, u32[]{:S(2)}) collective-permute-start(bf16[32,16,1024]{2,1,0:T(8,128)(2,1)S(1)} %get-tuple-element.25), channel_id=1, source_target_pairs={{0,4},{4,0},{1,5},{5,1},{2,6},{6,2},{3,7},{7,3},{8,12},{12,8},{9,1... | collective-permute-start | bytes 3145736 | tf_op jit(solution)/shard_map/ppermute | solution.py:268
  105.3 14.6 %collective-permute-start.3 = (bf16[512,256]{1,0:T(8,128)(2,1)S(1)}, bf16[512,256]{1,0:T(8,128)(2,1)S(1)}, u32[]{:S(2)}, u32[]{:S(2)}) collective-permute-start(bf16[512,256]{1,0:T(8,128)(2,1)S(1)} %bitcast.80), channel_id=1, source_target_pairs={{0,3},{1,0},{2,1},{3,2},{4,7},{5,4},{6,5},{7,6},{8,11},{9,8},{10,9... | collective-permute-start | bytes 786440 | tf_op jit(solution)/shard_map/ppermute | solution.py:219
  108.4 11.5 %collective-permute-start.2 = (bf16[512,256]{1,0:T(8,128)(2,1)S(1)}, bf16[512,256]{1,0:T(8,128)(2,1)S(1)}, u32[]{:S(2)}, u32[]{:S(2)}) collective-permute-start(bf16[512,256]{1,0:T(8,128)(2,1)S(1)} %bitcast.81), channel_id=1, source_target_pairs={{0,2},{1,3},{2,0},{3,1},{4,6},{5,7},{6,4},{7,5},{8,10},{9,11},{10,... | collective-permute-start | bytes 786440 | tf_op jit(solution)/shard_map/ppermute | solution.py:219
  109.9 13.8 %collective-permute-start.1 = (bf16[512,256]{1,0:T(8,128)(2,1)}, bf16[512,256]{1,0:T(8,128)(2,1)S(1)}, u32[]{:S(2)}, u32[]{:S(2)}) collective-permute-start(bf16[512,256]{1,0:T(8,128)(2,1)} %bitcast.66), channel_id=1, source_target_pairs={{0,1},{1,2},{2,3},{3,0},{4,5},{5,6},{6,7},{7,4},{8,9},{9,10},{10,1... | collective-permute-start | bytes 786440 | tf_op jit(solution)/shard_map/ppermute | solution.py:219
  123.9 5.0 %collective-permute-start.6 = (bf16[128,256]{1,0:T(8,128)(2,1)S(1)}, bf16[128,256]{1,0:T(8,128)(2,1)S(1)}, u32[]{:S(2)}, u32[]{:S(2)}) collective-permute-start(bf16[128,256]{1,0:T(8,128)(2,1)S(1)} %get-tuple-element.30), channel_id=1, source_target_pairs={{0,192},{64,0},{128,64},{192,128},{1,193},{65,1},{129,65},{193,129... | collective-permute-start | bytes 196616 | tf_op jit(solution)/shard_map/ppermute | solution.py:219
  124.6 7.2 %collective-permute-start.5 = (bf16[128,256]{1,0:T(8,128)(2,1)S(1)}, bf16[128,256]{1,0:T(8,128)(2,1)S(1)}, u32[]{:S(2)}, u32[]{:S(2)}) collective-permute-start(bf16[128,256]{1,0:T(8,128)(2,1)S(1)} %get-tuple-element.31), channel_id=1, source_target_pairs={{0,128},{64,192},{128,0},{192,64},{1,129},{65,193},{129,1},{193,65... | collective-permute-start | bytes 196616 | tf_op jit(solution)/shard_map/ppermute | solution.py:219
  127.0 4.8 %collective-permute-start.4 = (bf16[128,256]{1,0:T(8,128)(2,1)S(1)}, bf16[128,256]{1,0:T(8,128)(2,1)S(1)}, u32[]{:S(2)}, u32[]{:S(2)}) collective-permute-start(bf16[128,256]{1,0:T(8,128)(2,1)S(1)} %get-tuple-element.29), channel_id=1, source_target_pairs={{0,64},{64,128},{128,192},{192,0},{1,65},{65,129},{129,193},{193,1... | collective-permute-start | bytes 196616 | tf_op jit(solution)/shard_map/ppermute | solution.py:219
  131.8 10.3 %collective-permute-start.13 = (bf16[16,256]{1,0:T(8,128)(2,1)S(1)}, bf16[16,256]{1,0:T(8,128)(2,1)S(1)}, u32[]{:S(2)}, u32[]{:S(2)}) collective-permute-start(bf16[16,256]{1,0:T(8,128)(2,1)S(1)} %get-tuple-element.33), channel_id=1, source_target_pairs={{0,56},{8,0},{16,8},{24,16},{32,24},{40,32},{48,40},{56,48},{1,57}... | collective-permute-start | bytes 24584 | tf_op jit(solution)/shard_map/ppermute | solution.py:219
  134.6 10.9 %collective-permute-start.12 = (bf16[16,256]{1,0:T(8,128)(2,1)S(1)}, bf16[16,256]{1,0:T(8,128)(2,1)S(1)}, u32[]{:S(2)}, u32[]{:S(2)}) collective-permute-start(bf16[16,256]{1,0:T(8,128)(2,1)S(1)} %get-tuple-element.34), channel_id=1, source_target_pairs={{0,48},{8,56},{16,0},{24,8},{32,16},{40,24},{48,32},{56,40},{1,49}... | collective-permute-start | bytes 24584 | tf_op jit(solution)/shard_map/ppermute | solution.py:219
  136.9 12.8 %collective-permute-start.11 = (bf16[16,256]{1,0:T(8,128)(2,1)S(1)}, bf16[16,256]{1,0:T(8,128)(2,1)S(1)}, u32[]{:S(2)}, u32[]{:S(2)}) collective-permute-start(bf16[16,256]{1,0:T(8,128)(2,1)S(1)} %get-tuple-element.35), channel_id=1, source_target_pairs={{0,40},{8,48},{16,56},{24,0},{32,8},{40,16},{48,24},{56,32},{1,41}... | collective-permute-start | bytes 24584 | tf_op jit(solution)/shard_map/ppermute | solution.py:219
  138.0 11.6 %collective-permute-start.10 = (bf16[16,256]{1,0:T(8,128)(2,1)S(1)}, bf16[16,256]{1,0:T(8,128)(2,1)S(1)}, u32[]{:S(2)}, u32[]{:S(2)}) collective-permute-start(bf16[16,256]{1,0:T(8,128)(2,1)S(1)} %get-tuple-element.36), channel_id=1, source_target_pairs={{0,32},{8,40},{16,48},{24,56},{32,0},{40,8},{48,16},{56,24},{1,33}... | collective-permute-start | bytes 24584 | tf_op jit(solution)/shard_map/ppermute | solution.py:219
  142.1 7.6 %collective-permute-start.9 = (bf16[16,256]{1,0:T(8,128)(2,1)S(1)}, bf16[16,256]{1,0:T(8,128)(2,1)S(1)}, u32[]{:S(2)}, u32[]{:S(2)}) collective-permute-start(bf16[16,256]{1,0:T(8,128)(2,1)S(1)} %get-tuple-element.37), channel_id=1, source_target_pairs={{0,24},{8,32},{16,40},{24,48},{32,56},{40,0},{48,8},{56,16},{1,25}... | collective-permute-start | bytes 24584 | tf_op jit(solution)/shard_map/ppermute | solution.py:219
  142.2 7.5 %collective-permute-start.8 = (bf16[16,256]{1,0:T(8,128)(2,1)S(1)}, bf16[16,256]{1,0:T(8,128)(2,1)S(1)}, u32[]{:S(2)}, u32[]{:S(2)}) collective-permute-start(bf16[16,256]{1,0:T(8,128)(2,1)S(1)} %get-tuple-element.38), channel_id=1, source_target_pairs={{0,16},{8,24},{16,32},{24,40},{32,48},{40,56},{48,0},{56,8},{1,17}... | collective-permute-start | bytes 24584 | tf_op jit(solution)/shard_map/ppermute | solution.py:219
  145.5 4.9 %collective-permute-start.7 = (bf16[16,256]{1,0:T(8,128)(2,1)S(1)}, bf16[16,256]{1,0:T(8,128)(2,1)S(1)}, u32[]{:S(2)}, u32[]{:S(2)}) collective-permute-start(bf16[16,256]{1,0:T(8,128)(2,1)S(1)} %get-tuple-element.32), channel_id=1, source_target_pairs={{0,8},{8,16},{16,24},{24,32},{32,40},{40,48},{48,56},{56,0},{1,9},... | collective-permute-start | bytes 24584 | tf_op jit(solution)/shard_map/ppermute | solution.py:219
  (9 other events, 8.1 us)

commit v2 on v1

v2 whole, which is shorter than its diff:
```python
import jax
import jax.numpy as jnp
from jax import lax
from jax.experimental import pallas as pl
from jax.experimental.pallas import tpu as pltpu
from jax.sharding import Mesh, PartitionSpec as P

f32, bf16, i32 = jnp.float32, jnp.bfloat16, jnp.int32

CAP = 12
LIVE = 264
SUB = 272
LAN = 384
MARGIN = 0.5
NX, NZ, NC, NY = 4, 8, 2, 4
REC = ("x", "z", "c")
MIB = 2**20


def iota(shape, dim):
    return lax.broadcasted_iota(i32, shape, dim)


def ones_where(mask):
    return jnp.where(mask, 1.0, 0.0).astype(f32)


def nt(a, b):
    return lax.dot_general(a, b, (((1,), (1,)), ((), ())), preferred_element_type=f32)


def tn(a, b):
    return lax.dot_general(a, b, (((0,), (0,)), ((), ())), preferred_element_type=f32)


def mm(a, b):
    return jnp.dot(a, b, preferred_element_type=f32)


def bucket_tables(members_ref, padded, n_rec, rec_rows):
    blocks, most = members_ref.shape
    padded[...] = jnp.full(padded.shape, -1, i32)
    padded[:, :most] = members_ref[...]
    earlier = ones_where(iota((128, 128), 0) < iota((128, 128), 1)).astype(bf16)
    running = jnp.zeros((n_rec, 1), f32)
    out = []
    for b in range(blocks):
        ids = padded[b : b + 1, :]
        source = (lax.shift_right_arithmetic(ids, 7) * 171) >> 9
        row = ids - source * rec_rows
        source = jnp.where(ids >= 0, source, -1)
        hit = ones_where(iota((n_rec, 128), 0) == source)
        place = mm(hit.astype(bf16), earlier) + running
        running = running + jnp.sum(hit, axis=1, keepdims=True)
        out.append((source, row, hit, place))
    return out


def request_kernel(members_ref, out_ref, padded):
    n_rec = out_ref.shape[0]
    tables = bucket_tables(members_ref, padded, n_rec, LAN)
    lane = iota((n_rec, 128), 1)
    asked = jnp.zeros((n_rec, 128), f32)
    for k in range(CAP):
        found = jnp.zeros((n_rec, 128), f32)
        for source, row, hit, place in tables:
            found = found + jnp.where(place == k, hit, 0.0) * (row + 1).astype(f32)
        asked = jnp.where(lane == k, jnp.sum(found, axis=1, keepdims=True), asked)
    out_ref[...] = asked.astype(i32).reshape(out_ref.shape)


def wanted_rows(asked_ref):
    n_rec = asked_ref.shape[0]
    asked = asked_ref[...].reshape(n_rec, 1, 128).astype(f32)
    step = iota((n_rec, 2 * CAP, 128), 1)
    step = jnp.where(step >= CAP, step - CAP, step)
    mine = jnp.where(iota((n_rec, 2 * CAP, 128), 2) == step, asked, 0.0)
    wanted = jnp.sum(mine, axis=2, keepdims=True).astype(i32) - 1
    later = iota((n_rec, 2 * CAP, 1), 1) >= CAP
    return wanted + jnp.where(later & (wanted >= 0), LAN, 0)


def fetch_kernel(asked_ref, emb_ref, out_ref, table, sem):
    n_rec = asked_ref.shape[0]
    half = out_ref.shape[1]
    rows = n_rec * 2 * CAP
    load = pltpu.make_async_copy(emb_ref, table, sem)
    load.start()
    wanted = wanted_rows(asked_ref)
    pick = ones_where(iota((n_rec, 2 * CAP, 2 * LAN), 2) == wanted).reshape(rows, 2 * LAN).astype(bf16)
    load.wait()
    left = table[:, :half].astype(bf16)
    right = table[:, half:].astype(bf16)
    out_ref[...] = mm(pick, jnp.concatenate([left, right], axis=0)).astype(bf16)


def prepare_kernel(
    members_ref, pairs_ref, labels_ref, asked_ref,
    gather_ref, table_ref, back_ref, padded,
):
    arrivals = gather_ref.shape[1]
    n_rec = arrivals // (2 * CAP)
    blocks, most = members_ref.shape
    tables = bucket_tables(members_ref, padded, n_rec, LAN)
    sub = iota((LAN, 128), 0)
    lane = iota((1, 128), 1)
    offset = jnp.zeros((1, 1), i32)
    offsets, lengths = [], []
    bucket = jnp.zeros((LAN, 1), f32)
    for b, (source, row, hit, place) in enumerate(tables):
        live = source >= 0
        length = jnp.sum(ones_where(live), axis=1, keepdims=True).astype(i32)
        offsets.append(offset)
        lengths.append(length)
        slot = jnp.where(live, offset + lane, -1)
        offset = offset + length
        at = jnp.sum(hit * place, axis=0, keepdims=True) + (source * (2 * CAP) + 1).astype(f32)
        bucket = bucket + jnp.sum(jnp.where(sub == slot, at, 0.0), axis=1, keepdims=True)
    bucket_col = bucket.astype(i32) - 1
    bucket_col = jnp.where(bucket_col < 0, -4096, bucket_col)
    bucket_row = jnp.transpose(jnp.broadcast_to(bucket, (LAN, 128)))[0:1, :].astype(i32) - 1
    bucket_row = jnp.where(bucket_row < 0, -4096, bucket_row)
    lanes = iota((SUB, arrivals), 1)
    gather_ref[:SUB, :] = ones_where(lanes == bucket_col[:SUB]).astype(bf16)
    gather_ref[SUB:, :] = ones_where(lanes == bucket_col[:SUB] + CAP).astype(bf16)
    rows = iota((arrivals, LAN), 0)
    table_ref[:arrivals, :LAN] = ones_where(rows == bucket_row).astype(bf16)
    table_ref[:arrivals, LAN:] = ones_where(rows == bucket_row + CAP).astype(bf16)

    col, row = iota((SUB, 1), 0), iota((1, LAN), 1)
    block_col, block_row = jnp.zeros((SUB, 1), i32), jnp.zeros((1, LAN), i32)
    count = jnp.zeros((1, LAN), f32) + lengths[0].astype(f32)
    for b in range(1, blocks):
        block_col = jnp.where(col >= offsets[b], b, block_col)
        block_row = jnp.where(row >= offsets[b], b, block_row)
        count = jnp.where(row >= offsets[b], lengths[b].astype(f32), count)
    block_col = jnp.where(col < LIVE, block_col, -1)
    block_row = jnp.where(row < LIVE, block_row, -2)
    counts = jnp.where((block_col == block_row) & (col != row), count, 0.0)
    table_ref[arrivals : arrivals + SUB, :LAN] = counts.astype(bf16)

    def packed(slots):
        at = jnp.zeros((1, 128), i32) + offsets[0]
        first = jnp.zeros((1, 128), i32)
        for b in range(1, blocks):
            at = jnp.where(slots >= b * most, offsets[b], at)
            first = jnp.where(slots >= b * most, b * most, first)
        return at + slots - first

    label = labels_ref[...].astype(f32)
    one = jnp.where(iota((SUB, 128), 0) == packed(pairs_ref[0:1, :]), 1.0, 0.0)
    two = ones_where(iota((LAN, 128), 0) == packed(pairs_ref[1:2, :])).astype(bf16)
    table_ref[arrivals : arrivals + SUB, LAN:] = nt((one * (1.0 - label)).astype(bf16), two).astype(bf16)
    table_ref[arrivals + SUB :, :LAN] = nt((one * label).astype(bf16), two).astype(bf16)
    table_ref[arrivals + SUB :, LAN:] = jnp.zeros((SUB, LAN), bf16)
    wanted = wanted_rows(asked_ref).reshape(arrivals, 1).astype(f32)
    wanted = jnp.transpose(jnp.broadcast_to(wanted, (arrivals, 128)))[0:1, :].astype(i32)
    back_ref[...] = ones_where(iota((2 * LAN, arrivals), 0) == wanted).astype(bf16)


def owner_kernel(
    core_ref, arrived_ref, gather_hbm, weight_hbm, table_hbm,
    out_ref, keep_ref, send_ref,
    gather_s, rows_s, right_s, stacked_s, weight_s, spread_s, terms_s, sems,
):
    arrivals, half = arrived_ref.shape
    width = 2 * half
    terms_hbm, spread_hbm = table_hbm.at[arrivals:], table_hbm.at[:arrivals]
    loads = []
    for n, (source, target) in enumerate(
        [(gather_hbm, gather_s), (weight_hbm, weight_s), (terms_hbm, terms_s), (spread_hbm, spread_s)]
    ):
        loads.append(pltpu.make_async_copy(source, target, sems.at[n]))
        loads[n].start()
    loads[0].wait()
    both = mm(gather_s[...], arrived_ref[...]).astype(bf16)
    rows_s[:SUB, :half] = both[:SUB]
    rows_s[:SUB, half:] = both[SUB:]
    rows_s[SUB:, :] = jnp.zeros((LAN - SUB, width), bf16)
    rows = rows_s[:SUB, :]
    loads[1].wait()
    left = mm(rows, weight_s[...]).astype(bf16)
    right_s[:SUB, :] = nt(rows, weight_s[...]).astype(bf16)
    right_s[SUB:, :] = jnp.zeros((LAN - SUB, width), bf16)
    shifted = nt(left, rows_s[...]) - MARGIN
    small = jnp.exp(-jnp.abs(shifted))
    larger = 1.0 / (1.0 + small)
    smaller = small * larger
    up = jnp.where(shifted >= 0, larger, smaller)
    down = jnp.where(shifted >= 0, smaller, larger)
    loads[2].wait()
    count = terms_s[:SUB, :LAN].astype(f32)
    plus = terms_s[:SUB, LAN:].astype(f32)
    minus = terms_s[SUB:, :LAN].astype(f32)
    dscore = jnp.where(count > 0, up / jnp.maximum(count, 1.0), 0.0) + (up * plus - down * minus)
    dscore = dscore.astype(bf16)
    grad = mm(dscore, right_s[...]) + tn(dscore, left)[:SUB]
    grad = grad.astype(bf16)
    stacked_s[:SUB, :] = grad[:, :half]
    stacked_s[SUB:LAN, :] = jnp.zeros((LAN - SUB, half), bf16)
    stacked_s[LAN : LAN + SUB, :] = grad[:, half:]
    stacked_s[LAN + SUB :, :] = jnp.zeros((LAN - SUB, half), bf16)
    loads[3].wait()
    out_ref[...] = mm(spread_s[...], stacked_s[...]).astype(bf16)
    carried = mm(dscore, rows_s[...]).astype(bf16)
    core = core_ref[0]
    tile = 256
    for t in range(width // tile):
        part = tn(rows_s[:SUB, t * tile : (t + 1) * tile], carried)
        part = part.reshape(tile // 32, 2, 16, width)
        even = jnp.broadcast_to(core, (tile // 32, 16, width)) == 0
        here = jnp.where(even, part[:, 0], part[:, 1]).reshape(tile // 2, width)
        there = jnp.where(even, part[:, 1], part[:, 0]).reshape(tile // 2, width)
        keep_ref[t * tile // 2 : (t + 1) * tile // 2, :] = here
        send_ref[t * tile // 2 : (t + 1) * tile // 2, :] = there.astype(bf16)


def split_kernel(y_ref, keep_ref, got_ref, own_ref, *send_refs):
    size = own_ref.shape[1]
    for k in range(NY):
        at = pl.multiple_of(((y_ref[0] + k) % NY) * size, size)
        part = keep_ref[:, pl.ds(at, size)] + got_ref[:, pl.ds(at, size)].astype(f32)
        if k == 0:
            own_ref[...] = part
        else:
            send_refs[k - 1][...] = part.astype(bf16)


def join_kernel(y_ref, *refs):
    *piece_refs, out_ref = refs
    size = piece_refs[0].shape[1]
    for k, piece_ref in enumerate(piece_refs):
        at = pl.multiple_of(((y_ref[0] + NY - k) % NY) * size, size)
        out_ref[:, pl.ds(at, size)] = piece_ref[...]


def return_kernel(back_ref, pick_hbm, out_ref, pick_s, sem):
    half = back_ref.shape[1]
    load = pltpu.make_async_copy(pick_hbm, pick_s, sem)
    load.start()
    load.wait()
    total = mm(pick_s[...], back_ref[...])
    rec_rows = out_ref.shape[0]
    out_ref[:, :half] = total[:rec_rows]
    out_ref[:, half:] = total[rec_rows:]


def vmem(n):
    return [pl.BlockSpec(memory_space=pltpu.VMEM)] * n


def call(kernel, outs, n_in, scratch=(), flops=0, moved=0, smem=0, hbm=0, grant=60):
    single = not isinstance(outs, (list, tuple))
    return pl.pallas_call(
        kernel,
        out_shape=outs,
        in_specs=[pl.BlockSpec(memory_space=pltpu.SMEM)] * smem + vmem(n_in) + [pl.BlockSpec(memory_space=pltpu.HBM)] * hbm,
        out_specs=vmem(1)[0] if single else vmem(len(outs)),
        scratch_shapes=list(scratch),
        compiler_params=pltpu.CompilerParams(vmem_limit_bytes=int(grant * MIB)),
        cost_estimate=pl.CostEstimate(flops=flops, bytes_accessed=moved, transcendentals=0),
    )


def shifted_blocks(value, axis, size):
    here = lax.axis_index(axis)
    got = []
    for k in range(1, size):
        block = lax.dynamic_index_in_dim(value, (here + k) % size, 0, keepdims=False).astype(bf16)
        got.append(lax.ppermute(block, axis, [(i, (i + k) % size) for i in range(size)]))
    total = lax.dynamic_index_in_dim(value, here, 0, keepdims=False)
    for block in got:
        total = total + block.astype(f32)
    return total


def on_device(embeddings, weight, members, pair_slots, labels):
    n_rec = NX * NZ * NC
    rec_rows, width = embeddings.shape[1:]
    half = width // 2
    arrivals = n_rec * 2 * CAP
    struct = jax.ShapeDtypeStruct
    ids = members[0]
    padded = pltpu.VMEM((ids.shape[0], 128), i32)

    requests = call(request_kernel, struct((n_rec, 1, 128), i32), 1, [padded])(ids)
    asked = lax.all_to_all(requests, REC, split_axis=0, concat_axis=0, tiled=True)
    dma = pltpu.SemaphoreType.DMA
    found = call(
        fetch_kernel, struct((arrivals, half), bf16), 1,
        [pltpu.VMEM((rec_rows, width), f32), dma],
        flops=4 * arrivals * rec_rows * half, moved=4 * MIB, hbm=1,
    )(asked, embeddings[0])
    arrived = lax.all_to_all(
        found.reshape(n_rec, 2 * CAP, half), REC, split_axis=0, concat_axis=0, tiled=True
    ).reshape(arrivals, half)
    gather, table, back = call(
        prepare_kernel,
        [
            struct((2 * SUB, arrivals), bf16),
            struct((arrivals + 2 * SUB, 2 * LAN), bf16),
            struct((2 * LAN, arrivals), bf16),
        ],
        4, [padded], moved=8 * MIB,
    )(ids, pair_slots[0].T, labels, asked)

    core = lax.axis_index("c").astype(i32).reshape(1)
    rows_core = width // NC
    out, keep, send = call(
        owner_kernel,
        [struct((arrivals, half), bf16), struct((rows_core, width), f32), struct((rows_core, width), bf16)],
        1,
        [pltpu.VMEM((2 * SUB, arrivals), bf16)]
        + [pltpu.VMEM((LAN, width), bf16)] * 2
        + [pltpu.VMEM((2 * LAN, half), bf16), pltpu.VMEM((width, width), bf16), pltpu.VMEM((arrivals, 2 * LAN), bf16)]
        + [pltpu.VMEM((2 * SUB, 2 * LAN), bf16)]
        + [dma((4,))],
        flops=5 * 10**9, moved=12 * MIB, smem=1, hbm=3, grant=49.5,
    )(core, arrived, gather, weight, table)
    got = lax.ppermute(send, "c", [(0, 1), (1, 0)])
    returned = lax.all_to_all(
        out.reshape(n_rec, 2 * CAP, half), REC, split_axis=0, concat_axis=0, tiled=True
    ).reshape(arrivals, half)

    y = lax.axis_index("y").astype(i32).reshape(1)
    cols = width // NY
    summed, *sends = call(
        split_kernel,
        [struct((rows_core, cols), f32)] + [struct((rows_core, cols), bf16)] * (NY - 1), 2,
        flops=10**6, moved=4 * MIB, smem=1, grant=16,
    )(y, keep, got)
    for k in range(1, NY):
        summed = summed + lax.ppermute(sends[k - 1], "y", [(i, (i + k) % NY) for i in range(NY)]).astype(f32)
    summed = shifted_blocks(summed.reshape(NX, NZ * 16, cols), "x", NX)
    half_z = NZ // 2
    z = lax.axis_index("z")
    summed = summed.reshape(2, half_z, 16, cols)
    far = lax.dynamic_index_in_dim(summed, 1 - z // half_z, 0, keepdims=False).astype(bf16)
    near = lax.dynamic_index_in_dim(summed, z // half_z, 0, keepdims=False)
    far = lax.ppermute(far, "z", [(i, (i + half_z) % NZ) for i in range(NZ)])
    summed = near + far.astype(f32)
    blocks = []
    for k in range(1, half_z):
        block = lax.dynamic_index_in_dim(summed, (z + k) % half_z, 0, keepdims=False).astype(bf16)
        to = [(i, i // half_z * half_z + (i + k) % half_z) for i in range(NZ)]
        blocks.append(lax.ppermute(block, "z", to))
    summed = lax.dynamic_index_in_dim(summed, z % half_z, 0, keepdims=False)
    for block in blocks:
        summed = summed + block.astype(f32)
    pieces = [summed]
    for k in range(1, NY):
        pieces.append(lax.ppermute(summed, "y", [(i, (i + k) % NY) for i in range(NY)]))
    emb_grad = call(
        return_kernel, struct((rec_rows, width), f32), 1, [pltpu.VMEM((2 * rec_rows, arrivals), bf16), dma],
        flops=4 * arrivals * rec_rows * half, moved=6 * MIB, hbm=1, grant=52,
    )(returned, back)
    emb_grad, pieces = lax.optimization_barrier((emb_grad, pieces))
    weight_part = call(join_kernel, struct((16, width), f32), NY, smem=1, flops=10**4, moved=10**5, grant=16)(y, *pieces)

    return (emb_grad[None], weight_part)


def solution(mesh):
    fine = Mesh(mesh.devices.reshape(NX, NZ, NC, NY), ("x", "z", "c", "y"))
    return jax.shard_map(
        on_device,
        mesh=fine,
        in_specs=(
            P("y", REC, None),
            P(),
            P("y", REC, None),
            P("y", REC, None),
            P("y", REC),
        ),
        out_specs=(P("y", REC, None), P(REC, None)),
        check_vma=False,
    )
```

time: 168 us -> 151 us (0.90)
  local copies, waits for them, and re-layouts: 24 us -> 2.64 us
  blocking collectives: 32.3 us -> 20.7 us
  Pallas kernels: 17.3 us -> 28.1 us
  waiting for transfers between devices: 51.2 us -> 60 us
  other arithmetic: 3.06 us -> 0.15 us
    ppermute x13 -> x3, starting transfers between devices: 24.7 us -> 4.98 us  [shifted_blocks(): lax.ppermute(block, axis, [(i, (i + k) % size) for i in range(size)])]
    ppermute x0 -> x10, waiting for transfers between devices: none -> 19.4 us  [the longest x3 13.7 us: on_device(): lax.ppermute(sends[k - 1], 'y', [(i, (i + k) % NY) for i in range(NY)])]
    ppermute x0 -> x10, starting transfers between devices: none -> 18.8 us  [the longest x1 5.74 us: on_device(): far = lax.ppermute(far, 'z', [(i, (i + half_z) % NZ) for i in range(NZ)])]
    unnamed x38 -> x4, local copies, waits for them, and re-layouts: 17 us -> 2.57 us
    all_gather x1 -> x0, blocking collectives: 11.9 us -> none  [on_device(): weight_part = lax.all_gather(summed, 'y', axis=1, tiled=True)]
    ppermute x13 -> x3, waiting for transfers between devices: 16 us -> 5.48 us  [shifted_blocks(): lax.ppermute(block, axis, [(i, (i + k) % size) for i in range(size)])]
    pallas_call x4 -> x5, Pallas kernels: 14.4 us -> 20 us  [the longest x1 9.37 us: on_device(): call(owner_kernel, [struct((arrivals, half), bf16), struct((rows_core, wi...]
    pallas_call x1, Pallas kernels: 2.3 us -> 6.16 us  [on_device(): call(prepare_kernel, [struct((2 * SUB, arrivals), bf16), struct((arrivals...]
  transfers between devices with their start and end apart: 16 -> 16, of which waited for: 6 -> 9; matrix products, arithmetic and copies ran while one was open for 7% -> 0% of each run, Pallas kernels for 2% -> 8%
where the time goes in v2:
time: 151 us; the launch traced here: 149 us
  waiting for transfers between devices  60 us (40%)
  starting transfers between devices  36.8 us (24%)
  Pallas kernels  28.1 us (19%)
  blocking collectives  20.7 us (14%)
  local copies, waits for them, and re-layouts  2.64 us (2%)
    all_to_all x1, waiting for transfers between devices, on_device(): lax.all_to_all(found.reshape(n_rec, 2 * CAP, half), REC, split_axis=0, co...  32.4 us
    all_to_all x1, blocking collectives, on_device(): lax.all_to_all(requests, REC, split_axis=0, concat_axis=0, tiled=True)  20.7 us
    ppermute x3, waiting for transfers between devices, on_device(): lax.ppermute(sends[k - 1], 'y', [(i, (i + k) % NY) for i in range(NY)])  13.7 us
    pallas_call x1, Pallas kernels, on_device(): call(owner_kernel, [struct((arrivals, half), bf16), struct((rows_core, wi...  9.37 us
    all_to_all x1, starting transfers between devices, on_device(): lax.all_to_all(out.reshape(n_rec, 2 * CAP, half), REC, split_axis=0, conc...  7.32 us
    pallas_call x1, Pallas kernels, on_device(): call(prepare_kernel, [struct((2 * SUB, arrivals), bf16), struct((arrivals...  6.16 us
    ppermute x1, starting transfers between devices, on_device(): far = lax.ppermute(far, 'z', [(i, (i + half_z) % NZ) for i in range(NZ)])  5.74 us
    ppermute x3, waiting for transfers between devices, shifted_blocks(): lax.ppermute(block, axis, [(i, (i + k) % size) for i in range(size)])  5.48 us
  transfers between devices with their start and end apart: 16, of which 9 were waited for; matrix products, arithmetic and copies ran while one was open for 0% of the time, Pallas kernels for 8%

profile of v2, /device:TPU:2, one launch (start us, length us, event | category | flops | bytes accessed | tf_op | source)
XLA Modules:
  0.0 149.1 jit_solution(18316518212928059675)
XLA Ops:
  0.6 2.0 %shard_map.68 = s32[64,1,128]{2,1,0:T(1,128)} custom-call(s32[8,99]{1,0:T(8,128)} %bitcast.50), custom_call_target="tpu_custom_call" | custom-call | tf_op jit(solution)/shard_map/pallas_call | solution.py:286
  2.6 20.7 %all_to_all.15.asked_ref = s32[64,1,128]{2,1,0:T(1,128)} all-to-all(s32[64,1,128]{2,1,0:T(1,128)} %shard_map.68), channel_id=1, replica_groups=mesh['x'=4,'z'=8,'c'=2,'y'=4] {'x','z','c'}, dimensions={0} | all-to-all | bytes 65536 | tf_op jit(solution)/shard_map/all_to_all | solution.py:287
  23.3 4.7 %shard_map.69 = bf16[1536,512]{1,0:T(8,128)(2,1)} custom-call(s32[64,1,128]{2,1,0:T(1,128)} %all_to_all.15.asked_ref, f32[384,1024]{1,0:T(8,128)} %bitcast.53), custom_call_target="tpu_custom_call" | custom-call | flops 1207959552 | bytes 4194304 | tf_op jit(solution)/shard_map/pallas_call | solution.py:289
  28.0 5.4 %all-to-all-start.1 = ((bf16[64,24,512]{2,1,0:T(8,128)(2,1)}), bf16[64,24,512]{2,1,0:T(8,128)(2,1)S(1)}, u32[]{:S(2)}, u32[]{:S(2)}) async-start(bf16[64,24,512]{2,1,0:T(8,128)(2,1)} %bitcast.44), calls=%async_computation.1 | async-start | bytes 3145728 | tf_op jit(solution)/shard_map/all_to_all | solution.py:294
  33.4 6.2 %shard_map.70 = (bf16[544,1536]{1,0:T(8,128)(2,1)}, bf16[2080,768]{1,0:T(8,128)(2,1)}, bf16[768,1536]{1,0:T(8,128)(2,1)}) custom-call(s32[8,99]{1,0:T(8,128)} %bitcast.51, s32[2,128]{1,0:T(2,128)} %bitcast.52, s32[1,128]{1,0:T(1,128)} %labels_ref.1, s32[64,1,128]{2,1,0:T(1,128)} %all_to_all.15.asked_ref), custom_call_target="tpu_custom_call" | custom-call | bytes 8388608 | tf_op jit(solution)/shard_map/pallas_call | solution.py:297
  39.6 32.4 %all-to-all-done.1 = bf16[64,24,512]{2,1,0:T(8,128)(2,1)S(1)} async-done(((bf16[64,24,512]{2,1,0:T(8,128)(2,1)}), bf16[64,24,512]{2,1,0:T(8,128)(2,1)S(1)}, u32[]{:S(2)}, u32[]{:S(2)}) %all-to-all-start.1) | async-done | bytes 1572896 | tf_op jit(solution)/shard_map/all_to_all | solution.py:294
  72.0 9.4 %shard_map.71 = (bf16[1536,512]{1,0:T(8,128)(2,1)}, f32[512,1024]{1,0:T(8,128)}, bf16[512,1024]{1,0:T(8,128)(2,1)S(1)}) custom-call(s32[1]{0:T(128)} %bitcast.core_ref, bf16[1536,512]{1,0:T(8,128)(2,1)S(1)} %bitcast.43, bf16[544,1536]{1,0:T(8,128)(2,1)} %get-tuple-element.17.gather_hbm, bf16[1024,1024]{1,0:T(8,128)(2,1)} %weight_hbm.1, ...), custom_call_target="tpu_custom_call" | custom-call | flops 5000000000 | bytes 12582912 | tf_op jit(solution)/shard_map/pallas_call | solution.py:309
  82.4 7.3 %all-to-all-start.2 = ((bf16[64,24,512]{2,1,0:T(8,128)(2,1)}), bf16[64,24,512]{2,1,0:T(8,128)(2,1)S(1)}, u32[]{:S(2)}, u32[]{:S(2)}) async-start(bf16[64,24,512]{2,1,0:T(8,128)(2,1)} %bitcast.7), calls=%async_computation.2 | async-start | bytes 3145728 | tf_op jit(solution)/shard_map/all_to_all | solution.py:321
  89.9 2.7 %collective-permute-done.got_ref = bf16[512,1024]{1,0:T(8,128)(2,1)S(1)} collective-permute-done((bf16[512,1024]{1,0:T(8,128)(2,1)}, bf16[512,1024]{1,0:T(8,128)(2,1)S(1)}, u32[]{:S(2)}, u32[]{:S(2)}) %collective-permute-start) | collective-permute-done | bytes 1048608 | tf_op jit(solution)/shard_map/ppermute | solution.py:320
  92.7 1.6 %copy-done = f32[512,1024]{1,0:T(8,128)S(1)} copy-done((f32[512,1024]{1,0:T(8,128)S(1)}, f32[512,1024]{1,0:T(8,128)}, u32[]{:S(2)}) %copy-start) | copy-done | bytes 2097176
  95.3 3.0 %collective-permute-start.3 = (bf16[512,256]{1,0:T(8,128)(2,1)}, bf16[512,256]{1,0:T(8,128)(2,1)S(1)}, u32[]{:S(2)}, u32[]{:S(2)}) collective-permute-start(bf16[512,256]{1,0:T(8,128)(2,1)} %get-tuple-element.26), channel_id=1, source_target_pairs={{0,3},{1,0},{2,1},{3,2},{4,7},{5,4},{6,5},{7,6},{8,11},{9,8},{10,9... | collective-permute-start | bytes 786440 | tf_op jit(solution)/shard_map/ppermute | solution.py:333
  99.9 10.2 %collective-permute-done.3 = bf16[512,256]{1,0:T(8,128)(2,1)S(1)} collective-permute-done((bf16[512,256]{1,0:T(8,128)(2,1)}, bf16[512,256]{1,0:T(8,128)(2,1)S(1)}, u32[]{:S(2)}, u32[]{:S(2)}) %collective-permute-start.3) | collective-permute-done | bytes 262176 | tf_op jit(solution)/shard_map/ppermute | solution.py:333
  110.2 3.4 %collective-permute-done.1 = bf16[512,256]{1,0:T(8,128)(2,1)S(1)} collective-permute-done((bf16[512,256]{1,0:T(8,128)(2,1)S(1)}, bf16[512,256]{1,0:T(8,128)(2,1)S(1)}, u32[]{:S(2)}, u32[]{:S(2)}) %collective-permute-start.1) | collective-permute-done | bytes 262176 | tf_op jit(solution)/shard_map/ppermute | solution.py:333
  114.3 2.6 %collective-permute-start.5 = (bf16[128,256]{1,0:T(8,128)(2,1)S(1)}, bf16[128,256]{1,0:T(8,128)(2,1)S(1)}, u32[]{:S(2)}, u32[]{:S(2)}) collective-permute-start(bf16[128,256]{1,0:T(8,128)(2,1)S(1)} %get-tuple-element.34), channel_id=1, source_target_pairs={{0,128},{64,192},{128,0},{192,64},{1,129},{65,193},{129,1},{193,65... | collective-permute-start | bytes 196616 | tf_op jit(solution)/shard_map/ppermute | solution.py:270
  116.8 1.9 %collective-permute-start.4 = (bf16[128,256]{1,0:T(8,128)(2,1)S(1)}, bf16[128,256]{1,0:T(8,128)(2,1)S(1)}, u32[]{:S(2)}, u32[]{:S(2)}) collective-permute-start(bf16[128,256]{1,0:T(8,128)(2,1)S(1)} %get-tuple-element.32), channel_id=1, source_target_pairs={{0,64},{64,128},{128,192},{192,0},{1,65},{65,129},{129,193},{193,1... | collective-permute-start | bytes 196616 | tf_op jit(solution)/shard_map/ppermute | solution.py:270
  119.1 5.1 %collective-permute-done.5 = bf16[128,256]{1,0:T(8,128)(2,1)S(1)} collective-permute-done((bf16[128,256]{1,0:T(8,128)(2,1)S(1)}, bf16[128,256]{1,0:T(8,128)(2,1)S(1)}, u32[]{:S(2)}, u32[]{:S(2)}) %collective-permute-start.5) | collective-permute-done | bytes 65568 | tf_op jit(solution)/shard_map/ppermute | solution.py:270
  124.3 5.7 %collective-permute-start.7 = (bf16[4,16,256]{2,1,0:T(8,128)(2,1)S(1)}, bf16[4,16,256]{2,1,0:T(8,128)(2,1)S(1)}, u32[]{:S(2)}, u32[]{:S(2)}) collective-permute-start(bf16[4,16,256]{2,1,0:T(8,128)(2,1)S(1)} %fusion.5), channel_id=1, source_target_pairs={{0,32},{8,40},{16,48},{24,56},{32,0},{40,8},{48,16},{56,24},{1,33}... | collective-permute-start | bytes 98312 | tf_op jit(solution)/shard_map/ppermute | solution.py:340
  130.0 2.2 %collective-permute-done.7 = bf16[4,16,256]{2,1,0:T(8,128)(2,1)S(1)} collective-permute-done((bf16[4,16,256]{2,1,0:T(8,128)(2,1)S(1)}, bf16[4,16,256]{2,1,0:T(8,128)(2,1)S(1)}, u32[]{:S(2)}, u32[]{:S(2)}) %collective-permute-start.7) | collective-permute-done | bytes 32800 | tf_op jit(solution)/shard_map/ppermute | solution.py:340
  132.2 1.9 %collective-permute-start.10 = (bf16[16,256]{1,0:T(8,128)(2,1)S(1)}, bf16[16,256]{1,0:T(8,128)(2,1)S(1)}, u32[]{:S(2)}, u32[]{:S(2)}) collective-permute-start(bf16[16,256]{1,0:T(8,128)(2,1)S(1)} %get-tuple-element.36), channel_id=1, source_target_pairs={{0,24},{8,0},{16,8},{24,16},{32,56},{40,32},{48,40},{56,48},{1,25}... | collective-permute-start | bytes 24584 | tf_op jit(solution)/shard_map/ppermute | solution.py:346
  134.3 1.9 %collective-permute-start.8 = (bf16[16,256]{1,0:T(8,128)(2,1)S(1)}, bf16[16,256]{1,0:T(8,128)(2,1)S(1)}, u32[]{:S(2)}, u32[]{:S(2)}) collective-permute-start(bf16[16,256]{1,0:T(8,128)(2,1)S(1)} %get-tuple-element.35), channel_id=1, source_target_pairs={{0,8},{8,16},{16,24},{24,0},{32,40},{40,48},{48,56},{56,32},{1,9},... | collective-permute-start | bytes 24584 | tf_op jit(solution)/shard_map/ppermute | solution.py:346
  136.2 2.5 %collective-permute-done.9 = bf16[16,256]{1,0:T(8,128)(2,1)S(1)} collective-permute-done((bf16[16,256]{1,0:T(8,128)(2,1)S(1)}, bf16[16,256]{1,0:T(8,128)(2,1)S(1)}, u32[]{:S(2)}, u32[]{:S(2)}) %collective-permute-start.9) | collective-permute-done | bytes 8224 | tf_op jit(solution)/shard_map/ppermute | solution.py:346
  140.0 2.9 %collective-permute-start.12 = (f32[16,256]{1,0:T(8,128)S(1)}, f32[16,256]{1,0:T(8,128)S(1)}, u32[]{:S(2)}, u32[]{:S(2)}) collective-permute-start(f32[16,256]{1,0:T(8,128)S(1)} %fusion.7.refs_0_), channel_id=1, source_target_pairs={{0,2},{1,3},{2,0},{3,1},{4,6},{5,7},{6,4},{7,5},{8,10},{9,11},{10,... | collective-permute-start | bytes 49160 | tf_op jit(solution)/shard_map/ppermute | solution.py:352
  142.9 1.4 collective-permute-start.13
  144.2 4.2 %shard_map.72 = f32[384,1024]{1,0:T(8,128)} custom-call(bf16[1536,512]{1,0:T(8,128)(2,1)S(1)} %bitcast.42, bf16[768,1536]{1,0:T(8,128)(2,1)} %get-tuple-element.20.pick_hbm), custom_call_target="tpu_custom_call" | custom-call | flops 1207959552 | bytes 6291456 | tf_op jit(solution)/shard_map/pallas_call | solution.py:353
  (27 shorter events, 7.0 us)
Async XLA Ops:
  28.0 44.0 %all-to-all-start.1 = ((bf16[64,24,512]{2,1,0:T(8,128)(2,1)}), bf16[64,24,512]{2,1,0:T(8,128)(2,1)S(1)}, u32[]{:S(2)}, u32[]{:S(2)}) async-start(bf16[64,24,512]{2,1,0:T(8,128)(2,1)} %bitcast.44), calls=%async_computation.1 | async-start | bytes 3145728 | tf_op jit(solution)/shard_map/all_to_all | solution.py:294
  81.4 1.0 copy-start.1
  82.4 61.9 %all-to-all-start.2 = ((bf16[64,24,512]{2,1,0:T(8,128)(2,1)}), bf16[64,24,512]{2,1,0:T(8,128)(2,1)S(1)}, u32[]{:S(2)}, u32[]{:S(2)}) async-start(bf16[64,24,512]{2,1,0:T(8,128)(2,1)} %bitcast.7), calls=%async_computation.2 | async-start | bytes 3145728 | tf_op jit(solution)/shard_map/all_to_all | solution.py:321
  89.7 3.0 %collective-permute-start = (bf16[512,1024]{1,0:T(8,128)(2,1)}, bf16[512,1024]{1,0:T(8,128)(2,1)S(1)}, u32[]{:S(2)}, u32[]{:S(2)}) collective-permute-start(bf16[512,1024]{1,0:T(8,128)(2,1)} %copy-done.1), channel_id=1, source_target_pairs={{0,4},{4,0},{1,5},{5,1},{2,6},{6,2},{3,7},{7,3},{8,12},{12,8},{9,1... | collective-permute-start | bytes 3145736 | tf_op jit(solution)/shard_map/ppermute | solution.py:320
  92.7 1.6 %copy-start = (f32[512,1024]{1,0:T(8,128)S(1)}, f32[512,1024]{1,0:T(8,128)}, u32[]{:S(2)}) copy-start(f32[512,1024]{1,0:T(8,128)} %get-tuple-element.21.keep_ref) | copy-start | bytes 6291460
  95.3 14.8 %collective-permute-start.3 = (bf16[512,256]{1,0:T(8,128)(2,1)}, bf16[512,256]{1,0:T(8,128)(2,1)S(1)}, u32[]{:S(2)}, u32[]{:S(2)}) collective-permute-start(bf16[512,256]{1,0:T(8,128)(2,1)} %get-tuple-element.26), channel_id=1, source_target_pairs={{0,3},{1,0},{2,1},{3,2},{4,7},{5,4},{6,5},{7,6},{8,11},{9,8},{10,9... | collective-permute-start | bytes 786440 | tf_op jit(solution)/shard_map/ppermute | solution.py:333
  98.3 11.8 %collective-permute-start.2 = (bf16[512,256]{1,0:T(8,128)(2,1)}, bf16[512,256]{1,0:T(8,128)(2,1)S(1)}, u32[]{:S(2)}, u32[]{:S(2)}) collective-permute-start(bf16[512,256]{1,0:T(8,128)(2,1)} %get-tuple-element.25), channel_id=1, source_target_pairs={{0,2},{1,3},{2,0},{3,1},{4,6},{5,7},{6,4},{7,5},{8,10},{9,11},{10,... | collective-permute-start | bytes 786440 | tf_op jit(solution)/shard_map/ppermute | solution.py:333
  99.0 14.6 %collective-permute-start.1 = (bf16[512,256]{1,0:T(8,128)(2,1)S(1)}, bf16[512,256]{1,0:T(8,128)(2,1)S(1)}, u32[]{:S(2)}, u32[]{:S(2)}) collective-permute-start(bf16[512,256]{1,0:T(8,128)(2,1)S(1)} %get-tuple-element.24), channel_id=1, source_target_pairs={{0,1},{1,2},{2,3},{3,0},{4,5},{5,6},{6,7},{7,4},{8,9},{9,10},{10,1... | collective-permute-start | bytes 786440 | tf_op jit(solution)/shard_map/ppermute | solution.py:333
  113.7 5.3 %collective-permute-start.6 = (bf16[128,256]{1,0:T(8,128)(2,1)S(1)}, bf16[128,256]{1,0:T(8,128)(2,1)S(1)}, u32[]{:S(2)}, u32[]{:S(2)}) collective-permute-start(bf16[128,256]{1,0:T(8,128)(2,1)S(1)} %get-tuple-element.33), channel_id=1, source_target_pairs={{0,192},{64,0},{128,64},{192,128},{1,193},{65,1},{129,65},{193,129... | collective-permute-start | bytes 196616 | tf_op jit(solution)/shard_map/ppermute | solution.py:270
  114.3 9.9 %collective-permute-start.5 = (bf16[128,256]{1,0:T(8,128)(2,1)S(1)}, bf16[128,256]{1,0:T(8,128)(2,1)S(1)}, u32[]{:S(2)}, u32[]{:S(2)}) collective-permute-start(bf16[128,256]{1,0:T(8,128)(2,1)S(1)} %get-tuple-element.34), channel_id=1, source_target_pairs={{0,128},{64,192},{128,0},{192,64},{1,129},{65,193},{129,1},{193,65... | collective-permute-start | bytes 196616 | tf_op jit(solution)/shard_map/ppermute | solution.py:270
  116.8 7.4 %collective-permute-start.4 = (bf16[128,256]{1,0:T(8,128)(2,1)S(1)}, bf16[128,256]{1,0:T(8,128)(2,1)S(1)}, u32[]{:S(2)}, u32[]{:S(2)}) collective-permute-start(bf16[128,256]{1,0:T(8,128)(2,1)S(1)} %get-tuple-element.32), channel_id=1, source_target_pairs={{0,64},{64,128},{128,192},{192,0},{1,65},{65,129},{129,193},{193,1... | collective-permute-start | bytes 196616 | tf_op jit(solution)/shard_map/ppermute | solution.py:270
  124.3 7.9 %collective-permute-start.7 = (bf16[4,16,256]{2,1,0:T(8,128)(2,1)S(1)}, bf16[4,16,256]{2,1,0:T(8,128)(2,1)S(1)}, u32[]{:S(2)}, u32[]{:S(2)}) collective-permute-start(bf16[4,16,256]{2,1,0:T(8,128)(2,1)S(1)} %fusion.5), channel_id=1, source_target_pairs={{0,32},{8,40},{16,48},{24,56},{32,0},{40,8},{48,16},{56,24},{1,33}... | collective-permute-start | bytes 98312 | tf_op jit(solution)/shard_map/ppermute | solution.py:340
  132.2 4.0 %collective-permute-start.10 = (bf16[16,256]{1,0:T(8,128)(2,1)S(1)}, bf16[16,256]{1,0:T(8,128)(2,1)S(1)}, u32[]{:S(2)}, u32[]{:S(2)}) collective-permute-start(bf16[16,256]{1,0:T(8,128)(2,1)S(1)} %get-tuple-element.36), channel_id=1, source_target_pairs={{0,24},{8,0},{16,8},{24,16},{32,56},{40,32},{48,40},{56,48},{1,25}... | collective-permute-start | bytes 24584 | tf_op jit(solution)/shard_map/ppermute | solution.py:346
  134.2 4.5 %collective-permute-start.9 = (bf16[16,256]{1,0:T(8,128)(2,1)S(1)}, bf16[16,256]{1,0:T(8,128)(2,1)S(1)}, u32[]{:S(2)}, u32[]{:S(2)}) collective-permute-start(bf16[16,256]{1,0:T(8,128)(2,1)S(1)} %get-tuple-element.37), channel_id=1, source_target_pairs={{0,16},{8,24},{16,0},{24,8},{32,48},{40,56},{48,32},{56,40},{1,17}... | collective-permute-start | bytes 24584 | tf_op jit(solution)/shard_map/ppermute | solution.py:346
  134.3 5.4 %collective-permute-start.8 = (bf16[16,256]{1,0:T(8,128)(2,1)S(1)}, bf16[16,256]{1,0:T(8,128)(2,1)S(1)}, u32[]{:S(2)}, u32[]{:S(2)}) collective-permute-start(bf16[16,256]{1,0:T(8,128)(2,1)S(1)} %get-tuple-element.35), channel_id=1, source_target_pairs={{0,8},{8,16},{16,24},{24,0},{32,40},{40,48},{48,56},{56,32},{1,9},... | collective-permute-start | bytes 24584 | tf_op jit(solution)/shard_map/ppermute | solution.py:346
  139.7 8.7 %collective-permute-start.11 = (f32[16,256]{1,0:T(8,128)S(1)}, f32[16,256]{1,0:T(8,128)S(1)}, u32[]{:S(2)}, u32[]{:S(2)}) collective-permute-start(f32[16,256]{1,0:T(8,128)S(1)} %fusion.7.refs_0_), channel_id=1, source_target_pairs={{0,1},{1,2},{2,3},{3,0},{4,5},{5,6},{6,7},{7,4},{8,9},{9,10},{10,1... | collective-permute-start | bytes 49160 | tf_op jit(solution)/shard_map/ppermute | solution.py:352
  140.0 8.5 %collective-permute-start.12 = (f32[16,256]{1,0:T(8,128)S(1)}, f32[16,256]{1,0:T(8,128)S(1)}, u32[]{:S(2)}, u32[]{:S(2)}) collective-permute-start(f32[16,256]{1,0:T(8,128)S(1)} %fusion.7.refs_0_), channel_id=1, source_target_pairs={{0,2},{1,3},{2,0},{3,1},{4,6},{5,7},{6,4},{7,5},{8,10},{9,11},{10,... | collective-permute-start | bytes 49160 | tf_op jit(solution)/shard_map/ppermute | solution.py:352
  142.9 5.6 %collective-permute-start.13 = (f32[16,256]{1,0:T(8,128)S(1)}, f32[16,256]{1,0:T(8,128)S(1)}, u32[]{:S(2)}, u32[]{:S(2)}) collective-permute-start(f32[16,256]{1,0:T(8,128)S(1)} %fusion.7.refs_0_), channel_id=1, source_target_pairs={{0,3},{1,0},{2,1},{3,2},{4,7},{5,4},{6,5},{7,6},{8,11},{9,8},{10,9... | collective-permute-start | bytes 49160 | tf_op jit(solution)/shard_map/ppermute | solution.py:352

commit v3 on v2

--- a/solution.py
+++ b/solution.py
@@ -80,18 +80,27 @@
     return wanted + jnp.where(later & (wanted >= 0), LAN, 0)
 
 
-def fetch_kernel(asked_ref, emb_ref, out_ref, table, sem):
+def stack_kernel(emb_ref, out_ref):
+    rows, width = emb_ref.shape
+    out_ref[:rows, :] = emb_ref[:, : width // 2].astype(bf16)
+    out_ref[rows:, :] = emb_ref[:, width // 2 :].astype(bf16)
+
+
+def fetch_kernel(asked_ref, stacked_ref, out_hbm, out_s, sems):
     n_rec = asked_ref.shape[0]
-    half = out_ref.shape[1]
-    rows = n_rec * 2 * CAP
-    load = pltpu.make_async_copy(emb_ref, table, sem)
-    load.start()
+    parts = sems.shape[0]
+    rows = n_rec * 2 * CAP // parts
     wanted = wanted_rows(asked_ref)
-    pick = ones_where(iota((n_rec, 2 * CAP, 2 * LAN), 2) == wanted).reshape(rows, 2 * LAN).astype(bf16)
-    load.wait()
-    left = table[:, :half].astype(bf16)
-    right = table[:, half:].astype(bf16)
-    out_ref[...] = mm(pick, jnp.concatenate([left, right], axis=0)).astype(bf16)
+    stores = []
+    for t in range(parts):
+        mine = wanted[t * n_rec // parts : (t + 1) * n_rec // parts]
+        pick = ones_where(iota((n_rec // parts, 2 * CAP, 2 * LAN), 2) == mine).reshape(rows, 2 * LAN).astype(bf16)
+        here = pl.ds(t * rows, rows)
+        out_s[here, :] = mm(pick, stacked_ref[...]).astype(bf16)
+        stores.append(pltpu.make_async_copy(out_s.at[here], out_hbm.at[here], sems.at[t]))
+        stores[t].start()
+    for store in stores:
+        store.wait()
 
 
 def prepare_kernel(
@@ -159,26 +168,31 @@
 
 
 def owner_kernel(
-    core_ref, arrived_ref, gather_hbm, weight_hbm, table_hbm,
-    out_ref, keep_ref, send_ref,
-    gather_s, rows_s, right_s, stacked_s, weight_s, spread_s, terms_s, sems,
+    arrived_ref, gather_hbm, weight_hbm, table_hbm,
+    out_hbm, rows_ref, dscore_ref,
+    gather_s, rows_s, right_s, stacked_s, weight_s, spread_s, terms_s, out_s, sems, out_sems,
 ):
     arrivals, half = arrived_ref.shape
     width = 2 * half
     terms_hbm, spread_hbm = table_hbm.at[arrivals:], table_hbm.at[:arrivals]
     loads = []
-    for n, (source, target) in enumerate(
-        [(gather_hbm, gather_s), (weight_hbm, weight_s), (terms_hbm, terms_s), (spread_hbm, spread_s)]
-    ):
+    for n, (source, target) in enumerate([
+        (gather_hbm.at[:SUB], gather_s.at[:SUB]),
+        (gather_hbm.at[SUB:], gather_s.at[SUB:]),
+        (weight_hbm, weight_s),
+        (terms_hbm, terms_s),
+        (spread_hbm, spread_s),
+    ]):
         loads.append(pltpu.make_async_copy(source, target, sems.at[n]))
         loads[n].start()
     loads[0].wait()
-    both = mm(gather_s[...], arrived_ref[...]).astype(bf16)
-    rows_s[:SUB, :half] = both[:SUB]
-    rows_s[:SUB, half:] = both[SUB:]
+    rows_s[:SUB, :half] = mm(gather_s[:SUB, :], arrived_ref[...]).astype(bf16)
+    loads[1].wait()
+    rows_s[:SUB, half:] = mm(gather_s[SUB:, :], arrived_ref[...]).astype(bf16)
     rows_s[SUB:, :] = jnp.zeros((LAN - SUB, width), bf16)
     rows = rows_s[:SUB, :]
-    loads[1].wait()
+    rows_ref[...] = rows
+    loads[2].wait()
     left = mm(rows, weight_s[...]).astype(bf16)
     right_s[:SUB, :] = nt(rows, weight_s[...]).astype(bf16)
     right_s[SUB:, :] = jnp.zeros((LAN - SUB, width), bf16)
@@ -188,31 +202,45 @@
     smaller = small * larger
     up = jnp.where(shifted >= 0, larger, smaller)
     down = jnp.where(shifted >= 0, smaller, larger)
-    loads[2].wait()
+    loads[3].wait()
     count = terms_s[:SUB, :LAN].astype(f32)
     plus = terms_s[:SUB, LAN:].astype(f32)
     minus = terms_s[SUB:, :LAN].astype(f32)
     dscore = jnp.where(count > 0, up / jnp.maximum(count, 1.0), 0.0) + (up * plus - down * minus)
     dscore = dscore.astype(bf16)
+    dscore_ref[...] = dscore
     grad = mm(dscore, right_s[...]) + tn(dscore, left)[:SUB]
     grad = grad.astype(bf16)
     stacked_s[:SUB, :] = grad[:, :half]
     stacked_s[SUB:LAN, :] = jnp.zeros((LAN - SUB, half), bf16)
     stacked_s[LAN : LAN + SUB, :] = grad[:, half:]
     stacked_s[LAN + SUB :, :] = jnp.zeros((LAN - SUB, half), bf16)
-    loads[3].wait()
-    out_ref[...] = mm(spread_s[...], stacked_s[...]).astype(bf16)
-    carried = mm(dscore, rows_s[...]).astype(bf16)
+    loads[4].wait()
+    parts = out_sems.shape[0]
+    size = arrivals // parts
+    stores = []
+    for t in range(parts):
+        here = pl.ds(t * size, size)
+        out_s[here, :] = mm(spread_s[here, :], stacked_s[...]).astype(bf16)
+        stores.append(pltpu.make_async_copy(out_s.at[here], out_hbm.at[here], out_sems.at[t]))
+        stores[t].start()
+    for store in stores:
+        store.wait()
+
+
+def weight_kernel(core_ref, rows_ref, dscore_ref, out_ref, rows_s):
+    width = rows_ref.shape[1]
+    rows_s[:SUB, :] = rows_ref[...]
+    rows_s[SUB:, :] = jnp.zeros((LAN - SUB, width), bf16)
+    carried = mm(dscore_ref[...], rows_s[...]).astype(bf16)
     core = core_ref[0]
     tile = 256
     for t in range(width // tile):
         part = tn(rows_s[:SUB, t * tile : (t + 1) * tile], carried)
         part = part.reshape(tile // 32, 2, 16, width)
         even = jnp.broadcast_to(core, (tile // 32, 16, width)) == 0
-        here = jnp.where(even, part[:, 0], part[:, 1]).reshape(tile // 2, width)
-        there = jnp.where(even, part[:, 1], part[:, 0]).reshape(tile // 2, width)
-        keep_ref[t * tile // 2 : (t + 1) * tile // 2, :] = here
-        send_ref[t * tile // 2 : (t + 1) * tile // 2, :] = there.astype(bf16)
+        part = jnp.where(even, part[:, 0], part[:, 1]).reshape(tile // 2, width)
+        out_ref[t * tile // 2 : (t + 1) * tile // 2, :] = part.astype(out_ref.dtype)
 
 
 def split_kernel(y_ref, keep_ref, got_ref, own_ref, *send_refs):
@@ -249,13 +277,15 @@
     return [pl.BlockSpec(memory_space=pltpu.VMEM)] * n
 
 
-def call(kernel, outs, n_in, scratch=(), flops=0, moved=0, smem=0, hbm=0, grant=60):
+def call(kernel, outs, n_in, scratch=(), flops=0, moved=0, smem=0, hbm=0, hbm_outs=0, grant=60):
     single = not isinstance(outs, (list, tuple))
+    n_out = 1 if single else len(outs)
+    out_specs = [pl.BlockSpec(memory_space=pltpu.HBM)] * hbm_outs + vmem(n_out - hbm_outs)
     return pl.pallas_call(
         kernel,
         out_shape=outs,
         in_specs=[pl.BlockSpec(memory_space=pltpu.SMEM)] * smem + vmem(n_in) + [pl.BlockSpec(memory_space=pltpu.HBM)] * hbm,
-        out_specs=vmem(1)[0] if single else vmem(len(outs)),
+        out_specs=out_specs[0] if single else out_specs,
         scratch_shapes=list(scratch),
         compiler_params=pltpu.CompilerParams(vmem_limit_bytes=int(grant * MIB)),
         cost_estimate=pl.CostEstimate(flops=flops, bytes_accessed=moved, transcendentals=0),
@@ -283,14 +313,17 @@
     ids = members[0]
     padded = pltpu.VMEM((ids.shape[0], 128), i32)
 
-    requests = call(request_kernel, struct((n_rec, 1, 128), i32), 1, [padded])(ids)
+    requests = call(request_kernel, struct((n_rec, 1, 128), i32), 1, [padded], grant=16)(ids)
     asked = lax.all_to_all(requests, REC, split_axis=0, concat_axis=0, tiled=True)
     dma = pltpu.SemaphoreType.DMA
+    stacked = call(
+        stack_kernel, struct((2 * rec_rows, half), bf16), 1, flops=10**6, moved=3 * MIB, grant=16
+    )(embeddings[0])
     found = call(
-        fetch_kernel, struct((arrivals, half), bf16), 1,
-        [pltpu.VMEM((rec_rows, width), f32), dma],
-        flops=4 * arrivals * rec_rows * half, moved=4 * MIB, hbm=1,
-    )(asked, embeddings[0])
+        fetch_kernel, struct((arrivals, half), bf16), 2,
+        [pltpu.VMEM((arrivals, half), bf16), dma((4,))],
+        flops=4 * arrivals * rec_rows * half, moved=3 * MIB, hbm_outs=1, grant=32,
+    )(asked, stacked)
     arrived = lax.all_to_all(
         found.reshape(n_rec, 2 * CAP, half), REC, split_axis=0, concat_axis=0, tiled=True
     ).reshape(arrivals, half)
@@ -304,49 +337,46 @@
         4, [padded], moved=8 * MIB,
     )(ids, pair_slots[0].T, labels, asked)
 
-    core = lax.axis_index("c").astype(i32).reshape(1)
-    rows_core = width // NC
-    out, keep, send = call(
+    out, rows, dscore = call(
         owner_kernel,
-        [struct((arrivals, half), bf16), struct((rows_core, width), f32), struct((rows_core, width), bf16)],
+        [struct((arrivals, half), bf16), struct((SUB, width), bf16), struct((SUB, LAN), bf16)],
         1,
         [pltpu.VMEM((2 * SUB, arrivals), bf16)]
         + [pltpu.VMEM((LAN, width), bf16)] * 2
         + [pltpu.VMEM((2 * LAN, half), bf16), pltpu.VMEM((width, width), bf16), pltpu.VMEM((arrivals, 2 * LAN), bf16)]
-        + [pltpu.VMEM((2 * SUB, 2 * LAN), bf16)]
-        + [dma((4,))],
-        flops=5 * 10**9, moved=12 * MIB, smem=1, hbm=3, grant=49.5,
-    )(core, arrived, gather, weight, table)
-    got = lax.ppermute(send, "c", [(0, 1), (1, 0)])
+        + [pltpu.VMEM((2 * SUB, 2 * LAN), bf16), pltpu.VMEM((arrivals, half), bf16)]
+        + [dma((5,)), dma((4,))],
+        flops=4 * 10**9, moved=12 * MIB, hbm=3, hbm_outs=1, grant=49.5,
+    )(arrived, gather, weight, table)
     returned = lax.all_to_all(
         out.reshape(n_rec, 2 * CAP, half), REC, split_axis=0, concat_axis=0, tiled=True
     ).reshape(arrivals, half)
 
+    core = lax.axis_index("c").astype(i32).reshape(1)
+    rows_core = width // NC
+
+    def term(half_of, dtype):
+        return call(
+            weight_kernel, struct((rows_core, width), dtype), 2, [pltpu.VMEM((LAN, width), bf16)],
+            flops=10**9, moved=4 * MIB, smem=1, grant=24,
+        )(half_of, rows, dscore)
+
+    send, keep = term(1 - core, bf16), term(core, f32)
+    got = lax.ppermute(send, "c", [(0, 1), (1, 0)])
     y = lax.axis_index("y").astype(i32).reshape(1)
     cols = width // NY
     summed, *sends = call(
         split_kernel,
         [struct((rows_core, cols), f32)] + [struct((rows_core, cols), bf16)] * (NY - 1), 2,
-        flops=10**6, moved=4 * MIB, smem=1, grant=16,
+        flops=10**6, moved=4 * MIB, smem=1, grant=24,
     )(y, keep, got)
     for k in range(1, NY):
         summed = summed + lax.ppermute(sends[k - 1], "y", [(i, (i + k) % NY) for i in range(NY)]).astype(f32)
     summed = shifted_blocks(summed.reshape(NX, NZ * 16, cols), "x", NX)
-    half_z = NZ // 2
-    z = lax.axis_index("z")
-    summed = summed.reshape(2, half_z, 16, cols)
-    far = lax.dynamic_index_in_dim(summed, 1 - z // half_z, 0, keepdims=False).astype(bf16)
-    near = lax.dynamic_index_in_dim(summed, z // half_z, 0, keepdims=False)
-    far = lax.ppermute(far, "z", [(i, (i + half_z) % NZ) for i in range(NZ)])
-    summed = near + far.astype(f32)
-    blocks = []
-    for k in range(1, half_z):
-        block = lax.dynamic_index_in_dim(summed, (z + k) % half_z, 0, keepdims=False).astype(bf16)
-        to = [(i, i // half_z * half_z + (i + k) % half_z) for i in range(NZ)]
-        blocks.append(lax.ppermute(block, "z", to))
-    summed = lax.dynamic_index_in_dim(summed, z % half_z, 0, keepdims=False)
-    for block in blocks:
-        summed = summed + block.astype(f32)
+    shares = summed.reshape(NZ, 16, cols).astype(bf16)
+    returned, shares = lax.optimization_barrier((returned, shares))
+    shares = lax.all_to_all(shares, "z", split_axis=0, concat_axis=0, tiled=True)
+    summed = jnp.sum(shares.astype(f32), axis=0)
     pieces = [summed]
     for k in range(1, NY):
         pieces.append(lax.ppermute(summed, "y", [(i, (i + k) % NY) for i in range(NY)]))
@@ -354,9 +384,7 @@
         return_kernel, struct((rec_rows, width), f32), 1, [pltpu.VMEM((2 * rec_rows, arrivals), bf16), dma],
         flops=4 * arrivals * rec_rows * half, moved=6 * MIB, hbm=1, grant=52,
     )(returned, back)
-    emb_grad, pieces = lax.optimization_barrier((emb_grad, pieces))
     weight_part = call(join_kernel, struct((16, width), f32), NY, smem=1, flops=10**4, moved=10**5, grant=16)(y, *pieces)
-
     return (emb_grad[None], weight_part)
 
 

time: 151 us -> 147 us (0.974)
  blocking collectives: 20.7 us -> 12.1 us
  starting transfers between devices: 36.8 us -> 41.8 us
    all_to_all x0 -> x1, starting transfers between devices: none -> 12 us  [on_device(): lax.all_to_all(requests, REC, split_axis=0, concat_axis=0, tiled=True)]
    ppermute x4 -> x0, starting transfers between devices: 9.72 us -> none  [the longest x1 5.74 us: on_device(): far = lax.ppermute(far, 'z', [(i, (i + half_z) % NZ) for i in range(NZ)])]
    all_to_all x1, blocking collectives: 20.7 us -> 12.1 us  [on_device(): lax.all_to_all(shares, 'z', split_axis=0, concat_axis=0, tiled=True)]
    all_to_all x0 -> x1, waiting for transfers between devices: none -> 7.03 us  [on_device(): lax.all_to_all(requests, REC, split_axis=0, concat_axis=0, tiled=True)]
    ppermute x4 -> x0, waiting for transfers between devices: 5.69 us -> none  [the longest x3 3.52 us: on_device(): blocks.append(lax.ppermute(block, 'z', to))]
    all_to_all x1, waiting for transfers between devices: 0.01 us -> 3.77 us  [on_device(): lax.all_to_all(out.reshape(n_rec, 2 * CAP, half), REC, split_axis=0, conc...]
    ppermute x3, waiting for transfers between devices: 13.7 us -> 10.8 us  [on_device(): lax.ppermute(sends[k - 1], 'y', [(i, (i + k) % NY) for i in range(NY)])]
    ppermute x1, waiting for transfers between devices: 2.72 us -> 1.16 us  [on_device(): got = lax.ppermute(send, 'c', [(0, 1), (1, 0)])]
  transfers between devices with their start and end apart: 16 -> 13, of which waited for: 9 -> 8; matrix products, arithmetic and copies ran while one was open for 0% -> 1% of each run, Pallas kernels for 8% -> 11%
where the time goes in v3:
time: 147 us; the launch traced here: 146 us
  waiting for transfers between devices  60.1 us (41%)
  starting transfers between devices  41.8 us (28%)
  Pallas kernels  27.1 us (18%)
  blocking collectives  12.1 us (8%)
  local copies, waits for them, and re-layouts  2.82 us (2%)
    all_to_all x1, waiting for transfers between devices, on_device(): lax.all_to_all(found.reshape(n_rec, 2 * CAP, half), REC, split_axis=0, co...  32.5 us
    all_to_all x1, blocking collectives, on_device(): lax.all_to_all(shares, 'z', split_axis=0, concat_axis=0, tiled=True)  12.1 us
    all_to_all x1, starting transfers between devices, on_device(): lax.all_to_all(requests, REC, split_axis=0, concat_axis=0, tiled=True)  12 us
    ppermute x3, waiting for transfers between devices, on_device(): lax.ppermute(sends[k - 1], 'y', [(i, (i + k) % NY) for i in range(NY)])  10.8 us
    pallas_call x1, Pallas kernels, on_device(): call(owner_kernel, [struct((arrivals, half), bf16), struct((SUB, width),...  7.34 us
    all_to_all x1, starting transfers between devices, on_device(): lax.all_to_all(out.reshape(n_rec, 2 * CAP, half), REC, split_axis=0, conc...  7.34 us
    all_to_all x1, waiting for transfers between devices, on_device(): lax.all_to_all(requests, REC, split_axis=0, concat_axis=0, tiled=True)  7.03 us
    pallas_call x1, Pallas kernels, on_device(): call(prepare_kernel, [struct((2 * SUB, arrivals), bf16), struct((arrivals...  6.15 us
  transfers between devices with their start and end apart: 13, of which 8 were waited for; matrix products, arithmetic and copies ran while one was open for 1% of the time, Pallas kernels for 11%

profile of v3, /device:TPU:2, one launch (start us, length us, event | category | flops | bytes accessed | tf_op | source)
XLA Modules:
  0.0 145.8 jit_solution(3685672302489281081)
XLA Ops:
  2.6 12.0 %all-to-all-start = ((s32[64,1,128]{2,1,0:T(1,128)}), s32[64,1,128]{2,1,0:T(1,128)S(1)}, u32[]{:S(2)}, u32[]{:S(2)}) async-start(s32[64,1,128]{2,1,0:T(1,128)} %shard_map.68), calls=%async_computation | async-start | bytes 65536 | tf_op jit(solution)/shard_map/all_to_all | solution.py:317
  14.6 1.4 copy-done
  16.1 7.0 %all-to-all-done.asked_ref = s32[64,1,128]{2,1,0:T(1,128)S(1)} async-done(((s32[64,1,128]{2,1,0:T(1,128)}), s32[64,1,128]{2,1,0:T(1,128)S(1)}, u32[]{:S(2)}, u32[]{:S(2)}) %all-to-all-start) | async-done | bytes 32800 | tf_op jit(solution)/shard_map/all_to_all | solution.py:317
  23.2 2.2 %shard_map.70 = bf16[1536,512]{1,0:T(8,128)(2,1)} custom-call(s32[64,1,128]{2,1,0:T(1,128)S(1)} %all-to-all-done.asked_ref, bf16[768,512]{1,0:T(8,128)(2,1)S(1)} %shard_map.69.stacked_ref), custom_call_target="tpu_custom_call" | custom-call | flops 1207959552 | bytes 3145728 | tf_op jit(solution)/shard_map/pallas_call | solution.py:322
  25.4 5.6 %all-to-all-start.1 = ((bf16[64,24,512]{2,1,0:T(8,128)(2,1)}), bf16[64,24,512]{2,1,0:T(8,128)(2,1)S(1)}, u32[]{:S(2)}, u32[]{:S(2)}) async-start(bf16[64,24,512]{2,1,0:T(8,128)(2,1)} %bitcast.2), calls=%async_computation.1 | async-start | bytes 3145728 | tf_op jit(solution)/shard_map/all_to_all | solution.py:327
  31.0 6.2 %shard_map.71 = (bf16[544,1536]{1,0:T(8,128)(2,1)}, bf16[2080,768]{1,0:T(8,128)(2,1)}, bf16[768,1536]{1,0:T(8,128)(2,1)}) custom-call(s32[8,99]{1,0:T(8,128)} %bitcast.31, s32[2,128]{1,0:T(2,128)} %bitcast.37, s32[1,128]{1,0:T(1,128)} %labels_ref.1, s32[64,1,128]{2,1,0:T(1,128)} %copy-done.1), custom_call_target="tpu_custom_call" | custom-call | bytes 8388608 | tf_op jit(solution)/shard_map/pallas_call | solution.py:330
  37.1 32.5 %all-to-all-done.1 = bf16[64,24,512]{2,1,0:T(8,128)(2,1)S(1)} async-done(((bf16[64,24,512]{2,1,0:T(8,128)(2,1)}), bf16[64,24,512]{2,1,0:T(8,128)(2,1)S(1)}, u32[]{:S(2)}, u32[]{:S(2)}) %all-to-all-start.1) | async-done | bytes 1572896 | tf_op jit(solution)/shard_map/all_to_all | solution.py:327
  69.6 7.3 %shard_map.72 = (bf16[1536,512]{1,0:T(8,128)(2,1)}, bf16[272,1024]{1,0:T(8,128)(2,1)S(1)}, bf16[272,384]{1,0:T(8,128)(2,1)S(1)}) custom-call(bf16[1536,512]{1,0:T(8,128)(2,1)S(1)} %bitcast.30, bf16[544,1536]{1,0:T(8,128)(2,1)} %get-tuple-element.14.gather_hbm, bf16[1024,1024]{1,0:T(8,128)(2,1)} %weight_hbm.1, bf16[2080,768]{1,0:T(8,128)(2,1)} %get-tuple-element.15.table_hbm), custom_call_target="tpu_custom_call" | custom-call | flops 4000000000 | bytes 12582912 | tf_op jit(solution)/shard_map/pallas_call | solution.py:340
  77.0 7.3 %all-to-all-start.2 = ((bf16[64,24,512]{2,1,0:T(8,128)(2,1)}), bf16[64,24,512]{2,1,0:T(8,128)(2,1)S(1)}, u32[]{:S(2)}, u32[]{:S(2)}) async-start(bf16[64,24,512]{2,1,0:T(8,128)(2,1)} %bitcast.6), calls=%async_computation.2 | async-start | bytes 3145728 | tf_op jit(solution)/shard_map/all_to_all | solution.py:351
  84.3 2.5 %shard_map.74 = bf16[512,1024]{1,0:T(8,128)(2,1)} custom-call(s32[1]{0:T(128)S(6)} %sub.3.core_ref, bf16[272,1024]{1,0:T(8,128)(2,1)S(1)} %get-tuple-element.17.rows_ref, bf16[272,384]{1,0:T(8,128)(2,1)S(1)} %get-tuple-element.18.dscore_ref), custom_call_target="tpu_custom_call" | custom-call | flops 1000000000 | bytes 4194304 | tf_op jit(solution)/shard_map/pallas_call | solution.py:359
  87.0 1.6 %shard_map.73.keep_ref = f32[512,1024]{1,0:T(8,128)S(1)} custom-call(s32[1]{0:T(128)} %bitcast.9.core_ref, bf16[272,1024]{1,0:T(8,128)(2,1)S(1)} %get-tuple-element.17.rows_ref, bf16[272,384]{1,0:T(8,128)(2,1)S(1)} %get-tuple-element.18.dscore_ref), custom_call_target="tpu_custom_call" | custom-call | flops 1000000000 | bytes 4194304 | tf_op jit(solution)/shard_map/pallas_call | solution.py:359
  90.8 1.6 %collective-permute-start.1 = (bf16[512,256]{1,0:T(8,128)(2,1)}, bf16[512,256]{1,0:T(8,128)(2,1)S(1)}, u32[]{:S(2)}, u32[]{:S(2)}) collective-permute-start(bf16[512,256]{1,0:T(8,128)(2,1)} %get-tuple-element.20), channel_id=1, source_target_pairs={{0,1},{1,2},{2,3},{3,0},{4,5},{5,6},{6,7},{7,4},{8,9},{9,10},{10,1... | collective-permute-start | bytes 786440 | tf_op jit(solution)/shard_map/ppermute | solution.py:374
  92.4 2.9 %collective-permute-start.2 = (bf16[512,256]{1,0:T(8,128)(2,1)}, bf16[512,256]{1,0:T(8,128)(2,1)S(1)}, u32[]{:S(2)}, u32[]{:S(2)}) collective-permute-start(bf16[512,256]{1,0:T(8,128)(2,1)} %get-tuple-element.21), channel_id=1, source_target_pairs={{0,2},{1,3},{2,0},{3,1},{4,6},{5,7},{6,4},{7,5},{8,10},{9,11},{10,... | collective-permute-start | bytes 786440 | tf_op jit(solution)/shard_map/ppermute | solution.py:374
  96.6 4.0 %collective-permute-done.1 = bf16[512,256]{1,0:T(8,128)(2,1)S(1)} collective-permute-done((bf16[512,256]{1,0:T(8,128)(2,1)}, bf16[512,256]{1,0:T(8,128)(2,1)S(1)}, u32[]{:S(2)}, u32[]{:S(2)}) %collective-permute-start.1) | collective-permute-done | bytes 262176 | tf_op jit(solution)/shard_map/ppermute | solution.py:374
  100.6 6.8 %collective-permute-done.2 = bf16[512,256]{1,0:T(8,128)(2,1)S(1)} collective-permute-done((bf16[512,256]{1,0:T(8,128)(2,1)}, bf16[512,256]{1,0:T(8,128)(2,1)S(1)}, u32[]{:S(2)}, u32[]{:S(2)}) %collective-permute-start.2) | collective-permute-done | bytes 262176 | tf_op jit(solution)/shard_map/ppermute | solution.py:374
  109.2 1.6 %collective-permute-start.4 = (bf16[128,256]{1,0:T(8,128)(2,1)S(1)}, bf16[128,256]{1,0:T(8,128)(2,1)S(1)}, u32[]{:S(2)}, u32[]{:S(2)}) collective-permute-start(bf16[128,256]{1,0:T(8,128)(2,1)S(1)} %get-tuple-element.26), channel_id=1, source_target_pairs={{0,64},{64,128},{128,192},{192,0},{1,65},{65,129},{129,193},{193,1... | collective-permute-start | bytes 196616 | tf_op jit(solution)/shard_map/ppermute | solution.py:300
  111.8 2.4 %collective-permute-start.6 = (bf16[128,256]{1,0:T(8,128)(2,1)S(1)}, bf16[128,256]{1,0:T(8,128)(2,1)S(1)}, u32[]{:S(2)}, u32[]{:S(2)}) collective-permute-start(bf16[128,256]{1,0:T(8,128)(2,1)S(1)} %get-tuple-element.27), channel_id=1, source_target_pairs={{0,192},{64,0},{128,64},{192,128},{1,193},{65,1},{129,65},{193,129... | collective-permute-start | bytes 196616 | tf_op jit(solution)/shard_map/ppermute | solution.py:300
  114.2 4.6 %collective-permute-done.5 = bf16[128,256]{1,0:T(8,128)(2,1)S(1)} collective-permute-done((bf16[128,256]{1,0:T(8,128)(2,1)S(1)}, bf16[128,256]{1,0:T(8,128)(2,1)S(1)}, u32[]{:S(2)}, u32[]{:S(2)}) %collective-permute-start.5) | collective-permute-done | bytes 65568 | tf_op jit(solution)/shard_map/ppermute | solution.py:300
  119.1 3.8 %all-to-all-done.2 = bf16[64,24,512]{2,1,0:T(8,128)(2,1)S(1)} async-done(((bf16[64,24,512]{2,1,0:T(8,128)(2,1)}), bf16[64,24,512]{2,1,0:T(8,128)(2,1)S(1)}, u32[]{:S(2)}, u32[]{:S(2)}) %all-to-all-start.2) | async-done | bytes 1572896 | tf_op jit(solution)/shard_map/all_to_all | solution.py:351
  122.9 12.1 %all_to_all.20 = bf16[8,16,256]{2,1,0:T(8,128)(2,1)S(1)} all-to-all(bf16[8,16,256]{2,1,0:T(8,128)(2,1)S(1)} %bitcast.36), channel_id=1, replica_groups=mesh['x'=4,'z'=8,'c'=2,'y'=4] {'z'}, dimensions={0} | all-to-all | bytes 131072 | tf_op jit(solution)/shard_map/all_to_all | solution.py:378
  135.0 1.7 %collective-permute-start.7 = (f32[16,256]{1,0:T(8,128)S(1)}, f32[16,256]{1,0:T(8,128)S(1)}, u32[]{:S(2)}, u32[]{:S(2)}) collective-permute-start(f32[16,256]{1,0:T(8,128)S(1)} %convert_reduce_fusion.refs_0_), channel_id=1, source_target_pairs={{0,1},{1,2},{2,3},{3,0},{4,5},{5,6},{6,7},{7,4},{8,9},{9,10},{10,1... | collective-permute-start | bytes 49160 | tf_op jit(solution)/shard_map/ppermute | solution.py:382
  136.7 2.9 %collective-permute-start.8 = (f32[16,256]{1,0:T(8,128)S(1)}, f32[16,256]{1,0:T(8,128)S(1)}, u32[]{:S(2)}, u32[]{:S(2)}) collective-permute-start(f32[16,256]{1,0:T(8,128)S(1)} %convert_reduce_fusion.refs_0_), channel_id=1, source_target_pairs={{0,2},{1,3},{2,0},{3,1},{4,6},{5,7},{6,4},{7,5},{8,10},{9,11},{10,... | collective-permute-start | bytes 49160 | tf_op jit(solution)/shard_map/ppermute | solution.py:382
  139.6 1.3 collective-permute-start.9
  140.9 4.2 %shard_map.76 = f32[384,1024]{1,0:T(8,128)} custom-call(bf16[1536,512]{1,0:T(8,128)(2,1)S(1)} %bitcast.28, bf16[768,1536]{1,0:T(8,128)(2,1)} %get-tuple-element.24.pick_hbm), custom_call_target="tpu_custom_call" | custom-call | flops 1207959552 | bytes 6291456 | tf_op jit(solution)/shard_map/pallas_call | solution.py:383
  (25 shorter events, 9.4 us)
Async XLA Ops:
  0.6 0.7 copy-start.2
  2.6 20.6 %all-to-all-start = ((s32[64,1,128]{2,1,0:T(1,128)}), s32[64,1,128]{2,1,0:T(1,128)S(1)}, u32[]{:S(2)}, u32[]{:S(2)}) async-start(s32[64,1,128]{2,1,0:T(1,128)} %shard_map.68), calls=%async_computation | async-start | bytes 65536 | tf_op jit(solution)/shard_map/all_to_all | solution.py:317
  14.6 1.4 copy-start
  23.2 2.2 %copy-start.1 = (s32[64,1,128]{2,1,0:T(1,128)}, s32[64,1,128]{2,1,0:T(1,128)S(1)}, u32[]{:S(2)}) copy-start(s32[64,1,128]{2,1,0:T(1,128)S(1)} %all-to-all-done.asked_ref) | copy-start | bytes 98308
  25.4 44.2 %all-to-all-start.1 = ((bf16[64,24,512]{2,1,0:T(8,128)(2,1)}), bf16[64,24,512]{2,1,0:T(8,128)(2,1)S(1)}, u32[]{:S(2)}, u32[]{:S(2)}) async-start(bf16[64,24,512]{2,1,0:T(8,128)(2,1)} %bitcast.2), calls=%async_computation.1 | async-start | bytes 3145728 | tf_op jit(solution)/shard_map/all_to_all | solution.py:327
  77.0 45.9 %all-to-all-start.2 = ((bf16[64,24,512]{2,1,0:T(8,128)(2,1)}), bf16[64,24,512]{2,1,0:T(8,128)(2,1)S(1)}, u32[]{:S(2)}, u32[]{:S(2)}) async-start(bf16[64,24,512]{2,1,0:T(8,128)(2,1)} %bitcast.6), calls=%async_computation.2 | async-start | bytes 3145728 | tf_op jit(solution)/shard_map/all_to_all | solution.py:351
  86.9 2.9 %collective-permute-start = (bf16[512,1024]{1,0:T(8,128)(2,1)}, bf16[512,1024]{1,0:T(8,128)(2,1)S(1)}, u32[]{:S(2)}, u32[]{:S(2)}) collective-permute-start(bf16[512,1024]{1,0:T(8,128)(2,1)} %shard_map.74), channel_id=1, source_target_pairs={{0,4},{4,0},{1,5},{5,1},{2,6},{6,2},{3,7},{7,3},{8,12},{12,8},{9,1... | collective-permute-start | bytes 3145736 | tf_op jit(solution)/shard_map/ppermute | solution.py:365
  90.8 9.9 %collective-permute-start.1 = (bf16[512,256]{1,0:T(8,128)(2,1)}, bf16[512,256]{1,0:T(8,128)(2,1)S(1)}, u32[]{:S(2)}, u32[]{:S(2)}) collective-permute-start(bf16[512,256]{1,0:T(8,128)(2,1)} %get-tuple-element.20), channel_id=1, source_target_pairs={{0,1},{1,2},{2,3},{3,0},{4,5},{5,6},{6,7},{7,4},{8,9},{9,10},{10,1... | collective-permute-start | bytes 786440 | tf_op jit(solution)/shard_map/ppermute | solution.py:374
  92.4 15.1 %collective-permute-start.2 = (bf16[512,256]{1,0:T(8,128)(2,1)}, bf16[512,256]{1,0:T(8,128)(2,1)S(1)}, u32[]{:S(2)}, u32[]{:S(2)}) collective-permute-start(bf16[512,256]{1,0:T(8,128)(2,1)} %get-tuple-element.21), channel_id=1, source_target_pairs={{0,2},{1,3},{2,0},{3,1},{4,6},{5,7},{6,4},{7,5},{8,10},{9,11},{10,... | collective-permute-start | bytes 786440 | tf_op jit(solution)/shard_map/ppermute | solution.py:374
  95.3 12.2 %collective-permute-start.3 = (bf16[512,256]{1,0:T(8,128)(2,1)S(1)}, bf16[512,256]{1,0:T(8,128)(2,1)S(1)}, u32[]{:S(2)}, u32[]{:S(2)}) collective-permute-start(bf16[512,256]{1,0:T(8,128)(2,1)S(1)} %get-tuple-element.22), channel_id=1, source_target_pairs={{0,3},{1,0},{2,1},{3,2},{4,7},{5,4},{6,5},{7,6},{8,11},{9,8},{10,9... | collective-permute-start | bytes 786440 | tf_op jit(solution)/shard_map/ppermute | solution.py:374
  107.4 0.7 copy-start.3
  109.2 5.0 %collective-permute-start.4 = (bf16[128,256]{1,0:T(8,128)(2,1)S(1)}, bf16[128,256]{1,0:T(8,128)(2,1)S(1)}, u32[]{:S(2)}, u32[]{:S(2)}) collective-permute-start(bf16[128,256]{1,0:T(8,128)(2,1)S(1)} %get-tuple-element.26), channel_id=1, source_target_pairs={{0,64},{64,128},{128,192},{192,0},{1,65},{65,129},{129,193},{193,1... | collective-permute-start | bytes 196616 | tf_op jit(solution)/shard_map/ppermute | solution.py:300
  110.9 8.0 %collective-permute-start.5 = (bf16[128,256]{1,0:T(8,128)(2,1)S(1)}, bf16[128,256]{1,0:T(8,128)(2,1)S(1)}, u32[]{:S(2)}, u32[]{:S(2)}) collective-permute-start(bf16[128,256]{1,0:T(8,128)(2,1)S(1)} %get-tuple-element.28), channel_id=1, source_target_pairs={{0,128},{64,192},{128,0},{192,64},{1,129},{65,193},{129,1},{193,65... | collective-permute-start | bytes 196616 | tf_op jit(solution)/shard_map/ppermute | solution.py:300
  111.8 7.3 %collective-permute-start.6 = (bf16[128,256]{1,0:T(8,128)(2,1)S(1)}, bf16[128,256]{1,0:T(8,128)(2,1)S(1)}, u32[]{:S(2)}, u32[]{:S(2)}) collective-permute-start(bf16[128,256]{1,0:T(8,128)(2,1)S(1)} %get-tuple-element.27), channel_id=1, source_target_pairs={{0,192},{64,0},{128,64},{192,128},{1,193},{65,1},{129,65},{193,129... | collective-permute-start | bytes 196616 | tf_op jit(solution)/shard_map/ppermute | solution.py:300
  135.0 10.1 %collective-permute-start.7 = (f32[16,256]{1,0:T(8,128)S(1)}, f32[16,256]{1,0:T(8,128)S(1)}, u32[]{:S(2)}, u32[]{:S(2)}) collective-permute-start(f32[16,256]{1,0:T(8,128)S(1)} %convert_reduce_fusion.refs_0_), channel_id=1, source_target_pairs={{0,1},{1,2},{2,3},{3,0},{4,5},{5,6},{6,7},{7,4},{8,9},{9,10},{10,1... | collective-permute-start | bytes 49160 | tf_op jit(solution)/shard_map/ppermute | solution.py:382
  136.7 8.5 %collective-permute-start.8 = (f32[16,256]{1,0:T(8,128)S(1)}, f32[16,256]{1,0:T(8,128)S(1)}, u32[]{:S(2)}, u32[]{:S(2)}) collective-permute-start(f32[16,256]{1,0:T(8,128)S(1)} %convert_reduce_fusion.refs_0_), channel_id=1, source_target_pairs={{0,2},{1,3},{2,0},{3,1},{4,6},{5,7},{6,4},{7,5},{8,10},{9,11},{10,... | collective-permute-start | bytes 49160 | tf_op jit(solution)/shard_map/ppermute | solution.py:382
  139.6 5.6 %collective-permute-start.9 = (f32[16,256]{1,0:T(8,128)S(1)}, f32[16,256]{1,0:T(8,128)S(1)}, u32[]{:S(2)}, u32[]{:S(2)}) collective-permute-start(f32[16,256]{1,0:T(8,128)S(1)} %convert_reduce_fusion.refs_0_), channel_id=1, source_target_pairs={{0,3},{1,0},{2,1},{3,2},{4,7},{5,4},{6,5},{7,6},{8,11},{9,8},{10,9... | collective-permute-start | bytes 49160 | tf_op jit(solution)/shard_map/ppermute | solution.py:382

commit v4 on v3

--- a/solution.py
+++ b/solution.py
@@ -262,15 +262,27 @@
         out_ref[:, pl.ds(at, size)] = piece_ref[...]
 
 
-def return_kernel(back_ref, pick_hbm, out_ref, pick_s, sem):
+def return_kernel(back_ref, pick_hbm, out_hbm, pick_s, out_s, in_sems, out_sems):
     half = back_ref.shape[1]
-    load = pltpu.make_async_copy(pick_hbm, pick_s, sem)
-    load.start()
-    load.wait()
-    total = mm(pick_s[...], back_ref[...])
-    rec_rows = out_ref.shape[0]
-    out_ref[:, :half] = total[:rec_rows]
-    out_ref[:, half:] = total[rec_rows:]
+    rows = out_s.shape[0]
+    loads = [
+        pltpu.make_async_copy(pick_hbm.at[pl.ds(h * rows, rows)], pick_s.at[pl.ds(h * rows, rows)], in_sems.at[h])
+        for h in range(2)
+    ]
+    stores = [
+        pltpu.make_async_copy(
+            out_s.at[:, pl.ds(h * half, half)], out_hbm.at[:, pl.ds(h * half, half)], out_sems.at[h]
+        )
+        for h in range(2)
+    ]
+    for load in loads:
+        load.start()
+    for h in range(2):
+        loads[h].wait()
+        out_s[:, h * half : (h + 1) * half] = mm(pick_s[h * rows : (h + 1) * rows, :], back_ref[...])
+        stores[h].start()
+    for store in stores:
+        store.wait()
 
 
 def vmem(n):
@@ -295,7 +307,7 @@
 def shifted_blocks(value, axis, size):
     here = lax.axis_index(axis)
     got = []
-    for k in range(1, size):
+    for k in (2, 1, 3):
         block = lax.dynamic_index_in_dim(value, (here + k) % size, 0, keepdims=False).astype(bf16)
         got.append(lax.ppermute(block, axis, [(i, (i + k) % size) for i in range(size)]))
     total = lax.dynamic_index_in_dim(value, here, 0, keepdims=False)
@@ -370,20 +382,33 @@
         [struct((rows_core, cols), f32)] + [struct((rows_core, cols), bf16)] * (NY - 1), 2,
         flops=10**6, moved=4 * MIB, smem=1, grant=24,
     )(y, keep, got)
-    for k in range(1, NY):
+    for k in (2, 1, 3):
         summed = summed + lax.ppermute(sends[k - 1], "y", [(i, (i + k) % NY) for i in range(NY)]).astype(f32)
     summed = shifted_blocks(summed.reshape(NX, NZ * 16, cols), "x", NX)
-    shares = summed.reshape(NZ, 16, cols).astype(bf16)
-    returned, shares = lax.optimization_barrier((returned, shares))
-    shares = lax.all_to_all(shares, "z", split_axis=0, concat_axis=0, tiled=True)
-    summed = jnp.sum(shares.astype(f32), axis=0)
+    half_z = NZ // 2
+    z = lax.axis_index("z")
+    summed = summed.reshape(2, half_z, 16, cols)
+    far = lax.dynamic_index_in_dim(summed, 1 - z // half_z, 0, keepdims=False).astype(bf16)
+    near = lax.dynamic_index_in_dim(summed, z // half_z, 0, keepdims=False)
+    far = lax.ppermute(far, "z", [(i, (i + half_z) % NZ) for i in range(NZ)])
+    emb_grad = call(
+        return_kernel, struct((rec_rows, width), f32), 1,
+        [pltpu.VMEM((2 * rec_rows, arrivals), bf16), pltpu.VMEM((rec_rows, width), f32), dma((2,)), dma((2,))],
+        flops=4 * arrivals * rec_rows * half, moved=6 * MIB, hbm=1, hbm_outs=1, grant=52,
+    )(returned, back)
+    emb_grad, far = lax.optimization_barrier((emb_grad, far))
+    summed = near + far.astype(f32)
+    blocks = []
+    for k in range(1, half_z):
+        block = lax.dynamic_index_in_dim(summed, (z + k) % half_z, 0, keepdims=False).astype(bf16)
+        to = [(i, i // half_z * half_z + (i + k) % half_z) for i in range(NZ)]
+        blocks.append(lax.ppermute(block, "z", to))
+    summed = lax.dynamic_index_in_dim(summed, z % half_z, 0, keepdims=False)
+    for block in blocks:
+        summed = summed + block.astype(f32)
     pieces = [summed]
     for k in range(1, NY):
         pieces.append(lax.ppermute(summed, "y", [(i, (i + k) % NY) for i in range(NY)]))
-    emb_grad = call(
-        return_kernel, struct((rec_rows, width), f32), 1, [pltpu.VMEM((2 * rec_rows, arrivals), bf16), dma],
-        flops=4 * arrivals * rec_rows * half, moved=6 * MIB, hbm=1, grant=52,
-    )(returned, back)
     weight_part = call(join_kernel, struct((16, width), f32), NY, smem=1, flops=10**4, moved=10**5, grant=16)(y, *pieces)
     return (emb_grad[None], weight_part)
 

time: 147 us -> 144 us (0.980)
  blocking collectives: 12.1 us -> 0 us
  starting transfers between devices: 41.8 us -> 50.9 us
  waiting for transfers between devices: 60.1 us -> 62 us
    all_to_all x1 -> x0, blocking collectives: 12.1 us -> none  [on_device(): lax.all_to_all(shares, 'z', split_axis=0, concat_axis=0, tiled=True)]
    ppermute x0 -> x4, starting transfers between devices: none -> 9.28 us  [the longest x1 5.78 us: on_device(): far = lax.ppermute(far, 'z', [(i, (i + half_z) % NZ) for i in range(NZ)])]
    all_to_all x1, waiting for transfers between devices: 3.77 us -> 0.01 us  [on_device(): lax.all_to_all(out.reshape(n_rec, 2 * CAP, half), REC, split_axis=0, conc...]
    ppermute x0 -> x4, waiting for transfers between devices: none -> 3.15 us  [the longest x3 3.15 us: on_device(): blocks.append(lax.ppermute(block, 'z', to))]
    ppermute x3, waiting for transfers between devices: 0.01 us -> 2.63 us  [on_device(): lax.ppermute(summed, 'y', [(i, (i + k) % NY) for i in range(NY)])]
  transfers between devices with their start and end apart: 13 -> 17, of which waited for: 8 -> 14; matrix products, arithmetic and copies ran while one was open for 1% -> 1% of each run, Pallas kernels for 11% -> 11%
where the time goes in v4:
time: 144 us
  waiting for transfers between devices  62 us (43%)
  starting transfers between devices  50.9 us (35%)
  Pallas kernels  26.7 us (19%)
  local copies, waits for them, and re-layouts  2.15 us (1%)
    all_to_all x1, waiting for transfers between devices, on_device(): lax.all_to_all(found.reshape(n_rec, 2 * CAP, half), REC, split_axis=0, co...  32.4 us
    all_to_all x1, starting transfers between devices, on_device(): lax.all_to_all(requests, REC, split_axis=0, concat_axis=0, tiled=True)  12 us
    ppermute x3, waiting for transfers between devices, on_device(): lax.ppermute(sends[k - 1], 'y', [(i, (i + k) % NY) for i in range(NY)])  9.73 us
    pallas_call x1, Pallas kernels, on_device(): call(owner_kernel, [struct((arrivals, half), bf16), struct((SUB, width),...  7.34 us
    all_to_all x1, starting transfers between devices, on_device(): lax.all_to_all(out.reshape(n_rec, 2 * CAP, half), REC, split_axis=0, conc...  7.34 us
    all_to_all x1, waiting for transfers between devices, on_device(): lax.all_to_all(requests, REC, split_axis=0, concat_axis=0, tiled=True)  7.03 us
    ppermute x3, starting transfers between devices, on_device(): lax.ppermute(sends[k - 1], 'y', [(i, (i + k) % NY) for i in range(NY)])  6.43 us
    pallas_call x1, Pallas kernels, on_device(): call(prepare_kernel, [struct((2 * SUB, arrivals), bf16), struct((arrivals...  6.18 us
  transfers between devices with their start and end apart: 17, of which 14 were waited for; matrix products, arithmetic and copies ran while one was open for 1% of the time, Pallas kernels for 11%

profile of v4, /device:TPU:2, one launch (start us, length us, event | category | flops | bytes accessed | tf_op | source)
XLA Modules:
  0.0 143.6 jit_solution(15397863223239863522)
XLA Ops:
  2.6 12.0 %all-to-all-start = ((s32[64,1,128]{2,1,0:T(1,128)}), s32[64,1,128]{2,1,0:T(1,128)S(1)}, u32[]{:S(2)}, u32[]{:S(2)}) async-start(s32[64,1,128]{2,1,0:T(1,128)} %shard_map.68), calls=%async_computation | async-start | bytes 65536 | tf_op jit(solution)/shard_map/all_to_all | solution.py:329
  14.6 1.4 copy-done
  16.1 7.0 %all-to-all-done.asked_ref = s32[64,1,128]{2,1,0:T(1,128)S(1)} async-done(((s32[64,1,128]{2,1,0:T(1,128)}), s32[64,1,128]{2,1,0:T(1,128)S(1)}, u32[]{:S(2)}, u32[]{:S(2)}) %all-to-all-start) | async-done | bytes 32800 | tf_op jit(solution)/shard_map/all_to_all | solution.py:329
  23.2 2.2 %shard_map.70 = bf16[1536,512]{1,0:T(8,128)(2,1)} custom-call(s32[64,1,128]{2,1,0:T(1,128)S(1)} %all-to-all-done.asked_ref, bf16[768,512]{1,0:T(8,128)(2,1)S(1)} %shard_map.69.stacked_ref), custom_call_target="tpu_custom_call" | custom-call | flops 1207959552 | bytes 3145728 | tf_op jit(solution)/shard_map/pallas_call | solution.py:334
  25.4 5.6 %all-to-all-start.1 = ((bf16[64,24,512]{2,1,0:T(8,128)(2,1)}), bf16[64,24,512]{2,1,0:T(8,128)(2,1)S(1)}, u32[]{:S(2)}, u32[]{:S(2)}) async-start(bf16[64,24,512]{2,1,0:T(8,128)(2,1)} %bitcast.2), calls=%async_computation.1 | async-start | bytes 3145728 | tf_op jit(solution)/shard_map/all_to_all | solution.py:339
  31.0 6.2 %shard_map.71 = (bf16[544,1536]{1,0:T(8,128)(2,1)}, bf16[2080,768]{1,0:T(8,128)(2,1)}, bf16[768,1536]{1,0:T(8,128)(2,1)}) custom-call(s32[8,99]{1,0:T(8,128)} %bitcast.45, s32[2,128]{1,0:T(2,128)} %bitcast.52, s32[1,128]{1,0:T(1,128)} %labels_ref.1, s32[64,1,128]{2,1,0:T(1,128)} %copy-done.1), custom_call_target="tpu_custom_call" | custom-call | bytes 8388608 | tf_op jit(solution)/shard_map/pallas_call | solution.py:342
  37.2 32.4 %all-to-all-done.1 = bf16[64,24,512]{2,1,0:T(8,128)(2,1)S(1)} async-done(((bf16[64,24,512]{2,1,0:T(8,128)(2,1)}), bf16[64,24,512]{2,1,0:T(8,128)(2,1)S(1)}, u32[]{:S(2)}, u32[]{:S(2)}) %all-to-all-start.1) | async-done | bytes 1572896 | tf_op jit(solution)/shard_map/all_to_all | solution.py:339
  69.6 7.3 %shard_map.72 = (bf16[1536,512]{1,0:T(8,128)(2,1)}, bf16[272,1024]{1,0:T(8,128)(2,1)S(1)}, bf16[272,384]{1,0:T(8,128)(2,1)S(1)}) custom-call(bf16[1536,512]{1,0:T(8,128)(2,1)S(1)} %bitcast.44, bf16[544,1536]{1,0:T(8,128)(2,1)} %get-tuple-element.14.gather_hbm, bf16[1024,1024]{1,0:T(8,128)(2,1)} %weight_hbm.1, bf16[2080,768]{1,0:T(8,128)(2,1)} %get-tuple-element.15.table_hbm), custom_call_target="tpu_custom_call" | custom-call | flops 4000000000 | bytes 12582912 | tf_op jit(solution)/shard_map/pallas_call | solution.py:352
  77.0 7.3 %all-to-all-start.2 = ((bf16[64,24,512]{2,1,0:T(8,128)(2,1)}), bf16[64,24,512]{2,1,0:T(8,128)(2,1)S(1)}, u32[]{:S(2)}, u32[]{:S(2)}) async-start(bf16[64,24,512]{2,1,0:T(8,128)(2,1)} %bitcast.6), calls=%async_computation.2 | async-start | bytes 3145728 | tf_op jit(solution)/shard_map/all_to_all | solution.py:363
  84.3 2.6 %shard_map.75 = bf16[512,1024]{1,0:T(8,128)(2,1)} custom-call(s32[1]{0:T(128)S(6)} %sub.11.core_ref, bf16[272,1024]{1,0:T(8,128)(2,1)S(1)} %get-tuple-element.18.rows_ref, bf16[272,384]{1,0:T(8,128)(2,1)S(1)} %get-tuple-element.19.dscore_ref), custom_call_target="tpu_custom_call" | custom-call | flops 1000000000 | bytes 4194304 | tf_op jit(solution)/shard_map/pallas_call | solution.py:371
  87.0 1.6 %shard_map.74.keep_ref = f32[512,1024]{1,0:T(8,128)S(1)} custom-call(s32[1]{0:T(128)} %bitcast.9.core_ref, bf16[272,1024]{1,0:T(8,128)(2,1)S(1)} %get-tuple-element.18.rows_ref, bf16[272,384]{1,0:T(8,128)(2,1)S(1)} %get-tuple-element.19.dscore_ref), custom_call_target="tpu_custom_call" | custom-call | flops 1000000000 | bytes 4194304 | tf_op jit(solution)/shard_map/pallas_call | solution.py:371
  90.8 3.2 %collective-permute-start.1 = (bf16[512,256]{1,0:T(8,128)(2,1)}, bf16[512,256]{1,0:T(8,128)(2,1)S(1)}, u32[]{:S(2)}, u32[]{:S(2)}) collective-permute-start(bf16[512,256]{1,0:T(8,128)(2,1)} %get-tuple-element.21), channel_id=1, source_target_pairs={{0,2},{1,3},{2,0},{3,1},{4,6},{5,7},{6,4},{7,5},{8,10},{9,11},{10,... | collective-permute-start | bytes 786440 | tf_op jit(solution)/shard_map/ppermute | solution.py:386
  94.7 2.6 %collective-permute-start.3 = (bf16[512,256]{1,0:T(8,128)(2,1)S(1)}, bf16[512,256]{1,0:T(8,128)(2,1)}, u32[]{:S(2)}, u32[]{:S(2)}) collective-permute-start(bf16[512,256]{1,0:T(8,128)(2,1)S(1)} %get-tuple-element.23), channel_id=1, source_target_pairs={{0,3},{1,0},{2,1},{3,2},{4,7},{5,4},{6,5},{7,6},{8,11},{9,8},{10,9... | collective-permute-start | bytes 786440 | tf_op jit(solution)/shard_map/ppermute | solution.py:386
  97.2 4.5 %collective-permute-done.1 = bf16[512,256]{1,0:T(8,128)(2,1)S(1)} collective-permute-done((bf16[512,256]{1,0:T(8,128)(2,1)}, bf16[512,256]{1,0:T(8,128)(2,1)S(1)}, u32[]{:S(2)}, u32[]{:S(2)}) %collective-permute-start.1) | collective-permute-done | bytes 262176 | tf_op jit(solution)/shard_map/ppermute | solution.py:386
  101.7 4.8 %collective-permute-done.2 = bf16[512,256]{1,0:T(8,128)(2,1)S(1)} collective-permute-done((bf16[512,256]{1,0:T(8,128)(2,1)}, bf16[512,256]{1,0:T(8,128)(2,1)S(1)}, u32[]{:S(2)}, u32[]{:S(2)}) %collective-permute-start.2) | collective-permute-done | bytes 262176 | tf_op jit(solution)/shard_map/ppermute | solution.py:386
  108.1 2.4 %collective-permute-start.4 = (bf16[128,256]{1,0:T(8,128)(2,1)S(1)}, bf16[128,256]{1,0:T(8,128)(2,1)S(1)}, u32[]{:S(2)}, u32[]{:S(2)}) collective-permute-start(bf16[128,256]{1,0:T(8,128)(2,1)S(1)} %get-tuple-element.26), channel_id=1, source_target_pairs={{0,128},{64,192},{128,0},{192,64},{1,129},{65,193},{129,1},{193,65... | collective-permute-start | bytes 196616 | tf_op jit(solution)/shard_map/ppermute | solution.py:312
  110.4 2.0 %collective-permute-start.6 = (bf16[128,256]{1,0:T(8,128)(2,1)S(1)}, bf16[128,256]{1,0:T(8,128)(2,1)S(1)}, u32[]{:S(2)}, u32[]{:S(2)}) collective-permute-start(bf16[128,256]{1,0:T(8,128)(2,1)S(1)} %get-tuple-element.27), channel_id=1, source_target_pairs={{0,192},{64,0},{128,64},{192,128},{1,193},{65,1},{129,65},{193,129... | collective-permute-start | bytes 196616 | tf_op jit(solution)/shard_map/ppermute | solution.py:312
  112.5 3.4 %collective-permute-done.4 = bf16[128,256]{1,0:T(8,128)(2,1)S(1)} collective-permute-done((bf16[128,256]{1,0:T(8,128)(2,1)S(1)}, bf16[128,256]{1,0:T(8,128)(2,1)S(1)}, u32[]{:S(2)}, u32[]{:S(2)}) %collective-permute-start.4) | collective-permute-done | bytes 65568 | tf_op jit(solution)/shard_map/ppermute | solution.py:312
  118.4 5.8 %collective-permute-start.7 = (bf16[4,16,256]{2,1,0:T(8,128)(2,1)S(1)}, bf16[4,16,256]{2,1,0:T(8,128)(2,1)S(1)}, u32[]{:S(2)}, u32[]{:S(2)}) collective-permute-start(bf16[4,16,256]{2,1,0:T(8,128)(2,1)S(1)} %fusion.5), channel_id=1, source_target_pairs={{0,32},{8,40},{16,48},{24,56},{32,0},{40,8},{48,16},{56,24},{1,33}... | collective-permute-start | bytes 98312 | tf_op jit(solution)/shard_map/ppermute | solution.py:393
  124.2 3.7 %shard_map.73 = f32[384,1024]{1,0:T(8,128)} custom-call(bf16[1536,512]{1,0:T(8,128)(2,1)S(1)} %bitcast.42, bf16[768,1536]{1,0:T(8,128)(2,1)} %get-tuple-element.17.pick_hbm), custom_call_target="tpu_custom_call" | custom-call | flops 1207959552 | bytes 6291456 | tf_op jit(solution)/shard_map/pallas_call | solution.py:394
  130.1 1.4 collective-permute-start.9
  131.7 2.7 %collective-permute-done.8 = bf16[16,256]{1,0:T(8,128)(2,1)S(1)} collective-permute-done((bf16[16,256]{1,0:T(8,128)(2,1)S(1)}, bf16[16,256]{1,0:T(8,128)(2,1)S(1)}, u32[]{:S(2)}, u32[]{:S(2)}) %collective-permute-start.8) | collective-permute-done | bytes 8224 | tf_op jit(solution)/shard_map/ppermute | solution.py:405
  134.6 1.7 %collective-permute-start.11 = (f32[16,256]{1,0:T(8,128)S(1)}, f32[16,256]{1,0:T(8,128)S(1)}, u32[]{:S(2)}, u32[]{:S(2)}) collective-permute-start(f32[16,256]{1,0:T(8,128)S(1)} %fusion.7.refs_0_), channel_id=1, source_target_pairs={{0,1},{1,2},{2,3},{3,0},{4,5},{5,6},{6,7},{7,4},{8,9},{9,10},{10,1... | collective-permute-start | bytes 49160 | tf_op jit(solution)/shard_map/ppermute | solution.py:411
  136.3 2.9 %collective-permute-start.12 = (f32[16,256]{1,0:T(8,128)S(1)}, f32[16,256]{1,0:T(8,128)S(1)}, u32[]{:S(2)}, u32[]{:S(2)}) collective-permute-start(f32[16,256]{1,0:T(8,128)S(1)} %fusion.7.refs_0_), channel_id=1, source_target_pairs={{0,2},{1,3},{2,0},{3,1},{4,6},{5,7},{6,4},{7,5},{8,10},{9,11},{10,... | collective-permute-start | bytes 49160 | tf_op jit(solution)/shard_map/ppermute | solution.py:411
  (33 shorter events, 16.1 us)
Async XLA Ops:
  0.6 0.7 copy-start.2
  2.6 20.6 %all-to-all-start = ((s32[64,1,128]{2,1,0:T(1,128)}), s32[64,1,128]{2,1,0:T(1,128)S(1)}, u32[]{:S(2)}, u32[]{:S(2)}) async-start(s32[64,1,128]{2,1,0:T(1,128)} %shard_map.68), calls=%async_computation | async-start | bytes 65536 | tf_op jit(solution)/shard_map/all_to_all | solution.py:329
  14.6 1.4 copy-start
  23.2 2.2 %copy-start.1 = (s32[64,1,128]{2,1,0:T(1,128)}, s32[64,1,128]{2,1,0:T(1,128)S(1)}, u32[]{:S(2)}) copy-start(s32[64,1,128]{2,1,0:T(1,128)S(1)} %all-to-all-done.asked_ref) | copy-start | bytes 98308
  25.4 44.2 %all-to-all-start.1 = ((bf16[64,24,512]{2,1,0:T(8,128)(2,1)}), bf16[64,24,512]{2,1,0:T(8,128)(2,1)S(1)}, u32[]{:S(2)}, u32[]{:S(2)}) async-start(bf16[64,24,512]{2,1,0:T(8,128)(2,1)} %bitcast.2), calls=%async_computation.1 | async-start | bytes 3145728 | tf_op jit(solution)/shard_map/all_to_all | solution.py:339
  77.0 47.2 %all-to-all-start.2 = ((bf16[64,24,512]{2,1,0:T(8,128)(2,1)}), bf16[64,24,512]{2,1,0:T(8,128)(2,1)S(1)}, u32[]{:S(2)}, u32[]{:S(2)}) async-start(bf16[64,24,512]{2,1,0:T(8,128)(2,1)} %bitcast.6), calls=%async_computation.2 | async-start | bytes 3145728 | tf_op jit(solution)/shard_map/all_to_all | solution.py:363
  86.9 2.9 %collective-permute-start = (bf16[512,1024]{1,0:T(8,128)(2,1)}, bf16[512,1024]{1,0:T(8,128)(2,1)S(1)}, u32[]{:S(2)}, u32[]{:S(2)}) collective-permute-start(bf16[512,1024]{1,0:T(8,128)(2,1)} %shard_map.75), channel_id=1, source_target_pairs={{0,4},{4,0},{1,5},{5,1},{2,6},{6,2},{3,7},{7,3},{8,12},{12,8},{9,1... | collective-permute-start | bytes 3145736 | tf_op jit(solution)/shard_map/ppermute | solution.py:377
  90.8 10.9 %collective-permute-start.1 = (bf16[512,256]{1,0:T(8,128)(2,1)}, bf16[512,256]{1,0:T(8,128)(2,1)S(1)}, u32[]{:S(2)}, u32[]{:S(2)}) collective-permute-start(bf16[512,256]{1,0:T(8,128)(2,1)} %get-tuple-element.21), channel_id=1, source_target_pairs={{0,2},{1,3},{2,0},{3,1},{4,6},{5,7},{6,4},{7,5},{8,10},{9,11},{10,... | collective-permute-start | bytes 786440 | tf_op jit(solution)/shard_map/ppermute | solution.py:386
  94.0 12.5 %collective-permute-start.2 = (bf16[512,256]{1,0:T(8,128)(2,1)}, bf16[512,256]{1,0:T(8,128)(2,1)S(1)}, u32[]{:S(2)}, u32[]{:S(2)}) collective-permute-start(bf16[512,256]{1,0:T(8,128)(2,1)} %get-tuple-element.22), channel_id=1, source_target_pairs={{0,1},{1,2},{2,3},{3,0},{4,5},{5,6},{6,7},{7,4},{8,9},{9,10},{10,1... | collective-permute-start | bytes 786440 | tf_op jit(solution)/shard_map/ppermute | solution.py:386
  94.7 12.3 %collective-permute-start.3 = (bf16[512,256]{1,0:T(8,128)(2,1)S(1)}, bf16[512,256]{1,0:T(8,128)(2,1)}, u32[]{:S(2)}, u32[]{:S(2)}) collective-permute-start(bf16[512,256]{1,0:T(8,128)(2,1)S(1)} %get-tuple-element.23), channel_id=1, source_target_pairs={{0,3},{1,0},{2,1},{3,2},{4,7},{5,4},{6,5},{7,6},{8,11},{9,8},{10,9... | collective-permute-start | bytes 786440 | tf_op jit(solution)/shard_map/ppermute | solution.py:386
  108.1 7.8 %collective-permute-start.4 = (bf16[128,256]{1,0:T(8,128)(2,1)S(1)}, bf16[128,256]{1,0:T(8,128)(2,1)S(1)}, u32[]{:S(2)}, u32[]{:S(2)}) collective-permute-start(bf16[128,256]{1,0:T(8,128)(2,1)S(1)} %get-tuple-element.26), channel_id=1, source_target_pairs={{0,128},{64,192},{128,0},{192,64},{1,129},{65,193},{129,1},{193,65... | collective-permute-start | bytes 196616 | tf_op jit(solution)/shard_map/ppermute | solution.py:312
  110.4 6.7 %collective-permute-start.5 = (bf16[128,256]{1,0:T(8,128)(2,1)S(1)}, bf16[128,256]{1,0:T(8,128)(2,1)S(1)}, u32[]{:S(2)}, u32[]{:S(2)}) collective-permute-start(bf16[128,256]{1,0:T(8,128)(2,1)S(1)} %get-tuple-element.28), channel_id=1, source_target_pairs={{0,64},{64,128},{128,192},{192,0},{1,65},{65,129},{129,193},{193,1... | collective-permute-start | bytes 196616 | tf_op jit(solution)/shard_map/ppermute | solution.py:312
  110.4 7.9 %collective-permute-start.6 = (bf16[128,256]{1,0:T(8,128)(2,1)S(1)}, bf16[128,256]{1,0:T(8,128)(2,1)S(1)}, u32[]{:S(2)}, u32[]{:S(2)}) collective-permute-start(bf16[128,256]{1,0:T(8,128)(2,1)S(1)} %get-tuple-element.27), channel_id=1, source_target_pairs={{0,192},{64,0},{128,64},{192,128},{1,193},{65,1},{129,65},{193,129... | collective-permute-start | bytes 196616 | tf_op jit(solution)/shard_map/ppermute | solution.py:312
  118.4 9.5 %collective-permute-start.7 = (bf16[4,16,256]{2,1,0:T(8,128)(2,1)S(1)}, bf16[4,16,256]{2,1,0:T(8,128)(2,1)S(1)}, u32[]{:S(2)}, u32[]{:S(2)}) collective-permute-start(bf16[4,16,256]{2,1,0:T(8,128)(2,1)S(1)} %fusion.5), channel_id=1, source_target_pairs={{0,32},{8,40},{16,48},{24,56},{32,0},{40,8},{48,16},{56,24},{1,33}... | collective-permute-start | bytes 98312 | tf_op jit(solution)/shard_map/ppermute | solution.py:393
  128.0 3.7 %collective-permute-start.10 = (bf16[16,256]{1,0:T(8,128)(2,1)S(1)}, bf16[16,256]{1,0:T(8,128)(2,1)S(1)}, u32[]{:S(2)}, u32[]{:S(2)}) collective-permute-start(bf16[16,256]{1,0:T(8,128)(2,1)S(1)} %get-tuple-element.30), channel_id=1, source_target_pairs={{0,24},{8,0},{16,8},{24,16},{32,56},{40,32},{48,40},{56,48},{1,25}... | collective-permute-start | bytes 24584 | tf_op jit(solution)/shard_map/ppermute | solution.py:405
  129.0 5.4 %collective-permute-start.8 = (bf16[16,256]{1,0:T(8,128)(2,1)S(1)}, bf16[16,256]{1,0:T(8,128)(2,1)S(1)}, u32[]{:S(2)}, u32[]{:S(2)}) collective-permute-start(bf16[16,256]{1,0:T(8,128)(2,1)S(1)} %get-tuple-element.29), channel_id=1, source_target_pairs={{0,8},{8,16},{16,24},{24,0},{32,40},{40,48},{48,56},{56,32},{1,9},... | collective-permute-start | bytes 24584 | tf_op jit(solution)/shard_map/ppermute | solution.py:405
  130.1 4.5 %collective-permute-start.9 = (bf16[16,256]{1,0:T(8,128)(2,1)S(1)}, bf16[16,256]{1,0:T(8,128)(2,1)S(1)}, u32[]{:S(2)}, u32[]{:S(2)}) collective-permute-start(bf16[16,256]{1,0:T(8,128)(2,1)S(1)} %get-tuple-element.31), channel_id=1, source_target_pairs={{0,16},{8,24},{16,0},{24,8},{32,48},{40,56},{48,32},{56,40},{1,17}... | collective-permute-start | bytes 24584 | tf_op jit(solution)/shard_map/ppermute | solution.py:405
  134.6 5.7 %collective-permute-start.11 = (f32[16,256]{1,0:T(8,128)S(1)}, f32[16,256]{1,0:T(8,128)S(1)}, u32[]{:S(2)}, u32[]{:S(2)}) collective-permute-start(f32[16,256]{1,0:T(8,128)S(1)} %fusion.7.refs_0_), channel_id=1, source_target_pairs={{0,1},{1,2},{2,3},{3,0},{4,5},{5,6},{6,7},{7,4},{8,9},{9,10},{10,1... | collective-permute-start | bytes 49160 | tf_op jit(solution)/shard_map/ppermute | solution.py:411
  136.3 5.2 %collective-permute-start.12 = (f32[16,256]{1,0:T(8,128)S(1)}, f32[16,256]{1,0:T(8,128)S(1)}, u32[]{:S(2)}, u32[]{:S(2)}) collective-permute-start(f32[16,256]{1,0:T(8,128)S(1)} %fusion.7.refs_0_), channel_id=1, source_target_pairs={{0,2},{1,3},{2,0},{3,1},{4,6},{5,7},{6,4},{7,5},{8,10},{9,11},{10,... | collective-permute-start | bytes 49160 | tf_op jit(solution)/shard_map/ppermute | solution.py:411
  139.2 3.7 %collective-permute-start.13 = (f32[16,256]{1,0:T(8,128)S(1)}, f32[16,256]{1,0:T(8,128)S(1)}, u32[]{:S(2)}, u32[]{:S(2)}) collective-permute-start(f32[16,256]{1,0:T(8,128)S(1)} %fusion.7.refs_0_), channel_id=1, source_target_pairs={{0,3},{1,0},{2,1},{3,2},{4,7},{5,4},{6,5},{7,6},{8,11},{9,8},{10,9... | collective-permute-start | bytes 49160 | tf_op jit(solution)/shard_map/ppermute | solution.py:411

commit v5 on v4

--- a/solution.py
+++ b/solution.py
@@ -104,8 +104,8 @@
 
 
 def prepare_kernel(
-    members_ref, pairs_ref, labels_ref, asked_ref,
-    gather_ref, table_ref, back_ref, padded,
+    members_ref, pairs_ref, labels_ref, asked_ref, weight_ref,
+    gather_ref, table_ref, back_ref, turned_ref, padded,
 ):
     arrivals = gather_ref.shape[1]
     n_rec = arrivals // (2 * CAP)
@@ -165,12 +165,13 @@
     wanted = wanted_rows(asked_ref).reshape(arrivals, 1).astype(f32)
     wanted = jnp.transpose(jnp.broadcast_to(wanted, (arrivals, 128)))[0:1, :].astype(i32)
     back_ref[...] = ones_where(iota((2 * LAN, arrivals), 0) == wanted).astype(bf16)
+    turned_ref[...] = jnp.transpose(weight_ref[...])
 
 
 def owner_kernel(
-    arrived_ref, gather_hbm, weight_hbm, table_hbm,
+    arrived_ref, gather_hbm, weight_hbm, turned_hbm, table_hbm,
     out_hbm, rows_ref, dscore_ref,
-    gather_s, rows_s, right_s, stacked_s, weight_s, spread_s, terms_s, out_s, sems, out_sems,
+    gather_s, rows_s, right_s, stacked_s, weight_s, turned_s, spread_s, terms_s, out_s, sems, out_sems,
 ):
     arrivals, half = arrived_ref.shape
     width = 2 * half
@@ -180,6 +181,7 @@
         (gather_hbm.at[:SUB], gather_s.at[:SUB]),
         (gather_hbm.at[SUB:], gather_s.at[SUB:]),
         (weight_hbm, weight_s),
+        (turned_hbm, turned_s),
         (terms_hbm, terms_s),
         (spread_hbm, spread_s),
     ]):
@@ -194,7 +196,8 @@
     rows_ref[...] = rows
     loads[2].wait()
     left = mm(rows, weight_s[...]).astype(bf16)
-    right_s[:SUB, :] = nt(rows, weight_s[...]).astype(bf16)
+    loads[3].wait()
+    right_s[:SUB, :] = mm(rows, turned_s[...]).astype(bf16)
     right_s[SUB:, :] = jnp.zeros((LAN - SUB, width), bf16)
     shifted = nt(left, rows_s[...]) - MARGIN
     small = jnp.exp(-jnp.abs(shifted))
@@ -202,7 +205,7 @@
     smaller = small * larger
     up = jnp.where(shifted >= 0, larger, smaller)
     down = jnp.where(shifted >= 0, smaller, larger)
-    loads[3].wait()
+    loads[4].wait()
     count = terms_s[:SUB, :LAN].astype(f32)
     plus = terms_s[:SUB, LAN:].astype(f32)
     minus = terms_s[SUB:, :LAN].astype(f32)
@@ -215,7 +218,7 @@
     stacked_s[SUB:LAN, :] = jnp.zeros((LAN - SUB, half), bf16)
     stacked_s[LAN : LAN + SUB, :] = grad[:, half:]
     stacked_s[LAN + SUB :, :] = jnp.zeros((LAN - SUB, half), bf16)
-    loads[4].wait()
+    loads[5].wait()
     parts = out_sems.shape[0]
     size = arrivals // parts
     stores = []
@@ -228,19 +231,32 @@
         store.wait()
 
 
-def weight_kernel(core_ref, rows_ref, dscore_ref, out_ref, rows_s):
+def half_term(core, rows_ref, dscore_ref, rows_s):
     width = rows_ref.shape[1]
     rows_s[:SUB, :] = rows_ref[...]
     rows_s[SUB:, :] = jnp.zeros((LAN - SUB, width), bf16)
     carried = mm(dscore_ref[...], rows_s[...]).astype(bf16)
-    core = core_ref[0]
     tile = 256
     for t in range(width // tile):
         part = tn(rows_s[:SUB, t * tile : (t + 1) * tile], carried)
         part = part.reshape(tile // 32, 2, 16, width)
         even = jnp.broadcast_to(core, (tile // 32, 16, width)) == 0
-        part = jnp.where(even, part[:, 0], part[:, 1]).reshape(tile // 2, width)
-        out_ref[t * tile // 2 : (t + 1) * tile // 2, :] = part.astype(out_ref.dtype)
+        yield pl.ds(t * tile // 2, tile // 2), jnp.where(even, part[:, 0], part[:, 1]).reshape(tile // 2, width)
+
+
+def keep_kernel(core_ref, rows_ref, dscore_ref, out_ref, rows_s):
+    for place, part in half_term(core_ref[0], rows_ref, dscore_ref, rows_s):
+        out_ref[place, :] = part
+
+
+def send_kernel(core_ref, rows_ref, dscore_ref, out_hbm, rows_s, out_s, sems):
+    stores = []
+    for n, (place, part) in enumerate(half_term(core_ref[0], rows_ref, dscore_ref, rows_s)):
+        out_s[place, :] = part.astype(bf16)
+        stores.append(pltpu.make_async_copy(out_s.at[place], out_hbm.at[place], sems.at[n]))
+        stores[n].start()
+    for store in stores:
+        store.wait()
 
 
 def split_kernel(y_ref, keep_ref, got_ref, own_ref, *send_refs):
@@ -339,15 +355,16 @@
     arrived = lax.all_to_all(
         found.reshape(n_rec, 2 * CAP, half), REC, split_axis=0, concat_axis=0, tiled=True
     ).reshape(arrivals, half)
-    gather, table, back = call(
+    gather, table, back, turned = call(
         prepare_kernel,
         [
             struct((2 * SUB, arrivals), bf16),
             struct((arrivals + 2 * SUB, 2 * LAN), bf16),
             struct((2 * LAN, arrivals), bf16),
+            struct((width, width), bf16),
         ],
-        4, [padded], moved=8 * MIB,
-    )(ids, pair_slots[0].T, labels, asked)
+        5, [padded], moved=12 * MIB,
+    )(ids, pair_slots[0].T, labels, asked, weight)
 
     out, rows, dscore = call(
         owner_kernel,
@@ -355,11 +372,13 @@
         1,
         [pltpu.VMEM((2 * SUB, arrivals), bf16)]
         + [pltpu.VMEM((LAN, width), bf16)] * 2
-        + [pltpu.VMEM((2 * LAN, half), bf16), pltpu.VMEM((width, width), bf16), pltpu.VMEM((arrivals, 2 * LAN), bf16)]
+        + [pltpu.VMEM((2 * LAN, half), bf16)]
+        + [pltpu.VMEM((width, width), bf16)] * 2
+        + [pltpu.VMEM((arrivals, 2 * LAN), bf16)]
         + [pltpu.VMEM((2 * SUB, 2 * LAN), bf16), pltpu.VMEM((arrivals, half), bf16)]
-        + [dma((5,)), dma((4,))],
-        flops=4 * 10**9, moved=12 * MIB, hbm=3, hbm_outs=1, grant=49.5,
-    )(arrived, gather, weight, table)
+        + [dma((6,)), dma((4,))],
+        flops=4 * 10**9, moved=14 * MIB, hbm=4, hbm_outs=1, grant=49.5,
+    )(arrived, gather, weight, turned, table)
     returned = lax.all_to_all(
         out.reshape(n_rec, 2 * CAP, half), REC, split_axis=0, concat_axis=0, tiled=True
     ).reshape(arrivals, half)
@@ -367,13 +386,15 @@
     core = lax.axis_index("c").astype(i32).reshape(1)
     rows_core = width // NC
 
-    def term(half_of, dtype):
-        return call(
-            weight_kernel, struct((rows_core, width), dtype), 2, [pltpu.VMEM((LAN, width), bf16)],
-            flops=10**9, moved=4 * MIB, smem=1, grant=24,
-        )(half_of, rows, dscore)
-
-    send, keep = term(1 - core, bf16), term(core, f32)
+    send = call(
+        send_kernel, struct((rows_core, width), bf16), 2,
+        [pltpu.VMEM((LAN, width), bf16), pltpu.VMEM((rows_core, width), bf16), dma((4,))],
+        flops=10**9, moved=4 * MIB, smem=1, hbm_outs=1, grant=24,
+    )(1 - core, rows, dscore)
+    keep = call(
+        keep_kernel, struct((rows_core, width), f32), 2, [pltpu.VMEM((LAN, width), bf16)],
+        flops=10**9, moved=4 * MIB, smem=1, grant=24,
+    )(core, rows, dscore)
     got = lax.ppermute(send, "c", [(0, 1), (1, 0)])
     y = lax.axis_index("y").astype(i32).reshape(1)
     cols = width // NY

time: 144 us -> 144 us (level)
  waiting for transfers between devices: 62 us -> 60.3 us
  Pallas kernels: 26.7 us -> 28.3 us
    pallas_call x1, Pallas kernels: 6.18 us -> 7.9 us  [on_device(): call(prepare_kernel, [struct((2 * SUB, arrivals), bf16), struct((arrivals...]
    all_to_all x1, waiting for transfers between devices: 32.4 us -> 30.7 us  [on_device(): lax.all_to_all(found.reshape(n_rec, 2 * CAP, half), REC, split_axis=0, co...]
  transfers between devices with their start and end apart: 17 -> 17, of which waited for: 14 -> 14; matrix products, arithmetic and copies ran while one was open for 1% -> 1% of each run, Pallas kernels for 11% -> 12%
where the time goes in v5:
time: 144 us
  waiting for transfers between devices  60.3 us (42%)
  starting transfers between devices  51.3 us (36%)
  Pallas kernels  28.3 us (20%)
  local copies, waits for them, and re-layouts  2.15 us (1%)
    all_to_all x1, waiting for transfers between devices, on_device(): lax.all_to_all(found.reshape(n_rec, 2 * CAP, half), REC, split_axis=0, co...  30.7 us
    all_to_all x1, starting transfers between devices, on_device(): lax.all_to_all(requests, REC, split_axis=0, concat_axis=0, tiled=True)  12 us
    ppermute x3, waiting for transfers between devices, on_device(): lax.ppermute(sends[k - 1], 'y', [(i, (i + k) % NY) for i in range(NY)])  9.73 us
    pallas_call x1, Pallas kernels, on_device(): call(prepare_kernel, [struct((2 * SUB, arrivals), bf16), struct((arrivals...  7.9 us
    pallas_call x1, Pallas kernels, on_device(): call(owner_kernel, [struct((arrivals, half), bf16), struct((SUB, width),...  7.52 us
    all_to_all x1, starting transfers between devices, on_device(): lax.all_to_all(out.reshape(n_rec, 2 * CAP, half), REC, split_axis=0, conc...  7.5 us
    all_to_all x1, waiting for transfers between devices, on_device(): lax.all_to_all(requests, REC, split_axis=0, concat_axis=0, tiled=True)  7.03 us
    ppermute x3, starting transfers between devices, on_device(): lax.ppermute(sends[k - 1], 'y', [(i, (i + k) % NY) for i in range(NY)])  6.44 us
  transfers between devices with their start and end apart: 17, of which 14 were waited for; matrix products, arithmetic and copies ran while one was open for 1% of the time, Pallas kernels for 12%

profile of v5, /device:TPU:2, one launch (start us, length us, event | category | flops | bytes accessed | tf_op | source)
XLA Modules:
  0.0 143.9 jit_solution(14041365114688819060)
XLA Ops:
  2.6 12.0 %all-to-all-start = ((s32[64,1,128]{2,1,0:T(1,128)}), s32[64,1,128]{2,1,0:T(1,128)S(1)}, u32[]{:S(2)}, u32[]{:S(2)}) async-start(s32[64,1,128]{2,1,0:T(1,128)} %shard_map.68), calls=%async_computation | async-start | bytes 65536 | tf_op jit(solution)/shard_map/all_to_all | solution.py:345
  14.6 1.4 copy-done
  16.1 7.0 %all-to-all-done.asked_ref = s32[64,1,128]{2,1,0:T(1,128)S(1)} async-done(((s32[64,1,128]{2,1,0:T(1,128)}), s32[64,1,128]{2,1,0:T(1,128)S(1)}, u32[]{:S(2)}, u32[]{:S(2)}) %all-to-all-start) | async-done | bytes 32800 | tf_op jit(solution)/shard_map/all_to_all | solution.py:345
  23.2 2.2 %shard_map.70 = bf16[1536,512]{1,0:T(8,128)(2,1)} custom-call(s32[64,1,128]{2,1,0:T(1,128)S(1)} %all-to-all-done.asked_ref, bf16[768,512]{1,0:T(8,128)(2,1)S(1)} %shard_map.69.stacked_ref), custom_call_target="tpu_custom_call" | custom-call | flops 1207959552 | bytes 3145728 | tf_op jit(solution)/shard_map/pallas_call | solution.py:350
  25.4 5.6 %all-to-all-start.1 = ((bf16[64,24,512]{2,1,0:T(8,128)(2,1)}), bf16[64,24,512]{2,1,0:T(8,128)(2,1)S(1)}, u32[]{:S(2)}, u32[]{:S(2)}) async-start(bf16[64,24,512]{2,1,0:T(8,128)(2,1)} %bitcast.2), calls=%async_computation.1 | async-start | bytes 3145728 | tf_op jit(solution)/shard_map/all_to_all | solution.py:355
  31.0 7.9 %shard_map.71 = (bf16[544,1536]{1,0:T(8,128)(2,1)}, bf16[2080,768]{1,0:T(8,128)(2,1)}, bf16[768,1536]{1,0:T(8,128)(2,1)}, bf16[1024,1024]{1,0:T(8,128)(2,1)}) custom-call(s32[8,99]{1,0:T(8,128)} %bitcast.45, s32[2,128]{1,0:T(2,128)} %bitcast.52, s32[1,128]{1,0:T(1,128)} %labels_ref.1, s32[64,1,128]{2,1,0:T(1,128)} %copy-done.1, bf16[1024,1024]{1,0:T(8,128)(2,1)} %weight_hbm.1), custom_call_target="tpu_custom_call" | custom-call | bytes 12582912 | tf_op jit(solution)/shard_map/pallas_call | solution.py:358
  38.9 30.7 %all-to-all-done.1 = bf16[64,24,512]{2,1,0:T(8,128)(2,1)S(1)} async-done(((bf16[64,24,512]{2,1,0:T(8,128)(2,1)}), bf16[64,24,512]{2,1,0:T(8,128)(2,1)S(1)}, u32[]{:S(2)}, u32[]{:S(2)}) %all-to-all-start.1) | async-done | bytes 1572896 | tf_op jit(solution)/shard_map/all_to_all | solution.py:355
  69.6 7.5 %shard_map.72 = (bf16[1536,512]{1,0:T(8,128)(2,1)}, bf16[272,1024]{1,0:T(8,128)(2,1)S(1)}, bf16[272,384]{1,0:T(8,128)(2,1)S(1)}) custom-call(bf16[1536,512]{1,0:T(8,128)(2,1)S(1)} %bitcast.44, bf16[544,1536]{1,0:T(8,128)(2,1)} %get-tuple-element.15.gather_hbm, bf16[1024,1024]{1,0:T(8,128)(2,1)} %weight_hbm.1, ...), custom_call_target="tpu_custom_call" | custom-call | flops 4000000000 | bytes 14680064 | tf_op jit(solution)/shard_map/pallas_call | solution.py:369
  77.1 7.5 %all-to-all-start.2 = ((bf16[64,24,512]{2,1,0:T(8,128)(2,1)}), bf16[64,24,512]{2,1,0:T(8,128)(2,1)S(1)}, u32[]{:S(2)}, u32[]{:S(2)}) async-start(bf16[64,24,512]{2,1,0:T(8,128)(2,1)} %bitcast.6), calls=%async_computation.2 | async-start | bytes 3145728 | tf_op jit(solution)/shard_map/all_to_all | solution.py:382
  84.7 2.3 %shard_map.75 = bf16[512,1024]{1,0:T(8,128)(2,1)} custom-call(s32[1]{0:T(128)S(6)} %sub.11.core_ref, bf16[272,1024]{1,0:T(8,128)(2,1)S(1)} %get-tuple-element.20.rows_ref, bf16[272,384]{1,0:T(8,128)(2,1)S(1)} %get-tuple-element.21.dscore_ref), custom_call_target="tpu_custom_call" | custom-call | flops 1000000000 | bytes 4194304 | tf_op jit(solution)/shard_map/pallas_call | solution.py:389
  87.2 1.5 %shard_map.74.keep_ref = f32[512,1024]{1,0:T(8,128)S(1)} custom-call(s32[1]{0:T(128)} %bitcast.9.core_ref, bf16[272,1024]{1,0:T(8,128)(2,1)S(1)} %get-tuple-element.20.rows_ref, bf16[272,384]{1,0:T(8,128)(2,1)S(1)} %get-tuple-element.21.dscore_ref), custom_call_target="tpu_custom_call" | custom-call | flops 1000000000 | bytes 4194304 | tf_op jit(solution)/shard_map/pallas_call | solution.py:394
  91.0 3.2 %collective-permute-start.1 = (bf16[512,256]{1,0:T(8,128)(2,1)}, bf16[512,256]{1,0:T(8,128)(2,1)S(1)}, u32[]{:S(2)}, u32[]{:S(2)}) collective-permute-start(bf16[512,256]{1,0:T(8,128)(2,1)} %get-tuple-element.23), channel_id=1, source_target_pairs={{0,2},{1,3},{2,0},{3,1},{4,6},{5,7},{6,4},{7,5},{8,10},{9,11},{10,... | collective-permute-start | bytes 786440 | tf_op jit(solution)/shard_map/ppermute | solution.py:407
  94.9 2.6 %collective-permute-start.3 = (bf16[512,256]{1,0:T(8,128)(2,1)S(1)}, bf16[512,256]{1,0:T(8,128)(2,1)}, u32[]{:S(2)}, u32[]{:S(2)}) collective-permute-start(bf16[512,256]{1,0:T(8,128)(2,1)S(1)} %get-tuple-element.25), channel_id=1, source_target_pairs={{0,3},{1,0},{2,1},{3,2},{4,7},{5,4},{6,5},{7,6},{8,11},{9,8},{10,9... | collective-permute-start | bytes 786440 | tf_op jit(solution)/shard_map/ppermute | solution.py:407
  97.4 4.5 %collective-permute-done.1 = bf16[512,256]{1,0:T(8,128)(2,1)S(1)} collective-permute-done((bf16[512,256]{1,0:T(8,128)(2,1)}, bf16[512,256]{1,0:T(8,128)(2,1)S(1)}, u32[]{:S(2)}, u32[]{:S(2)}) %collective-permute-start.1) | collective-permute-done | bytes 262176 | tf_op jit(solution)/shard_map/ppermute | solution.py:407
  101.9 4.8 %collective-permute-done.2 = bf16[512,256]{1,0:T(8,128)(2,1)S(1)} collective-permute-done((bf16[512,256]{1,0:T(8,128)(2,1)}, bf16[512,256]{1,0:T(8,128)(2,1)S(1)}, u32[]{:S(2)}, u32[]{:S(2)}) %collective-permute-start.2) | collective-permute-done | bytes 262176 | tf_op jit(solution)/shard_map/ppermute | solution.py:407
  108.3 2.4 %collective-permute-start.4 = (bf16[128,256]{1,0:T(8,128)(2,1)S(1)}, bf16[128,256]{1,0:T(8,128)(2,1)S(1)}, u32[]{:S(2)}, u32[]{:S(2)}) collective-permute-start(bf16[128,256]{1,0:T(8,128)(2,1)S(1)} %get-tuple-element.28), channel_id=1, source_target_pairs={{0,128},{64,192},{128,0},{192,64},{1,129},{65,193},{129,1},{193,65... | collective-permute-start | bytes 196616 | tf_op jit(solution)/shard_map/ppermute | solution.py:328
  110.6 2.0 %collective-permute-start.6 = (bf16[128,256]{1,0:T(8,128)(2,1)S(1)}, bf16[128,256]{1,0:T(8,128)(2,1)S(1)}, u32[]{:S(2)}, u32[]{:S(2)}) collective-permute-start(bf16[128,256]{1,0:T(8,128)(2,1)S(1)} %get-tuple-element.29), channel_id=1, source_target_pairs={{0,192},{64,0},{128,64},{192,128},{1,193},{65,1},{129,65},{193,129... | collective-permute-start | bytes 196616 | tf_op jit(solution)/shard_map/ppermute | solution.py:328
  112.6 3.7 %collective-permute-done.4 = bf16[128,256]{1,0:T(8,128)(2,1)S(1)} collective-permute-done((bf16[128,256]{1,0:T(8,128)(2,1)S(1)}, bf16[128,256]{1,0:T(8,128)(2,1)S(1)}, u32[]{:S(2)}, u32[]{:S(2)}) %collective-permute-start.4) | collective-permute-done | bytes 65568 | tf_op jit(solution)/shard_map/ppermute | solution.py:328
  118.7 5.7 %collective-permute-start.7 = (bf16[4,16,256]{2,1,0:T(8,128)(2,1)S(1)}, bf16[4,16,256]{2,1,0:T(8,128)(2,1)S(1)}, u32[]{:S(2)}, u32[]{:S(2)}) collective-permute-start(bf16[4,16,256]{2,1,0:T(8,128)(2,1)S(1)} %fusion.5), channel_id=1, source_target_pairs={{0,32},{8,40},{16,48},{24,56},{32,0},{40,8},{48,16},{56,24},{1,33}... | collective-permute-start | bytes 98312 | tf_op jit(solution)/shard_map/ppermute | solution.py:414
  124.4 3.7 %shard_map.73 = f32[384,1024]{1,0:T(8,128)} custom-call(bf16[1536,512]{1,0:T(8,128)(2,1)S(1)} %bitcast.42, bf16[768,1536]{1,0:T(8,128)(2,1)} %get-tuple-element.19.pick_hbm), custom_call_target="tpu_custom_call" | custom-call | flops 1207959552 | bytes 6291456 | tf_op jit(solution)/shard_map/pallas_call | solution.py:415
  130.3 1.5 %collective-permute-start.9 = (bf16[16,256]{1,0:T(8,128)(2,1)S(1)}, bf16[16,256]{1,0:T(8,128)(2,1)S(1)}, u32[]{:S(2)}, u32[]{:S(2)}) collective-permute-start(bf16[16,256]{1,0:T(8,128)(2,1)S(1)} %get-tuple-element.33), channel_id=1, source_target_pairs={{0,16},{8,24},{16,0},{24,8},{32,48},{40,56},{48,32},{56,40},{1,17}... | collective-permute-start | bytes 24584 | tf_op jit(solution)/shard_map/ppermute | solution.py:426
  132.0 2.8 %collective-permute-done.8 = bf16[16,256]{1,0:T(8,128)(2,1)S(1)} collective-permute-done((bf16[16,256]{1,0:T(8,128)(2,1)S(1)}, bf16[16,256]{1,0:T(8,128)(2,1)S(1)}, u32[]{:S(2)}, u32[]{:S(2)}) %collective-permute-start.8) | collective-permute-done | bytes 8224 | tf_op jit(solution)/shard_map/ppermute | solution.py:426
  134.9 1.7 %collective-permute-start.11 = (f32[16,256]{1,0:T(8,128)S(1)}, f32[16,256]{1,0:T(8,128)S(1)}, u32[]{:S(2)}, u32[]{:S(2)}) collective-permute-start(f32[16,256]{1,0:T(8,128)S(1)} %fusion.7.refs_0_), channel_id=1, source_target_pairs={{0,1},{1,2},{2,3},{3,0},{4,5},{5,6},{6,7},{7,4},{8,9},{9,10},{10,1... | collective-permute-start | bytes 49160 | tf_op jit(solution)/shard_map/ppermute | solution.py:432
  136.6 2.9 %collective-permute-start.12 = (f32[16,256]{1,0:T(8,128)S(1)}, f32[16,256]{1,0:T(8,128)S(1)}, u32[]{:S(2)}, u32[]{:S(2)}) collective-permute-start(f32[16,256]{1,0:T(8,128)S(1)} %fusion.7.refs_0_), channel_id=1, source_target_pairs={{0,2},{1,3},{2,0},{3,1},{4,6},{5,7},{6,4},{7,5},{8,10},{9,11},{10,... | collective-permute-start | bytes 49160 | tf_op jit(solution)/shard_map/ppermute | solution.py:432
  (33 shorter events, 15.9 us)
Async XLA Ops:
  0.6 0.7 copy-start.2
  2.6 20.6 %all-to-all-start = ((s32[64,1,128]{2,1,0:T(1,128)}), s32[64,1,128]{2,1,0:T(1,128)S(1)}, u32[]{:S(2)}, u32[]{:S(2)}) async-start(s32[64,1,128]{2,1,0:T(1,128)} %shard_map.68), calls=%async_computation | async-start | bytes 65536 | tf_op jit(solution)/shard_map/all_to_all | solution.py:345
  14.6 1.4 copy-start
  23.2 2.2 %copy-start.1 = (s32[64,1,128]{2,1,0:T(1,128)}, s32[64,1,128]{2,1,0:T(1,128)S(1)}, u32[]{:S(2)}) copy-start(s32[64,1,128]{2,1,0:T(1,128)S(1)} %all-to-all-done.asked_ref) | copy-start | bytes 98308
  25.4 44.2 %all-to-all-start.1 = ((bf16[64,24,512]{2,1,0:T(8,128)(2,1)}), bf16[64,24,512]{2,1,0:T(8,128)(2,1)S(1)}, u32[]{:S(2)}, u32[]{:S(2)}) async-start(bf16[64,24,512]{2,1,0:T(8,128)(2,1)} %bitcast.2), calls=%async_computation.1 | async-start | bytes 3145728 | tf_op jit(solution)/shard_map/all_to_all | solution.py:355
  77.1 47.3 %all-to-all-start.2 = ((bf16[64,24,512]{2,1,0:T(8,128)(2,1)}), bf16[64,24,512]{2,1,0:T(8,128)(2,1)S(1)}, u32[]{:S(2)}, u32[]{:S(2)}) async-start(bf16[64,24,512]{2,1,0:T(8,128)(2,1)} %bitcast.6), calls=%async_computation.2 | async-start | bytes 3145728 | tf_op jit(solution)/shard_map/all_to_all | solution.py:382
  87.0 3.0 %collective-permute-start = (bf16[512,1024]{1,0:T(8,128)(2,1)}, bf16[512,1024]{1,0:T(8,128)(2,1)S(1)}, u32[]{:S(2)}, u32[]{:S(2)}) collective-permute-start(bf16[512,1024]{1,0:T(8,128)(2,1)} %shard_map.75), channel_id=1, source_target_pairs={{0,4},{4,0},{1,5},{5,1},{2,6},{6,2},{3,7},{7,3},{8,12},{12,8},{9,1... | collective-permute-start | bytes 3145736 | tf_op jit(solution)/shard_map/ppermute | solution.py:398
  91.0 10.9 %collective-permute-start.1 = (bf16[512,256]{1,0:T(8,128)(2,1)}, bf16[512,256]{1,0:T(8,128)(2,1)S(1)}, u32[]{:S(2)}, u32[]{:S(2)}) collective-permute-start(bf16[512,256]{1,0:T(8,128)(2,1)} %get-tuple-element.23), channel_id=1, source_target_pairs={{0,2},{1,3},{2,0},{3,1},{4,6},{5,7},{6,4},{7,5},{8,10},{9,11},{10,... | collective-permute-start | bytes 786440 | tf_op jit(solution)/shard_map/ppermute | solution.py:407
  94.2 12.5 %collective-permute-start.2 = (bf16[512,256]{1,0:T(8,128)(2,1)}, bf16[512,256]{1,0:T(8,128)(2,1)S(1)}, u32[]{:S(2)}, u32[]{:S(2)}) collective-permute-start(bf16[512,256]{1,0:T(8,128)(2,1)} %get-tuple-element.24), channel_id=1, source_target_pairs={{0,1},{1,2},{2,3},{3,0},{4,5},{5,6},{6,7},{7,4},{8,9},{9,10},{10,1... | collective-permute-start | bytes 786440 | tf_op jit(solution)/shard_map/ppermute | solution.py:407
  94.9 12.3 %collective-permute-start.3 = (bf16[512,256]{1,0:T(8,128)(2,1)S(1)}, bf16[512,256]{1,0:T(8,128)(2,1)}, u32[]{:S(2)}, u32[]{:S(2)}) collective-permute-start(bf16[512,256]{1,0:T(8,128)(2,1)S(1)} %get-tuple-element.25), channel_id=1, source_target_pairs={{0,3},{1,0},{2,1},{3,2},{4,7},{5,4},{6,5},{7,6},{8,11},{9,8},{10,9... | collective-permute-start | bytes 786440 | tf_op jit(solution)/shard_map/ppermute | solution.py:407
  108.3 8.0 %collective-permute-start.4 = (bf16[128,256]{1,0:T(8,128)(2,1)S(1)}, bf16[128,256]{1,0:T(8,128)(2,1)S(1)}, u32[]{:S(2)}, u32[]{:S(2)}) collective-permute-start(bf16[128,256]{1,0:T(8,128)(2,1)S(1)} %get-tuple-element.28), channel_id=1, source_target_pairs={{0,128},{64,192},{128,0},{192,64},{1,129},{65,193},{129,1},{193,65... | collective-permute-start | bytes 196616 | tf_op jit(solution)/shard_map/ppermute | solution.py:328
  110.6 6.7 %collective-permute-start.5 = (bf16[128,256]{1,0:T(8,128)(2,1)S(1)}, bf16[128,256]{1,0:T(8,128)(2,1)S(1)}, u32[]{:S(2)}, u32[]{:S(2)}) collective-permute-start(bf16[128,256]{1,0:T(8,128)(2,1)S(1)} %get-tuple-element.30), channel_id=1, source_target_pairs={{0,64},{64,128},{128,192},{192,0},{1,65},{65,129},{129,193},{193,1... | collective-permute-start | bytes 196616 | tf_op jit(solution)/shard_map/ppermute | solution.py:328
  110.6 8.1 %collective-permute-start.6 = (bf16[128,256]{1,0:T(8,128)(2,1)S(1)}, bf16[128,256]{1,0:T(8,128)(2,1)S(1)}, u32[]{:S(2)}, u32[]{:S(2)}) collective-permute-start(bf16[128,256]{1,0:T(8,128)(2,1)S(1)} %get-tuple-element.29), channel_id=1, source_target_pairs={{0,192},{64,0},{128,64},{192,128},{1,193},{65,1},{129,65},{193,129... | collective-permute-start | bytes 196616 | tf_op jit(solution)/shard_map/ppermute | solution.py:328
  118.7 9.4 %collective-permute-start.7 = (bf16[4,16,256]{2,1,0:T(8,128)(2,1)S(1)}, bf16[4,16,256]{2,1,0:T(8,128)(2,1)S(1)}, u32[]{:S(2)}, u32[]{:S(2)}) collective-permute-start(bf16[4,16,256]{2,1,0:T(8,128)(2,1)S(1)} %fusion.5), channel_id=1, source_target_pairs={{0,32},{8,40},{16,48},{24,56},{32,0},{40,8},{48,16},{56,24},{1,33}... | collective-permute-start | bytes 98312 | tf_op jit(solution)/shard_map/ppermute | solution.py:414
  128.2 3.7 %collective-permute-start.10 = (bf16[16,256]{1,0:T(8,128)(2,1)S(1)}, bf16[16,256]{1,0:T(8,128)(2,1)S(1)}, u32[]{:S(2)}, u32[]{:S(2)}) collective-permute-start(bf16[16,256]{1,0:T(8,128)(2,1)S(1)} %get-tuple-element.32), channel_id=1, source_target_pairs={{0,24},{8,0},{16,8},{24,16},{32,56},{40,32},{48,40},{56,48},{1,25}... | collective-permute-start | bytes 24584 | tf_op jit(solution)/shard_map/ppermute | solution.py:426
  129.3 5.4 %collective-permute-start.8 = (bf16[16,256]{1,0:T(8,128)(2,1)S(1)}, bf16[16,256]{1,0:T(8,128)(2,1)S(1)}, u32[]{:S(2)}, u32[]{:S(2)}) collective-permute-start(bf16[16,256]{1,0:T(8,128)(2,1)S(1)} %get-tuple-element.31), channel_id=1, source_target_pairs={{0,8},{8,16},{16,24},{24,0},{32,40},{40,48},{48,56},{56,32},{1,9},... | collective-permute-start | bytes 24584 | tf_op jit(solution)/shard_map/ppermute | solution.py:426
  130.3 4.5 %collective-permute-start.9 = (bf16[16,256]{1,0:T(8,128)(2,1)S(1)}, bf16[16,256]{1,0:T(8,128)(2,1)S(1)}, u32[]{:S(2)}, u32[]{:S(2)}) collective-permute-start(bf16[16,256]{1,0:T(8,128)(2,1)S(1)} %get-tuple-element.33), channel_id=1, source_target_pairs={{0,16},{8,24},{16,0},{24,8},{32,48},{40,56},{48,32},{56,40},{1,17}... | collective-permute-start | bytes 24584 | tf_op jit(solution)/shard_map/ppermute | solution.py:426
  134.9 5.8 %collective-permute-start.11 = (f32[16,256]{1,0:T(8,128)S(1)}, f32[16,256]{1,0:T(8,128)S(1)}, u32[]{:S(2)}, u32[]{:S(2)}) collective-permute-start(f32[16,256]{1,0:T(8,128)S(1)} %fusion.7.refs_0_), channel_id=1, source_target_pairs={{0,1},{1,2},{2,3},{3,0},{4,5},{5,6},{6,7},{7,4},{8,9},{9,10},{10,1... | collective-permute-start | bytes 49160 | tf_op jit(solution)/shard_map/ppermute | solution.py:432
  136.6 5.2 %collective-permute-start.12 = (f32[16,256]{1,0:T(8,128)S(1)}, f32[16,256]{1,0:T(8,128)S(1)}, u32[]{:S(2)}, u32[]{:S(2)}) collective-permute-start(f32[16,256]{1,0:T(8,128)S(1)} %fusion.7.refs_0_), channel_id=1, source_target_pairs={{0,2},{1,3},{2,0},{3,1},{4,6},{5,7},{6,4},{7,5},{8,10},{9,11},{10,... | collective-permute-start | bytes 49160 | tf_op jit(solution)/shard_map/ppermute | solution.py:432
  139.5 3.7 %collective-permute-start.13 = (f32[16,256]{1,0:T(8,128)S(1)}, f32[16,256]{1,0:T(8,128)S(1)}, u32[]{:S(2)}, u32[]{:S(2)}) collective-permute-start(f32[16,256]{1,0:T(8,128)S(1)} %fusion.7.refs_0_), channel_id=1, source_target_pairs={{0,3},{1,0},{2,1},{3,2},{4,7},{5,4},{6,5},{7,6},{8,11},{9,8},{10,9... | collective-permute-start | bytes 49160 | tf_op jit(solution)/shard_map/ppermute | solution.py:432

commit v6 on v4

--- a/solution.py
+++ b/solution.py
@@ -184,7 +184,8 @@
         (spread_hbm, spread_s),
     ]):
         loads.append(pltpu.make_async_copy(source, target, sems.at[n]))
-        loads[n].start()
+        if n < 4:
+            loads[n].start()
     loads[0].wait()
     rows_s[:SUB, :half] = mm(gather_s[:SUB, :], arrived_ref[...]).astype(bf16)
     loads[1].wait()
@@ -193,6 +194,7 @@
     rows = rows_s[:SUB, :]
     rows_ref[...] = rows
     loads[2].wait()
+    loads[4].start()
     left = mm(rows, weight_s[...]).astype(bf16)
     right_s[:SUB, :] = nt(rows, weight_s[...]).astype(bf16)
     right_s[SUB:, :] = jnp.zeros((LAN - SUB, width), bf16)
@@ -228,19 +230,32 @@
         store.wait()
 
 
-def weight_kernel(core_ref, rows_ref, dscore_ref, out_ref, rows_s):
+def half_term(core, rows_ref, dscore_ref, rows_s):
     width = rows_ref.shape[1]
     rows_s[:SUB, :] = rows_ref[...]
     rows_s[SUB:, :] = jnp.zeros((LAN - SUB, width), bf16)
     carried = mm(dscore_ref[...], rows_s[...]).astype(bf16)
-    core = core_ref[0]
     tile = 256
     for t in range(width // tile):
         part = tn(rows_s[:SUB, t * tile : (t + 1) * tile], carried)
         part = part.reshape(tile // 32, 2, 16, width)
         even = jnp.broadcast_to(core, (tile // 32, 16, width)) == 0
-        part = jnp.where(even, part[:, 0], part[:, 1]).reshape(tile // 2, width)
-        out_ref[t * tile // 2 : (t + 1) * tile // 2, :] = part.astype(out_ref.dtype)
+        yield pl.ds(t * tile // 2, tile // 2), jnp.where(even, part[:, 0], part[:, 1]).reshape(tile // 2, width)
+
+
+def keep_kernel(core_ref, rows_ref, dscore_ref, out_ref, rows_s):
+    for place, part in half_term(core_ref[0], rows_ref, dscore_ref, rows_s):
+        out_ref[place, :] = part
+
+
+def send_kernel(core_ref, rows_ref, dscore_ref, out_hbm, rows_s, out_s, sems):
+    stores = []
+    for n, (place, part) in enumerate(half_term(core_ref[0], rows_ref, dscore_ref, rows_s)):
+        out_s[place, :] = part.astype(bf16)
+        stores.append(pltpu.make_async_copy(out_s.at[place], out_hbm.at[place], sems.at[n]))
+        stores[n].start()
+    for store in stores:
+        store.wait()
 
 
 def split_kernel(y_ref, keep_ref, got_ref, own_ref, *send_refs):
@@ -367,13 +382,15 @@
     core = lax.axis_index("c").astype(i32).reshape(1)
     rows_core = width // NC
 
-    def term(half_of, dtype):
-        return call(
-            weight_kernel, struct((rows_core, width), dtype), 2, [pltpu.VMEM((LAN, width), bf16)],
-            flops=10**9, moved=4 * MIB, smem=1, grant=24,
-        )(half_of, rows, dscore)
-
-    send, keep = term(1 - core, bf16), term(core, f32)
+    send = call(
+        send_kernel, struct((rows_core, width), bf16), 2,
+        [pltpu.VMEM((LAN, width), bf16), pltpu.VMEM((rows_core, width), bf16), dma((4,))],
+        flops=10**9, moved=4 * MIB, smem=1, hbm_outs=1, grant=24,
+    )(1 - core, rows, dscore)
+    keep = call(
+        keep_kernel, struct((rows_core, width), f32), 2, [pltpu.VMEM((LAN, width), bf16)],
+        flops=10**9, moved=4 * MIB, smem=1, grant=24,
+    )(core, rows, dscore)
     got = lax.ppermute(send, "c", [(0, 1), (1, 0)])
     y = lax.axis_index("y").astype(i32).reshape(1)
     cols = width // NY

time: 144 us -> 144 us (level)
  transfers between devices with their start and end apart: 17 -> 17, of which waited for: 14 -> 14; matrix products, arithmetic and copies ran while one was open for 1% -> 1% of each run, Pallas kernels for 11% -> 10%
where the time goes in v6:
time: 144 us
  waiting for transfers between devices  62 us (43%)
  starting transfers between devices  51.1 us (35%)
  Pallas kernels  26.4 us (18%)
  local copies, waits for them, and re-layouts  2.15 us (1%)
    all_to_all x1, waiting for transfers between devices, on_device(): lax.all_to_all(found.reshape(n_rec, 2 * CAP, half), REC, split_axis=0, co...  32.4 us
    all_to_all x1, starting transfers between devices, on_device(): lax.all_to_all(requests, REC, split_axis=0, concat_axis=0, tiled=True)  12 us
    ppermute x3, waiting for transfers between devices, on_device(): lax.ppermute(sends[k - 1], 'y', [(i, (i + k) % NY) for i in range(NY)])  9.73 us
    pallas_call x1, Pallas kernels, on_device(): call(owner_kernel, [struct((arrivals, half), bf16), struct((SUB, width),...  7.34 us
    all_to_all x1, starting transfers between devices, on_device(): lax.all_to_all(out.reshape(n_rec, 2 * CAP, half), REC, split_axis=0, conc...  7.34 us
    all_to_all x1, waiting for transfers between devices, on_device(): lax.all_to_all(requests, REC, split_axis=0, concat_axis=0, tiled=True)  7.03 us
    ppermute x3, starting transfers between devices, on_device(): lax.ppermute(sends[k - 1], 'y', [(i, (i + k) % NY) for i in range(NY)])  6.43 us
    pallas_call x1, Pallas kernels, on_device(): call(prepare_kernel, [struct((2 * SUB, arrivals), bf16), struct((arrivals...  6.18 us
  transfers between devices with their start and end apart: 17, of which 14 were waited for; matrix products, arithmetic and copies ran while one was open for 1% of the time, Pallas kernels for 10%

profile of v6, /device:TPU:2, one launch (start us, length us, event | category | flops | bytes accessed | tf_op | source)
XLA Modules:
  0.0 143.5 jit_solution(10242106567924124316)
XLA Ops:
  2.6 12.0 %all-to-all-start = ((s32[64,1,128]{2,1,0:T(1,128)}), s32[64,1,128]{2,1,0:T(1,128)S(1)}, u32[]{:S(2)}, u32[]{:S(2)}) async-start(s32[64,1,128]{2,1,0:T(1,128)} %shard_map.68), calls=%async_computation | async-start | bytes 65536 | tf_op jit(solution)/shard_map/all_to_all | solution.py:344
  14.6 1.4 copy-done
  16.1 7.0 %all-to-all-done.asked_ref = s32[64,1,128]{2,1,0:T(1,128)S(1)} async-done(((s32[64,1,128]{2,1,0:T(1,128)}), s32[64,1,128]{2,1,0:T(1,128)S(1)}, u32[]{:S(2)}, u32[]{:S(2)}) %all-to-all-start) | async-done | bytes 32800 | tf_op jit(solution)/shard_map/all_to_all | solution.py:344
  23.2 2.2 %shard_map.70 = bf16[1536,512]{1,0:T(8,128)(2,1)} custom-call(s32[64,1,128]{2,1,0:T(1,128)S(1)} %all-to-all-done.asked_ref, bf16[768,512]{1,0:T(8,128)(2,1)S(1)} %shard_map.69.stacked_ref), custom_call_target="tpu_custom_call" | custom-call | flops 1207959552 | bytes 3145728 | tf_op jit(solution)/shard_map/pallas_call | solution.py:349
  25.4 5.6 %all-to-all-start.1 = ((bf16[64,24,512]{2,1,0:T(8,128)(2,1)}), bf16[64,24,512]{2,1,0:T(8,128)(2,1)S(1)}, u32[]{:S(2)}, u32[]{:S(2)}) async-start(bf16[64,24,512]{2,1,0:T(8,128)(2,1)} %bitcast.2), calls=%async_computation.1 | async-start | bytes 3145728 | tf_op jit(solution)/shard_map/all_to_all | solution.py:354
  31.0 6.2 %shard_map.71 = (bf16[544,1536]{1,0:T(8,128)(2,1)}, bf16[2080,768]{1,0:T(8,128)(2,1)}, bf16[768,1536]{1,0:T(8,128)(2,1)}) custom-call(s32[8,99]{1,0:T(8,128)} %bitcast.45, s32[2,128]{1,0:T(2,128)} %bitcast.52, s32[1,128]{1,0:T(1,128)} %labels_ref.1, s32[64,1,128]{2,1,0:T(1,128)} %copy-done.1), custom_call_target="tpu_custom_call" | custom-call | bytes 8388608 | tf_op jit(solution)/shard_map/pallas_call | solution.py:357
  37.2 32.4 %all-to-all-done.1 = bf16[64,24,512]{2,1,0:T(8,128)(2,1)S(1)} async-done(((bf16[64,24,512]{2,1,0:T(8,128)(2,1)}), bf16[64,24,512]{2,1,0:T(8,128)(2,1)S(1)}, u32[]{:S(2)}, u32[]{:S(2)}) %all-to-all-start.1) | async-done | bytes 1572896 | tf_op jit(solution)/shard_map/all_to_all | solution.py:354
  69.6 7.3 %shard_map.72 = (bf16[1536,512]{1,0:T(8,128)(2,1)}, bf16[272,1024]{1,0:T(8,128)(2,1)S(1)}, bf16[272,384]{1,0:T(8,128)(2,1)S(1)}) custom-call(bf16[1536,512]{1,0:T(8,128)(2,1)S(1)} %bitcast.44, bf16[544,1536]{1,0:T(8,128)(2,1)} %get-tuple-element.14.gather_hbm, bf16[1024,1024]{1,0:T(8,128)(2,1)} %weight_hbm.1, bf16[2080,768]{1,0:T(8,128)(2,1)} %get-tuple-element.15.table_hbm), custom_call_target="tpu_custom_call" | custom-call | flops 4000000000 | bytes 12582912 | tf_op jit(solution)/shard_map/pallas_call | solution.py:367
  77.0 7.3 %all-to-all-start.2 = ((bf16[64,24,512]{2,1,0:T(8,128)(2,1)}), bf16[64,24,512]{2,1,0:T(8,128)(2,1)S(1)}, u32[]{:S(2)}, u32[]{:S(2)}) async-start(bf16[64,24,512]{2,1,0:T(8,128)(2,1)} %bitcast.6), calls=%async_computation.2 | async-start | bytes 3145728 | tf_op jit(solution)/shard_map/all_to_all | solution.py:378
  84.3 2.3 %shard_map.75 = bf16[512,1024]{1,0:T(8,128)(2,1)} custom-call(s32[1]{0:T(128)S(6)} %sub.11.core_ref, bf16[272,1024]{1,0:T(8,128)(2,1)S(1)} %get-tuple-element.18.rows_ref, bf16[272,384]{1,0:T(8,128)(2,1)S(1)} %get-tuple-element.19.dscore_ref), custom_call_target="tpu_custom_call" | custom-call | flops 1000000000 | bytes 4194304 | tf_op jit(solution)/shard_map/pallas_call | solution.py:385
  86.8 1.5 %shard_map.74.keep_ref = f32[512,1024]{1,0:T(8,128)S(1)} custom-call(s32[1]{0:T(128)} %bitcast.9.core_ref, bf16[272,1024]{1,0:T(8,128)(2,1)S(1)} %get-tuple-element.18.rows_ref, bf16[272,384]{1,0:T(8,128)(2,1)S(1)} %get-tuple-element.19.dscore_ref), custom_call_target="tpu_custom_call" | custom-call | flops 1000000000 | bytes 4194304 | tf_op jit(solution)/shard_map/pallas_call | solution.py:390
  90.6 3.2 %collective-permute-start.1 = (bf16[512,256]{1,0:T(8,128)(2,1)}, bf16[512,256]{1,0:T(8,128)(2,1)S(1)}, u32[]{:S(2)}, u32[]{:S(2)}) collective-permute-start(bf16[512,256]{1,0:T(8,128)(2,1)} %get-tuple-element.21), channel_id=1, source_target_pairs={{0,2},{1,3},{2,0},{3,1},{4,6},{5,7},{6,4},{7,5},{8,10},{9,11},{10,... | collective-permute-start | bytes 786440 | tf_op jit(solution)/shard_map/ppermute | solution.py:403
  94.5 2.6 %collective-permute-start.3 = (bf16[512,256]{1,0:T(8,128)(2,1)S(1)}, bf16[512,256]{1,0:T(8,128)(2,1)}, u32[]{:S(2)}, u32[]{:S(2)}) collective-permute-start(bf16[512,256]{1,0:T(8,128)(2,1)S(1)} %get-tuple-element.23), channel_id=1, source_target_pairs={{0,3},{1,0},{2,1},{3,2},{4,7},{5,4},{6,5},{7,6},{8,11},{9,8},{10,9... | collective-permute-start | bytes 786440 | tf_op jit(solution)/shard_map/ppermute | solution.py:403
  97.1 4.5 %collective-permute-done.1 = bf16[512,256]{1,0:T(8,128)(2,1)S(1)} collective-permute-done((bf16[512,256]{1,0:T(8,128)(2,1)}, bf16[512,256]{1,0:T(8,128)(2,1)S(1)}, u32[]{:S(2)}, u32[]{:S(2)}) %collective-permute-start.1) | collective-permute-done | bytes 262176 | tf_op jit(solution)/shard_map/ppermute | solution.py:403
  101.5 4.8 %collective-permute-done.2 = bf16[512,256]{1,0:T(8,128)(2,1)S(1)} collective-permute-done((bf16[512,256]{1,0:T(8,128)(2,1)}, bf16[512,256]{1,0:T(8,128)(2,1)S(1)}, u32[]{:S(2)}, u32[]{:S(2)}) %collective-permute-start.2) | collective-permute-done | bytes 262176 | tf_op jit(solution)/shard_map/ppermute | solution.py:403
  107.9 2.4 %collective-permute-start.4 = (bf16[128,256]{1,0:T(8,128)(2,1)S(1)}, bf16[128,256]{1,0:T(8,128)(2,1)S(1)}, u32[]{:S(2)}, u32[]{:S(2)}) collective-permute-start(bf16[128,256]{1,0:T(8,128)(2,1)S(1)} %get-tuple-element.26), channel_id=1, source_target_pairs={{0,128},{64,192},{128,0},{192,64},{1,129},{65,193},{129,1},{193,65... | collective-permute-start | bytes 196616 | tf_op jit(solution)/shard_map/ppermute | solution.py:327
  110.3 2.0 %collective-permute-start.6 = (bf16[128,256]{1,0:T(8,128)(2,1)S(1)}, bf16[128,256]{1,0:T(8,128)(2,1)S(1)}, u32[]{:S(2)}, u32[]{:S(2)}) collective-permute-start(bf16[128,256]{1,0:T(8,128)(2,1)S(1)} %get-tuple-element.27), channel_id=1, source_target_pairs={{0,192},{64,0},{128,64},{192,128},{1,193},{65,1},{129,65},{193,129... | collective-permute-start | bytes 196616 | tf_op jit(solution)/shard_map/ppermute | solution.py:327
  112.3 3.6 %collective-permute-done.4 = bf16[128,256]{1,0:T(8,128)(2,1)S(1)} collective-permute-done((bf16[128,256]{1,0:T(8,128)(2,1)S(1)}, bf16[128,256]{1,0:T(8,128)(2,1)S(1)}, u32[]{:S(2)}, u32[]{:S(2)}) %collective-permute-start.4) | collective-permute-done | bytes 65568 | tf_op jit(solution)/shard_map/ppermute | solution.py:327
  118.4 5.7 %collective-permute-start.7 = (bf16[4,16,256]{2,1,0:T(8,128)(2,1)S(1)}, bf16[4,16,256]{2,1,0:T(8,128)(2,1)S(1)}, u32[]{:S(2)}, u32[]{:S(2)}) collective-permute-start(bf16[4,16,256]{2,1,0:T(8,128)(2,1)S(1)} %fusion.5), channel_id=1, source_target_pairs={{0,32},{8,40},{16,48},{24,56},{32,0},{40,8},{48,16},{56,24},{1,33}... | collective-permute-start | bytes 98312 | tf_op jit(solution)/shard_map/ppermute | solution.py:410
  124.1 3.7 %shard_map.73 = f32[384,1024]{1,0:T(8,128)} custom-call(bf16[1536,512]{1,0:T(8,128)(2,1)S(1)} %bitcast.42, bf16[768,1536]{1,0:T(8,128)(2,1)} %get-tuple-element.17.pick_hbm), custom_call_target="tpu_custom_call" | custom-call | flops 1207959552 | bytes 6291456 | tf_op jit(solution)/shard_map/pallas_call | solution.py:411
  130.0 1.5 %collective-permute-start.9 = (bf16[16,256]{1,0:T(8,128)(2,1)S(1)}, bf16[16,256]{1,0:T(8,128)(2,1)S(1)}, u32[]{:S(2)}, u32[]{:S(2)}) collective-permute-start(bf16[16,256]{1,0:T(8,128)(2,1)S(1)} %get-tuple-element.31), channel_id=1, source_target_pairs={{0,16},{8,24},{16,0},{24,8},{32,48},{40,56},{48,32},{56,40},{1,17}... | collective-permute-start | bytes 24584 | tf_op jit(solution)/shard_map/ppermute | solution.py:422
  131.6 2.8 %collective-permute-done.8 = bf16[16,256]{1,0:T(8,128)(2,1)S(1)} collective-permute-done((bf16[16,256]{1,0:T(8,128)(2,1)S(1)}, bf16[16,256]{1,0:T(8,128)(2,1)S(1)}, u32[]{:S(2)}, u32[]{:S(2)}) %collective-permute-start.8) | collective-permute-done | bytes 8224 | tf_op jit(solution)/shard_map/ppermute | solution.py:422
  134.5 1.7 %collective-permute-start.11 = (f32[16,256]{1,0:T(8,128)S(1)}, f32[16,256]{1,0:T(8,128)S(1)}, u32[]{:S(2)}, u32[]{:S(2)}) collective-permute-start(f32[16,256]{1,0:T(8,128)S(1)} %fusion.7.refs_0_), channel_id=1, source_target_pairs={{0,1},{1,2},{2,3},{3,0},{4,5},{5,6},{6,7},{7,4},{8,9},{9,10},{10,1... | collective-permute-start | bytes 49160 | tf_op jit(solution)/shard_map/ppermute | solution.py:428
  136.3 2.9 %collective-permute-start.12 = (f32[16,256]{1,0:T(8,128)S(1)}, f32[16,256]{1,0:T(8,128)S(1)}, u32[]{:S(2)}, u32[]{:S(2)}) collective-permute-start(f32[16,256]{1,0:T(8,128)S(1)} %fusion.7.refs_0_), channel_id=1, source_target_pairs={{0,2},{1,3},{2,0},{3,1},{4,6},{5,7},{6,4},{7,5},{8,10},{9,11},{10,... | collective-permute-start | bytes 49160 | tf_op jit(solution)/shard_map/ppermute | solution.py:428
  (33 shorter events, 16.0 us)
Async XLA Ops:
  0.6 0.7 copy-start.2
  2.6 20.6 %all-to-all-start = ((s32[64,1,128]{2,1,0:T(1,128)}), s32[64,1,128]{2,1,0:T(1,128)S(1)}, u32[]{:S(2)}, u32[]{:S(2)}) async-start(s32[64,1,128]{2,1,0:T(1,128)} %shard_map.68), calls=%async_computation | async-start | bytes 65536 | tf_op jit(solution)/shard_map/all_to_all | solution.py:344
  14.6 1.4 copy-start
  23.2 2.2 %copy-start.1 = (s32[64,1,128]{2,1,0:T(1,128)}, s32[64,1,128]{2,1,0:T(1,128)S(1)}, u32[]{:S(2)}) copy-start(s32[64,1,128]{2,1,0:T(1,128)S(1)} %all-to-all-done.asked_ref) | copy-start | bytes 98308
  25.4 44.2 %all-to-all-start.1 = ((bf16[64,24,512]{2,1,0:T(8,128)(2,1)}), bf16[64,24,512]{2,1,0:T(8,128)(2,1)S(1)}, u32[]{:S(2)}, u32[]{:S(2)}) async-start(bf16[64,24,512]{2,1,0:T(8,128)(2,1)} %bitcast.2), calls=%async_computation.1 | async-start | bytes 3145728 | tf_op jit(solution)/shard_map/all_to_all | solution.py:354
  77.0 47.1 %all-to-all-start.2 = ((bf16[64,24,512]{2,1,0:T(8,128)(2,1)}), bf16[64,24,512]{2,1,0:T(8,128)(2,1)S(1)}, u32[]{:S(2)}, u32[]{:S(2)}) async-start(bf16[64,24,512]{2,1,0:T(8,128)(2,1)} %bitcast.6), calls=%async_computation.2 | async-start | bytes 3145728 | tf_op jit(solution)/shard_map/all_to_all | solution.py:378
  86.6 3.0 %collective-permute-start = (bf16[512,1024]{1,0:T(8,128)(2,1)}, bf16[512,1024]{1,0:T(8,128)(2,1)S(1)}, u32[]{:S(2)}, u32[]{:S(2)}) collective-permute-start(bf16[512,1024]{1,0:T(8,128)(2,1)} %shard_map.75), channel_id=1, source_target_pairs={{0,4},{4,0},{1,5},{5,1},{2,6},{6,2},{3,7},{7,3},{8,12},{12,8},{9,1... | collective-permute-start | bytes 3145736 | tf_op jit(solution)/shard_map/ppermute | solution.py:394
  90.6 10.9 %collective-permute-start.1 = (bf16[512,256]{1,0:T(8,128)(2,1)}, bf16[512,256]{1,0:T(8,128)(2,1)S(1)}, u32[]{:S(2)}, u32[]{:S(2)}) collective-permute-start(bf16[512,256]{1,0:T(8,128)(2,1)} %get-tuple-element.21), channel_id=1, source_target_pairs={{0,2},{1,3},{2,0},{3,1},{4,6},{5,7},{6,4},{7,5},{8,10},{9,11},{10,... | collective-permute-start | bytes 786440 | tf_op jit(solution)/shard_map/ppermute | solution.py:403
  93.8 12.5 %collective-permute-start.2 = (bf16[512,256]{1,0:T(8,128)(2,1)}, bf16[512,256]{1,0:T(8,128)(2,1)S(1)}, u32[]{:S(2)}, u32[]{:S(2)}) collective-permute-start(bf16[512,256]{1,0:T(8,128)(2,1)} %get-tuple-element.22), channel_id=1, source_target_pairs={{0,1},{1,2},{2,3},{3,0},{4,5},{5,6},{6,7},{7,4},{8,9},{9,10},{10,1... | collective-permute-start | bytes 786440 | tf_op jit(solution)/shard_map/ppermute | solution.py:403
  94.5 12.3 %collective-permute-start.3 = (bf16[512,256]{1,0:T(8,128)(2,1)S(1)}, bf16[512,256]{1,0:T(8,128)(2,1)}, u32[]{:S(2)}, u32[]{:S(2)}) collective-permute-start(bf16[512,256]{1,0:T(8,128)(2,1)S(1)} %get-tuple-element.23), channel_id=1, source_target_pairs={{0,3},{1,0},{2,1},{3,2},{4,7},{5,4},{6,5},{7,6},{8,11},{9,8},{10,9... | collective-permute-start | bytes 786440 | tf_op jit(solution)/shard_map/ppermute | solution.py:403
  107.9 8.0 %collective-permute-start.4 = (bf16[128,256]{1,0:T(8,128)(2,1)S(1)}, bf16[128,256]{1,0:T(8,128)(2,1)S(1)}, u32[]{:S(2)}, u32[]{:S(2)}) collective-permute-start(bf16[128,256]{1,0:T(8,128)(2,1)S(1)} %get-tuple-element.26), channel_id=1, source_target_pairs={{0,128},{64,192},{128,0},{192,64},{1,129},{65,193},{129,1},{193,65... | collective-permute-start | bytes 196616 | tf_op jit(solution)/shard_map/ppermute | solution.py:327
  110.3 6.7 %collective-permute-start.5 = (bf16[128,256]{1,0:T(8,128)(2,1)S(1)}, bf16[128,256]{1,0:T(8,128)(2,1)S(1)}, u32[]{:S(2)}, u32[]{:S(2)}) collective-permute-start(bf16[128,256]{1,0:T(8,128)(2,1)S(1)} %get-tuple-element.28), channel_id=1, source_target_pairs={{0,64},{64,128},{128,192},{192,0},{1,65},{65,129},{129,193},{193,1... | collective-permute-start | bytes 196616 | tf_op jit(solution)/shard_map/ppermute | solution.py:327
  110.3 8.1 %collective-permute-start.6 = (bf16[128,256]{1,0:T(8,128)(2,1)S(1)}, bf16[128,256]{1,0:T(8,128)(2,1)S(1)}, u32[]{:S(2)}, u32[]{:S(2)}) collective-permute-start(bf16[128,256]{1,0:T(8,128)(2,1)S(1)} %get-tuple-element.27), channel_id=1, source_target_pairs={{0,192},{64,0},{128,64},{192,128},{1,193},{65,1},{129,65},{193,129... | collective-permute-start | bytes 196616 | tf_op jit(solution)/shard_map/ppermute | solution.py:327
  118.4 9.4 %collective-permute-start.7 = (bf16[4,16,256]{2,1,0:T(8,128)(2,1)S(1)}, bf16[4,16,256]{2,1,0:T(8,128)(2,1)S(1)}, u32[]{:S(2)}, u32[]{:S(2)}) collective-permute-start(bf16[4,16,256]{2,1,0:T(8,128)(2,1)S(1)} %fusion.5), channel_id=1, source_target_pairs={{0,32},{8,40},{16,48},{24,56},{32,0},{40,8},{48,16},{56,24},{1,33}... | collective-permute-start | bytes 98312 | tf_op jit(solution)/shard_map/ppermute | solution.py:410
  127.9 3.7 %collective-permute-start.10 = (bf16[16,256]{1,0:T(8,128)(2,1)S(1)}, bf16[16,256]{1,0:T(8,128)(2,1)S(1)}, u32[]{:S(2)}, u32[]{:S(2)}) collective-permute-start(bf16[16,256]{1,0:T(8,128)(2,1)S(1)} %get-tuple-element.30), channel_id=1, source_target_pairs={{0,24},{8,0},{16,8},{24,16},{32,56},{40,32},{48,40},{56,48},{1,25}... | collective-permute-start | bytes 24584 | tf_op jit(solution)/shard_map/ppermute | solution.py:422
  129.0 5.4 %collective-permute-start.8 = (bf16[16,256]{1,0:T(8,128)(2,1)S(1)}, bf16[16,256]{1,0:T(8,128)(2,1)S(1)}, u32[]{:S(2)}, u32[]{:S(2)}) collective-permute-start(bf16[16,256]{1,0:T(8,128)(2,1)S(1)} %get-tuple-element.29), channel_id=1, source_target_pairs={{0,8},{8,16},{16,24},{24,0},{32,40},{40,48},{48,56},{56,32},{1,9},... | collective-permute-start | bytes 24584 | tf_op jit(solution)/shard_map/ppermute | solution.py:422
  130.0 4.5 %collective-permute-start.9 = (bf16[16,256]{1,0:T(8,128)(2,1)S(1)}, bf16[16,256]{1,0:T(8,128)(2,1)S(1)}, u32[]{:S(2)}, u32[]{:S(2)}) collective-permute-start(bf16[16,256]{1,0:T(8,128)(2,1)S(1)} %get-tuple-element.31), channel_id=1, source_target_pairs={{0,16},{8,24},{16,0},{24,8},{32,48},{40,56},{48,32},{56,40},{1,17}... | collective-permute-start | bytes 24584 | tf_op jit(solution)/shard_map/ppermute | solution.py:422
  134.5 5.8 %collective-permute-start.11 = (f32[16,256]{1,0:T(8,128)S(1)}, f32[16,256]{1,0:T(8,128)S(1)}, u32[]{:S(2)}, u32[]{:S(2)}) collective-permute-start(f32[16,256]{1,0:T(8,128)S(1)} %fusion.7.refs_0_), channel_id=1, source_target_pairs={{0,1},{1,2},{2,3},{3,0},{4,5},{5,6},{6,7},{7,4},{8,9},{9,10},{10,1... | collective-permute-start | bytes 49160 | tf_op jit(solution)/shard_map/ppermute | solution.py:428
  136.3 5.2 %collective-permute-start.12 = (f32[16,256]{1,0:T(8,128)S(1)}, f32[16,256]{1,0:T(8,128)S(1)}, u32[]{:S(2)}, u32[]{:S(2)}) collective-permute-start(f32[16,256]{1,0:T(8,128)S(1)} %fusion.7.refs_0_), channel_id=1, source_target_pairs={{0,2},{1,3},{2,0},{3,1},{4,6},{5,7},{6,4},{7,5},{8,10},{9,11},{10,... | collective-permute-start | bytes 49160 | tf_op jit(solution)/shard_map/ppermute | solution.py:428
  139.1 3.7 %collective-permute-start.13 = (f32[16,256]{1,0:T(8,128)S(1)}, f32[16,256]{1,0:T(8,128)S(1)}, u32[]{:S(2)}, u32[]{:S(2)}) collective-permute-start(f32[16,256]{1,0:T(8,128)S(1)} %fusion.7.refs_0_), channel_id=1, source_target_pairs={{0,3},{1,0},{2,1},{3,2},{4,7},{5,4},{6,5},{7,6},{8,11},{9,8},{10,9... | collective-permute-start | bytes 49160 | tf_op jit(solution)/shard_map/ppermute | solution.py:428
